TPU v7x, 32 devices: a whole 2x2x4 slice. The times are simulated.
32 devices in a mesh: leaf: 8 (over z, core), list: 4 (over y, x).
Axes of the slice: x: 2, y: 2, z: 4, core: 2. Of those that a mesh axis runs over, the one named last changes fastest.
Arguments:
- panel_charges: bfloat16 [512, 64, 256], P(('leaf', 'list')), may hold values from -6 to 6
- leaf_basis: bfloat16 [512, 64, 256], P(('leaf', 'list')), may hold values from -0.375 to 0.375
- near_blocks: bfloat16 [512, 4, 256, 256], P(('leaf', 'list')), may hold values from -0.1875 to 0.1875
- near_list: int32 [512, 4], P(('leaf', 'list')), may hold values from 0 to 15, as said below
- far_list: int32 [512, 8], P(('leaf', 'list')), may hold values from 0 to 63, as said below
- far_count: int32 [512], P(('leaf', 'list')), may hold values from 1 to 8, as said below
- far_coupling: bfloat16 [512, 8, 64, 64], P(('leaf', 'list')), may hold values from -0.25 to 0.25
- leaf_transfer: float32 [512, 64, 64], P(('leaf', 'list')), may hold values from -0.4375 to 0.4375
- device_transfer: float32 [8, 4, 64, 64], P('leaf', 'list'), may hold values from -0.375 to 0.375
- tree_transfer: float32 [8, 64, 64], replicated, may hold values from -0.75 to 0.75
- level_coupling: float32 [12, 4, 64, 64], replicated, may hold values from -0.4375 to 0.4375
Outputs:
- potential: bfloat16 [512, 64, 256], P(('leaf', 'list'))
Inputs may be any that keep to these rules, and one draw needn't show every extreme that they name: `far_list`: each row names 8 different leaves of the leaf's group subtree, none on the leaf's own device; the 16 leaves of one device name, over all their slots, exactly 8 different leaves of each other device of the group. Slots at and after far_count[c] are unused. `near_list`: each row names 4 different leaves of the leaf's own device, the first being the leaf itself.
All inputs are finite; a program needn't handle non-finite values.
Results may differ from a plain program's by a relative error of at most 0.0053.
Values may be sent and summed in bfloat16 or wider, within the bound.
No kernel may reach another device: no remote copies, remote signals or barrier semaphores. Data moves between devices by JAX's collectives and lax.ppermute only.
A program may use at most 64 MiB of HBM per device.

v0:
```python
import jax
import jax.numpy as jnp
from jax import lax
from jax.sharding import PartitionSpec as P

highest = lax.Precision.HIGHEST
offsets = (-3, -2, 2, 3)


def partner(array, axis, distance):
    return lax.ppermute(array, axis, [(i, i ^ 1 << distance) for i in range(lax.axis_size(axis))])


def shifted(array, axis, by):
    length = lax.axis_size(axis)
    pairs = [(i, i + by) for i in range(length) if 0 <= i + by < length]
    return lax.ppermute(array, axis, pairs)


def pick_usable(offset, parity):
    if offset == 3:
        return parity == 0
    if offset == -3:
        return parity == 1
    return parity >= 0


def upper_exchange(group_node, tree_transfer, level_coupling):
    leaf_count = lax.axis_size("leaf")
    depth = leaf_count.bit_length() - 2
    position = lax.axis_index("leaf")
    nodes = [group_node]
    for height in range(depth - 1):
        begin_row = 2 * leaf_count - 2 * (leaf_count >> height)
        matrix = tree_transfer[begin_row + (position >> height)]
        own_part = jnp.dot(nodes[-1], matrix, precision=highest)
        nodes.append(own_part + partner(own_part, "leaf", height))
    coupled = []
    for height in range(depth):
        begin_row = 2 * leaf_count - 2 * (leaf_count >> height)
        matrices = level_coupling[begin_row + (position >> height)]
        parity = (position >> height) % 2
        summed = jnp.zeros_like(group_node)
        for slot_index, offset in enumerate(offsets):
            source = shifted(nodes[height], "leaf", -offset * (1 << height))
            contribution = jnp.dot(source, matrices[slot_index].T, precision=highest)
            summed = summed + jnp.where(
                pick_usable(offset, parity), contribution, jnp.zeros((), jnp.float32)
            )
        coupled.append(summed)
    result = coupled[-1]
    for height in reversed(range(depth - 1)):
        begin_row = 2 * leaf_count - 2 * (leaf_count >> height)
        matrix = tree_transfer[begin_row + (position >> height)]
        result = coupled[height] + jnp.dot(result, matrix.T, precision=highest)
    return result


def on_device(
    panel_charges,
    leaf_basis,
    near_blocks,
    near_list,
    far_list,
    far_count,
    far_coupling,
    leaf_transfer,
    device_transfer,
    tree_transfer,
    level_coupling,
):
    leaf_local = panel_charges.shape[0]
    far_slots = far_list.shape[1]
    near_slots = near_list.shape[1]
    skeleton = jnp.einsum(
        "crm,ckm->crk", panel_charges, leaf_basis, preferred_element_type=jnp.float32
    ).astype(jnp.bfloat16)
    device_node = jnp.einsum(
        "irb,iba->ra", skeleton.astype(jnp.float32), leaf_transfer, precision=highest
    )
    device_term = jnp.dot(device_node, device_transfer[0, 0], precision=highest)
    group_node = lax.psum(device_term, "list")
    top_down = upper_exchange(group_node, tree_transfer, level_coupling)
    device_down = jnp.dot(top_down, device_transfer[0, 0].T, precision=highest)
    from_above = jnp.einsum("rd,ild->irl", device_down, leaf_transfer, precision=highest)
    row_width = skeleton.shape[1] * skeleton.shape[2]
    flattened = skeleton.reshape(leaf_local, row_width)
    wanted = far_list.reshape(-1)
    usable = (jnp.arange(far_slots, dtype=jnp.int32)[None, :] < far_count[:, None]).reshape(-1)
    piece = lax.all_gather(flattened, "list", axis=0, tiled=True)
    columns = jnp.arange(piece.shape[0], dtype=jnp.int32)
    hits = ((wanted[:, None] == columns[None, :]) & usable[:, None]).astype(jnp.bfloat16)
    collected = jnp.dot(hits, piece, preferred_element_type=jnp.float32)
    selected = collected.astype(jnp.bfloat16)
    selected = selected.reshape(leaf_local, far_slots, skeleton.shape[1], skeleton.shape[2])
    leaf_coupled = jnp.einsum(
        "ckrb,ckab->cra", selected, far_coupling, preferred_element_type=jnp.float32
    )
    coefficients = (leaf_coupled + from_above).astype(jnp.bfloat16)
    far_field = jnp.einsum(
        "crk,ckm->crm", coefficients, leaf_basis, preferred_element_type=jnp.float32
    )
    neighbours = jnp.take(panel_charges, near_list.reshape(-1), axis=0)
    neighbours = neighbours.reshape(
        leaf_local, near_slots, panel_charges.shape[1], panel_charges.shape[2]
    )
    near_field = jnp.einsum(
        "ckrm,cknm->crn", neighbours, near_blocks, preferred_element_type=jnp.float32
    )
    return (far_field + near_field).astype(jnp.bfloat16)


def solution(mesh):
    in_specs = (
        P(("leaf", "list"), None, None),
        P(("leaf", "list"), None, None),
        P(("leaf", "list"), None, None, None),
        P(("leaf", "list"), None),
        P(("leaf", "list"), None),
        P(("leaf", "list")),
        P(("leaf", "list"), None, None, None),
        P(("leaf", "list"), None, None),
        P("leaf", "list", None, None),
        P(),
        P(),
    )
    out_specs = P(("leaf", "list"), None, None)
    return jax.shard_map(
        on_device, mesh=mesh, in_specs=in_specs, out_specs=out_specs, check_vma=False
    )
```

profile of v0, /device:TPU:0, one launch (start us, length us, event | category | flops | bytes accessed | tf_op | source)
XLA Modules:
  0.0 83.7 jit_solution(2154308177923877270)
XLA Ops:
  0.0 1.6 %convolution_convert_fusion.1 = bf16[16,64,64]{2,1,0:T(8,128)(2,1)S(1)} fusion(bf16[16,64,256]{2,1,0:T(8,128)(2,1)} %param.11, bf16[16,64,256]{2,1,0:T(8,128)(2,1)} %param.12), kind=kOutput, calls=%fused_computation.12 | convolution fusion | flops 33619968 | bytes 1179648 | tf_op jit(solution)/shard_map/crm,ckm->crk/dot_general | solution.py:75
  1.7 1.4 %convolution_bitcast_fusion.3 = f32[64,64]{1,0:T(8,128)S(1)} fusion(bf16[16,64,64]{2,1,0:T(8,128)(2,1)S(1)} %convolution_convert_fusion.1, f32[16,64,64]{2,1,0:T(8,128)} %param.18), kind=kOutput, calls=%fused_computation.29 | convolution fusion | flops 50331648 | bytes 409600 | tf_op jit(solution)/shard_map/irb,iba->ra/dot_general | solution.py:78
  3.3 17.8 %psum.7 = f32[64,64]{1,0:T(8,128)S(1)} all-reduce(f32[64,64]{1,0:T(8,128)S(1)} %fusion.24), channel_id=1, replica_groups=mesh['leaf'=8,'list'=4] {'list'}, use_global_device_ids=true, to_apply=%region_0.0 | all-reduce | flops 4096 | bytes 32768 | tf_op jit(solution)/shard_map/psum | solution.py:82
  21.0 1.3 %collective-permute-start.3 = (f32[64,64]{1,0:T(8,128)S(1)}, f32[64,64]{1,0:T(8,128)S(1)}, u32[]{:S(2)}, u32[]{:S(2)}) collective-permute-start(f32[64,64]{1,0:T(8,128)S(1)} %psum.7), channel_id=1, source_target_pairs={{12,0},{16,4},{20,8},{24,12},{28,16},{13,1},{17,5},{21,9},{25,13},... | collective-permute-start | bytes 49160 | tf_op jit(solution)/shard_map/ppermute | solution.py:17
  22.3 1.3 %collective-permute-start.2 = (f32[64,64]{1,0:T(8,128)S(1)}, f32[64,64]{1,0:T(8,128)S(1)}, u32[]{:S(2)}, u32[]{:S(2)}) collective-permute-start(f32[64,64]{1,0:T(8,128)S(1)} %psum.7), channel_id=1, source_target_pairs={{8,0},{12,4},{16,8},{20,12},{24,16},{28,20},{9,1},{13,5},{17,9},{2... | collective-permute-start | bytes 49160 | tf_op jit(solution)/shard_map/ppermute | solution.py:17
  23.6 4.5 %collective-permute-start.1 = (f32[64,64]{1,0:T(8,128)S(1)}, f32[64,64]{1,0:T(8,128)S(1)}, u32[]{:S(2)}, u32[]{:S(2)}) collective-permute-start(f32[64,64]{1,0:T(8,128)S(1)} %psum.7), channel_id=1, source_target_pairs={{0,8},{4,12},{8,16},{12,20},{16,24},{20,28},{1,9},{5,13},{9,17},{1... | collective-permute-start | bytes 49160 | tf_op jit(solution)/shard_map/ppermute | solution.py:17
  28.2 3.7 %collective-permute-start = (f32[64,64]{1,0:T(8,128)S(1)}, f32[64,64]{1,0:T(8,128)S(1)}, u32[]{:S(2)}, u32[]{:S(2)}) collective-permute-start(f32[64,64]{1,0:T(8,128)S(1)} %psum.7), channel_id=1, source_target_pairs={{0,12},{4,16},{8,20},{12,24},{16,28},{1,13},{5,17},{9,21},{13,25},... | collective-permute-start | bytes 49160 | tf_op jit(solution)/shard_map/ppermute | solution.py:17
  32.8 1.6 %collective-permute-start.4 = (f32[64,64]{1,0:T(8,128)S(1)}, f32[64,64]{1,0:T(8,128)S(1)}, u32[]{:S(2)}, u32[]{:S(2)}) collective-permute-start(f32[64,64]{1,0:T(8,128)S(1)} %fusion.21), channel_id=1, source_target_pairs={{0,4},{4,0},{8,12},{12,8},{16,20},{20,16},{24,28},{28,24},{1,5},{5... | collective-permute-start | bytes 49160 | tf_op jit(solution)/shard_map/ppermute | solution.py:11
  35.4 9.1 %all_gather.3 = bf16[64,4096]{1,0:T(8,128)(2,1)S(1)} all-gather(bf16[16,4096]{1,0:T(8,128)(2,1)S(1)} %reshape.78), channel_id=1, replica_groups=mesh['leaf'=8,'list'=4] {'list'}, dimensions={0}, use_global_device_ids=true | all-gather | bytes 655360 | tf_op jit(solution)/shard_map/all_gather | solution.py:90
  44.5 1.5 %convolution_convert_fusion = bf16[128,4096]{1,0:T(8,128)(2,1)} fusion(bf16[64,4096]{1,0:T(8,128)(2,1)S(1)} %all_gather.3, s32[128]{0:T(128)S(1)} %eq.30, pred[128]{0:T(512)(128)(4,1)S(1)} %lt.61), kind=kOutput, calls=%fused_computation.1 | convolution fusion | flops 67649536 | bytes 1573504 | tf_op jit(solution)/shard_map/dot_general | solution.py:93
  45.9 4.2 %reshape.79 = bf16[16,8,64,64]{3,2,1,0:T(8,128)(2,1)} reshape(bf16[128,4096]{1,0:T(8,128)(2,1)} %convolution_convert_fusion) | data formatting | bytes 2097152 | tf_op jit(solution)/shard_map/reshape | solution.py:95
  50.2 2.0 %gather_fusion = bf16[64,64,256]{2,1,0:T(8,128)(2,1)} fusion(bf16[16,64,256]{2,1,0:T(8,128)(2,1)S(1)} %copy-done.1, s32[1024]{0:T(1024)S(1)} %pad_clamp_fusion), kind=kCustom, calls=%fused_computation | custom fusion | bytes 4194560 | tf_op jit(solution)/shard_map/jit(_take)/gather | solution.py:103
  52.2 6.8 %fusion.3 = f32[16,64,256]{2,1,0:T(8,128)S(1)} fusion(bf16[16,4,256,256]{3,2,1,0:T(8,128)(2,1)} %param.13, bf16[16,4,64,256]{3,2,1,0:T(8,128)(2,1)} %bitcast.77, pred[16,4]{1,0:T(8,128)(4,1)S(1)} %copy.16), kind=kOutput, calls=%fused_computation.5 | convolution fusion | flops 537919488 | bytes 11534400 | tf_op jit(solution)/shard_map/ckrm,cknm->crn/dot_general | solution.py:107
  59.0 1.5 %convolution_bitcast_fusion = f32[16,64,64]{2,1,0:T(8,128)} fusion(bf16[16,8,64,64]{3,2,1,0:T(8,128)(2,1)S(1)} %copy-done.2, bf16[16,8,64,64]{3,2,1,0:T(8,128)(2,1)S(1)} %copy-done), kind=kOutput, calls=%fused_computation.8 | convolution fusion | flops 67108864 | bytes 2359296 | tf_op jit(solution)/shard_map/ckrb,ckab->cra/dot_general | solution.py:96
  60.5 1.4 %collective-permute-start.8 = (f32[64,64]{1,0:T(8,128)S(1)}, f32[64,64]{1,0:T(8,128)S(1)}, u32[]{:S(2)}, u32[]{:S(2)}) collective-permute-start(f32[64,64]{1,0:T(8,128)S(1)} %add.83), channel_id=1, source_target_pairs={{24,0},{28,4},{25,1},{29,5},{26,2},{30,6},{27,3},{31,7}} | collective-permute-start | bytes 49160 | tf_op jit(solution)/shard_map/ppermute | solution.py:17
  62.0 1.3 %collective-permute-start.7 = (f32[64,64]{1,0:T(8,128)S(1)}, f32[64,64]{1,0:T(8,128)S(1)}, u32[]{:S(2)}, u32[]{:S(2)}) collective-permute-start(f32[64,64]{1,0:T(8,128)S(1)} %add.83), channel_id=1, source_target_pairs={{16,0},{20,4},{24,8},{28,12},{17,1},{21,5},{25,9},{29,13},{18,2},{... | collective-permute-start | bytes 49160 | tf_op jit(solution)/shard_map/ppermute | solution.py:17
  64.2 5.4 %collective-permute-start.6 = (f32[64,64]{1,0:T(8,128)S(1)}, f32[64,64]{1,0:T(8,128)S(1)}, u32[]{:S(2)}, u32[]{:S(2)}) collective-permute-start(f32[64,64]{1,0:T(8,128)S(1)} %add.83), channel_id=1, source_target_pairs={{0,16},{4,20},{8,24},{12,28},{1,17},{5,21},{9,25},{13,29},{2,18},{... | collective-permute-start | bytes 49160 | tf_op jit(solution)/shard_map/ppermute | solution.py:17
  70.7 2.2 %collective-permute-start.5 = (f32[64,64]{1,0:T(8,128)S(1)}, f32[64,64]{1,0:T(8,128)S(1)}, u32[]{:S(2)}, u32[]{:S(2)}) collective-permute-start(f32[64,64]{1,0:T(8,128)S(1)} %add.83), channel_id=1, source_target_pairs={{0,24},{4,28},{1,25},{5,29},{2,26},{6,30},{3,27},{7,31}} | collective-permute-start | bytes 49160 | tf_op jit(solution)/shard_map/ppermute | solution.py:17
  73.8 0.9 %convolution_select_fusion.1 = f32[64,64]{1,0:T(8,128)S(1)} fusion(f32[64,64]{1,0:T(8,128)S(1)} %collective-permute-done.7, f32[12,4,64,64]{3,2,1,0:T(8,128)} %param.21, s32[]{:T(128)S(6)} %select_n.101, s32[]{:T(128)S(6)} %add.97, pred[]{:T(512)S(6)} %ge.19), kind=kOutput, calls=%fused_computation.15 | convolution fusion | flops 3149824 | bytes 65545 | tf_op jit(solution)/shard_map/dot_general | solution.py:46
  74.8 0.9 %convolution_select_fusion.2 = f32[64,64]{1,0:T(8,128)S(1)} fusion(f32[64,64]{1,0:T(8,128)S(1)} %collective-permute-done.6, f32[12,4,64,64]{3,2,1,0:T(8,128)} %param.21, s32[]{:T(128)S(6)} %select_n.101, s32[]{:T(128)S(6)} %add.96, pred[]{:T(512)S(6)} %ge.19), kind=kOutput, calls=%fused_computation.16 | convolution fusion | flops 3149824 | bytes 65545 | tf_op jit(solution)/shard_map/dot_general | solution.py:46
  76.7 1.0 %fusion.11 = f32[64,64]{1,0:T(8,128)S(1)} fusion(f32[64,64]{1,0:T(8,128)S(1)} %convolution_select_fusion, f32[64,64]{1,0:T(8,128)S(1)} %convolution_select_fusion.1, f32[64,64]{1,0:T(8,128)S(1)} %convolution_select_fusion.2, f32[64,64]{1,0:T(8,128)S(1)} %collective-permute-done.5, f32[12,4,64,64]{3,2,1,0:T(8,128)} %param.21, s32[]{:T(128)S(6)} %select_n.101, ...), kind=kOutput, calls=%fused_computation.20 | convolution fusion | flops 3162112 | bytes 114693 | tf_op jit(solution)/shard_map/dot_general | solution.py:46
  78.7 1.0 %fusion.15 = f32[64,64]{1,0:T(8,128)S(1)} fusion(f32[64,64]{1,0:T(8,128)S(1)} %fusion.19, f32[64,64]{1,0:T(8,128)S(1)} %convolution_select_fusion.4, f32[64,64]{1,0:T(8,128)S(1)} %convolution_select_fusion.5, f32[64,64]{1,0:T(8,128)S(1)} %convolution_select_fusion.6, f32[64,64]{1,0:T(8,128)S(1)} %collective-permute-done, f32[12,4,64,64]{3,2,1,0:T(8,128)} %param.21, ...), kind=kOutput, calls=%fused_computation.28 | convolution fusion | flops 3166208 | bytes 131077 | tf_op jit(solution)/shard_map/dot_general | solution.py:46
  79.8 2.8 %fusion.8 = bf16[16,64,64]{2,1,0:T(8,128)(2,1)S(1)} fusion(f32[16,64,64]{2,1,0:T(8,128)} %convolution_bitcast_fusion, f32[64,64,1]{1,0,2:T(8,128)S(1)} %convolution_bitcast_fusion.2, f32[16,64,64]{2,1,0:T(8,128)} %param.18), kind=kOutput, calls=%fused_computation.11 | convolution fusion | flops 50462720 | bytes 671744 | tf_op jit(solution)/shard_map/rd,ild->irl/dot_general | solution.py:85
  82.6 1.1 %fusion.6 = bf16[16,64,256]{2,1,0:T(8,128)(2,1)} fusion(f32[16,64,256]{2,1,0:T(8,128)S(1)} %fusion.3, bf16[16,64,64]{2,1,0:T(8,128)(2,1)S(1)} %fusion.8, bf16[16,64,256]{2,1,0:T(8,128)(2,1)S(1)} %copy-done.3), kind=kOutput, calls=%fused_computation.7 | convolution fusion | flops 34078720 | bytes 2228224 | tf_op jit(solution)/shard_map/crk,ckm->crm/dot_general | solution.py:100
  (45 shorter events, 7.0 us)
Async XLA Ops:
  0.0 59.0 %copy-start = (bf16[16,8,64,64]{3,2,1,0:T(8,128)(2,1)S(1)}, bf16[16,8,64,64]{3,2,1,0:T(8,128)(2,1)}, u32[]{:S(2)}) copy-start(bf16[16,8,64,64]{3,2,1,0:T(8,128)(2,1)} %param.17) | copy-start | bytes 3145732
  0.0 3.1 %copy-start.4 = (f32[1,1,64,64]{3,2,1,0:T(8,128)S(1)}, f32[1,1,64,64]{3,2,1,0:T(8,128)}, u32[]{:S(2)}) copy-start(f32[1,1,64,64]{3,2,1,0:T(8,128)} %param.19) | copy-start | bytes 49156
  0.0 34.4 %copy-start.5 = (s32[16,4]{0,1:T(4,128)S(1)}, s32[16,4]{0,1:T(4,128)}, u32[]{:S(2)}) copy-start(s32[16,4]{0,1:T(4,128)} %param.14) | copy-start | bytes 772
  0.0 34.9 %copy-start.7 = (s32[16]{0:T(128)S(1)}, s32[16]{0:T(128)}, u32[]{:S(2)}) copy-start(s32[16]{0:T(128)} %param.16) | copy-start | bytes 196
  0.0 35.1 %copy-start.6 = (s32[16,8]{0,1:T(8,128)S(1)}, s32[16,8]{0,1:T(8,128)}, u32[]{:S(2)}) copy-start(s32[16,8]{0,1:T(8,128)} %param.15) | copy-start | bytes 1540
  21.0 49.6 %collective-permute-start.3 = (f32[64,64]{1,0:T(8,128)S(1)}, f32[64,64]{1,0:T(8,128)S(1)}, u32[]{:S(2)}, u32[]{:S(2)}) collective-permute-start(f32[64,64]{1,0:T(8,128)S(1)} %psum.7), channel_id=1, source_target_pairs={{12,0},{16,4},{20,8},{24,12},{28,16},{13,1},{17,5},{21,9},{25,13},... | collective-permute-start | bytes 49160 | tf_op jit(solution)/shard_map/ppermute | solution.py:17
  22.3 39.7 %collective-permute-start.2 = (f32[64,64]{1,0:T(8,128)S(1)}, f32[64,64]{1,0:T(8,128)S(1)}, u32[]{:S(2)}, u32[]{:S(2)}) collective-permute-start(f32[64,64]{1,0:T(8,128)S(1)} %psum.7), channel_id=1, source_target_pairs={{8,0},{12,4},{16,8},{20,12},{24,16},{28,20},{9,1},{13,5},{17,9},{2... | collective-permute-start | bytes 49160 | tf_op jit(solution)/shard_map/ppermute | solution.py:17
  23.6 40.6 %collective-permute-start.1 = (f32[64,64]{1,0:T(8,128)S(1)}, f32[64,64]{1,0:T(8,128)S(1)}, u32[]{:S(2)}, u32[]{:S(2)}) collective-permute-start(f32[64,64]{1,0:T(8,128)S(1)} %psum.7), channel_id=1, source_target_pairs={{0,8},{4,12},{8,16},{12,20},{16,24},{20,28},{1,9},{5,13},{9,17},{1... | collective-permute-start | bytes 49160 | tf_op jit(solution)/shard_map/ppermute | solution.py:17
  28.2 50.5 %collective-permute-start = (f32[64,64]{1,0:T(8,128)S(1)}, f32[64,64]{1,0:T(8,128)S(1)}, u32[]{:S(2)}, u32[]{:S(2)}) collective-permute-start(f32[64,64]{1,0:T(8,128)S(1)} %psum.7), channel_id=1, source_target_pairs={{0,12},{4,16},{8,20},{12,24},{16,28},{1,13},{5,17},{9,21},{13,25},... | collective-permute-start | bytes 49160 | tf_op jit(solution)/shard_map/ppermute | solution.py:17
  32.8 27.7 %collective-permute-start.4 = (f32[64,64]{1,0:T(8,128)S(1)}, f32[64,64]{1,0:T(8,128)S(1)}, u32[]{:S(2)}, u32[]{:S(2)}) collective-permute-start(f32[64,64]{1,0:T(8,128)S(1)} %fusion.21), channel_id=1, source_target_pairs={{0,4},{4,0},{8,12},{12,8},{16,20},{20,16},{24,28},{28,24},{1,5},{5... | collective-permute-start | bytes 49160 | tf_op jit(solution)/shard_map/ppermute | solution.py:11
  44.5 5.7 %copy-start.1 = (bf16[16,64,256]{2,1,0:T(8,128)(2,1)S(1)}, bf16[16,64,256]{2,1,0:T(8,128)(2,1)}, u32[]{:S(2)}) copy-start(bf16[16,64,256]{2,1,0:T(8,128)(2,1)} %param.11) | copy-start | bytes 1572868
  52.2 6.8 %copy-start.2 = (bf16[16,8,64,64]{3,2,1,0:T(8,128)(2,1)S(1)}, bf16[16,8,64,64]{3,2,1,0:T(8,128)(2,1)}, u32[]{:S(2)}) copy-start(bf16[16,8,64,64]{3,2,1,0:T(8,128)(2,1)} %reshape.79) | copy-start | bytes 3145732
  60.5 22.1 %copy-start.3 = (bf16[16,64,256]{2,1,0:T(8,128)(2,1)S(1)}, bf16[16,64,256]{2,1,0:T(8,128)(2,1)}, u32[]{:S(2)}) copy-start(bf16[16,64,256]{2,1,0:T(8,128)(2,1)} %param.12) | copy-start | bytes 1572868
  60.5 15.2 %collective-permute-start.8 = (f32[64,64]{1,0:T(8,128)S(1)}, f32[64,64]{1,0:T(8,128)S(1)}, u32[]{:S(2)}, u32[]{:S(2)}) collective-permute-start(f32[64,64]{1,0:T(8,128)S(1)} %add.83), channel_id=1, source_target_pairs={{24,0},{28,4},{25,1},{29,5},{26,2},{30,6},{27,3},{31,7}} | collective-permute-start | bytes 49160 | tf_op jit(solution)/shard_map/ppermute | solution.py:17
  62.0 11.8 %collective-permute-start.7 = (f32[64,64]{1,0:T(8,128)S(1)}, f32[64,64]{1,0:T(8,128)S(1)}, u32[]{:S(2)}, u32[]{:S(2)}) collective-permute-start(f32[64,64]{1,0:T(8,128)S(1)} %add.83), channel_id=1, source_target_pairs={{16,0},{20,4},{24,8},{28,12},{17,1},{21,5},{25,9},{29,13},{18,2},{... | collective-permute-start | bytes 49160 | tf_op jit(solution)/shard_map/ppermute | solution.py:17
  64.2 10.5 %collective-permute-start.6 = (f32[64,64]{1,0:T(8,128)S(1)}, f32[64,64]{1,0:T(8,128)S(1)}, u32[]{:S(2)}, u32[]{:S(2)}) collective-permute-start(f32[64,64]{1,0:T(8,128)S(1)} %add.83), channel_id=1, source_target_pairs={{0,16},{4,20},{8,24},{12,28},{1,17},{5,21},{9,25},{13,29},{2,18},{... | collective-permute-start | bytes 49160 | tf_op jit(solution)/shard_map/ppermute | solution.py:17
  70.7 6.1 %collective-permute-start.5 = (f32[64,64]{1,0:T(8,128)S(1)}, f32[64,64]{1,0:T(8,128)S(1)}, u32[]{:S(2)}, u32[]{:S(2)}) collective-permute-start(f32[64,64]{1,0:T(8,128)S(1)} %add.83), channel_id=1, source_target_pairs={{0,24},{4,28},{1,25},{5,29},{2,26},{6,30},{3,27},{7,31}} | collective-permute-start | bytes 49160 | tf_op jit(solution)/shard_map/ppermute | solution.py:17
where the time goes:
time: 84.8 us; the launch traced here: 83.7 us
  blocking collectives  26.9 us (32%)
  matrix products  26.5 us (31%)
  starting transfers between devices  22.8 us (27%)
  local copies, waits for them, and re-layouts  7.07 us (8%)
    ppermute x8, starting transfers between devices, shifted(): return lax.ppermute(array, axis, pairs)  21.2 us
    psum x1, blocking collectives, on_device(): group_node = lax.psum(device_term, 'list')  17.8 us
    all_gather x1, blocking collectives, on_device(): piece = lax.all_gather(flattened, 'list', axis=0, tiled=True)  9.12 us
    dot_general x8, matrix products, upper_exchange(): contribution = jnp.dot(source, matrices[slot_index].T, precision=highest)  7.6 us
    dot_general x1, matrix products, on_device(): jnp.einsum('ckrm,cknm->crn', neighbours, near_blocks, preferred_element_t...  6.8 us
    reshape x1, local copies, waits for them, and re-layouts, on_device(): selected.reshape(leaf_local, far_slots, skeleton.shape[1], skeleton.shape...  4.24 us
    dot_general x1, matrix products, on_device(): jnp.einsum('rd,ild->irl', device_down, leaf_transfer, precision=highest)  2.82 us
    gather x1, local copies, waits for them, and re-layouts, on_device(): neighbours = jnp.take(panel_charges, near_list.reshape(-1), axis=0)  2 us
  transfers between devices with their start and end apart: 9, of which 0 were waited for; matrix products, arithmetic and copies ran while one was open for 30% of the time, Pallas kernels for 0%

commit v1 on v0

v1 whole, which is shorter than its diff:
```python
import functools

import jax
import jax.numpy as jnp
from jax import lax
from jax.experimental import pallas as pl
from jax.experimental.pallas import tpu as pltpu
from jax.sharding import PartitionSpec as P

highest = lax.Precision.HIGHEST
offsets = (-3, -2, 2, 3)
f32 = jnp.float32
bf16 = jnp.bfloat16
whole = pl.BlockSpec(memory_space=pltpu.VMEM)
scalars = pl.BlockSpec(memory_space=pltpu.SMEM)


def params(mebibytes):
    return pltpu.CompilerParams(vmem_limit_bytes=mebibytes << 20)


def times(left, right):
    return lax.dot_general(left, right, (((1,), (0,)), ((), ())), preferred_element_type=f32)


def times_transposed(left, right):
    return lax.dot_general(left, right, (((1,), (1,)), ((), ())), preferred_element_type=f32)


def split(array):
    high = array.astype(bf16)
    return high, (array - high.astype(f32)).astype(bf16)


def exact(product, left, right):
    left_high, left_low = split(left)
    right_high, right_low = split(right)
    return product(left_high, right_high) + (
        product(left_low, right_high) + product(left_high, right_low)
    )


def upward_kernel(charges, basis, transfer, device_transfer, payload):
    pair_count = charges.shape[0] // 2
    rank = basis.shape[1]
    node = jnp.zeros((charges.shape[1], rank), f32)
    for pair in range(pair_count):
        halves = [
            times_transposed(charges[leaf], basis[leaf]).astype(bf16)
            for leaf in (2 * pair, 2 * pair + 1)
        ]
        skeleton = jnp.concatenate(halves, axis=1)
        payload[pair] = skeleton
        matrix = transfer[pl.ds(2 * pair, 2)].reshape(2 * rank, rank)
        high, low = split(matrix)
        node = node + (times(skeleton, high) + times(skeleton, low))
    term = exact(times, node, device_transfer[...])
    payload[pair_count] = jnp.concatenate(split(term), axis=1)


def near_kernel(near_list, charges, blocks, near):
    step = pl.program_id(0)
    leaves, slots = blocks.shape[0], blocks.shape[1]
    for leaf in range(leaves):
        total = None
        for slot in range(slots):
            source = near_list[step * leaves + leaf, slot]
            part = times_transposed(charges[source], blocks[leaf, slot])
            total = part if total is None else total + part
        near[leaf] = total


def sum_kernel(count, *refs):
    payloads, node = refs[:count], refs[count]
    rank = node.shape[1]
    total = None
    for payload in payloads:
        both = payload[payload.shape[0] - 1].astype(f32)
        part = both[:, :rank] + both[:, rank:]
        total = part if total is None else total + part
    node[...] = total


def far_kernel(peer_count, position, far_list, far_count, *refs):
    peers = refs[:peer_count]
    coupling, coupled, table = refs[peer_count:]
    leaves, slots, rank = coupling.shape[0], coupling.shape[1], coupling.shape[2]
    pair_count = leaves // 2
    for peer in range(peer_count):
        for pair in range(pair_count):
            block = peers[peer][pair]
            first, second = block[:, :rank], block[:, rank:]
            table[peer * leaves + 2 * pair] = jnp.concatenate([first, first], axis=1)
            table[peer * leaves + 2 * pair + 1] = jnp.concatenate([second, second], axis=1)
    own = position[1]
    rows = table.shape[1]
    lower = lax.broadcasted_iota(jnp.int32, (rows, 2 * rank), 1) < rank

    def one(leaf):
        used = far_count[leaf]
        total = jnp.zeros((rows, rank), f32)
        for slot in range(0, slots, 2):
            picked = []
            for each in (slot, slot + 1):
                source = far_list[leaf, each]
                device = source // leaves
                entry = ((device ^ own) - 1) * leaves + (source - device * leaves)
                block = table[entry]
                picked.append(jnp.where(each < used, block, jnp.zeros_like(block)))
            left = jnp.where(lower, picked[0], picked[1])
            right = jnp.concatenate([coupling[leaf, slot], coupling[leaf, slot + 1]], axis=1)
            total = total + times_transposed(left, right)
        return total

    @pl.loop(0, pair_count)
    def _(pair):
        coupled[pair] = jnp.concatenate([one(2 * pair), one(2 * pair + 1)], axis=1)


def down_kernel(chip_count, position, *refs):
    own_nodes, other_nodes = refs[:chip_count], refs[chip_count : 2 * chip_count]
    tree, couplings, device_transfer, transfer, basis, coupled, near, out, pairs = refs[
        2 * chip_count :
    ]
    rank = device_transfer.shape[0]
    leaf_count = 2 * chip_count
    depth = leaf_count.bit_length() - 2
    place = position[0]
    chip, core = place // 2, place % 2
    for distance in range(chip_count):
        own, other = own_nodes[distance][...], other_nodes[distance][...]
        pairs[chip ^ distance] = jnp.where(
            core == 0,
            jnp.concatenate([own, other], axis=1),
            jnp.concatenate([other, own], axis=1),
        )
    begin, stored = 0, 0
    summed = []
    for height in range(depth):
        members = leaf_count >> height
        spot = place >> height
        if 0 < height < depth - 1:
            below = stored
            stored += members
            for pair in range(members // 2):
                halves = [
                    exact(
                        times,
                        pairs[below + each],
                        tree[pl.ds(begin - 2 * members + 2 * each, 2)].reshape(2 * rank, rank),
                    )
                    for each in (2 * pair, 2 * pair + 1)
                ]
                pairs[stored + pair] = jnp.concatenate(halves, axis=1)
        total = jnp.zeros((pairs.shape[1], rank), f32)
        for slot, offset in enumerate(offsets):
            source = spot + offset
            usable = jnp.logical_and(source >= 0, source < members)
            if abs(offset) == 3:
                usable = jnp.logical_and(usable, spot % 2 == (0 if offset > 0 else 1))
            source = jnp.clip(source, 0, members - 1)
            if 0 < height == depth - 1:
                matrix = tree[pl.ds(begin - 2 * members + 2 * source, 2)]
                node = exact(times, pairs[stored + source], matrix.reshape(2 * rank, rank))
            else:
                both = pairs[stored + source // 2]
                node = jnp.where(source % 2 == 0, both[:, :rank], both[:, rank:])
            part = exact(times_transposed, node, couplings[begin + spot, slot])
            total = total + jnp.where(usable, part, jnp.zeros_like(part))
        summed.append(total)
        begin += members
    result = summed[-1]
    for height in reversed(range(depth - 1)):
        begin_row = 2 * leaf_count - 2 * (leaf_count >> height)
        matrix = tree[begin_row + (place >> height)]
        result = summed[height] + exact(times_transposed, result, matrix)
    down = exact(times_transposed, result, device_transfer[...])
    down_high, down_low = split(down)
    for pair in range(coupled.shape[0]):
        matrix = transfer[pl.ds(2 * pair, 2)].reshape(2 * rank, rank)
        high, low = split(matrix)
        above = times_transposed(down_high, high) + (
            times_transposed(down_low, high) + times_transposed(down_high, low)
        )
        coefficients = (coupled[pair] + above).astype(bf16)
        for half in range(2):
            leaf = 2 * pair + half
            far = times(coefficients[:, half * rank : (half + 1) * rank], basis[leaf])
            out[leaf] = (far + near[leaf]).astype(bf16)


def on_device(
    panel_charges,
    leaf_basis,
    near_blocks,
    near_list,
    far_list,
    far_count,
    far_coupling,
    leaf_transfer,
    device_transfer,
    tree_transfer,
    level_coupling,
):
    leaves, rows, panels = panel_charges.shape
    rank = leaf_basis.shape[1]
    list_count, leaf_count = lax.axis_size("list"), lax.axis_size("leaf")
    chip_count = leaf_count // 2
    position = jnp.stack([lax.axis_index("leaf"), lax.axis_index("list")]).astype(jnp.int32)
    device_matrix = device_transfer[0, 0]

    payload = pl.pallas_call(
        upward_kernel,
        out_shape=jax.ShapeDtypeStruct((leaves // 2 + 1, rows, 2 * rank), bf16),
        in_specs=[whole] * 4,
        out_specs=whole,
        compiler_params=params(16),
        name="upward",
    )(panel_charges, leaf_basis, leaf_transfer, device_matrix)

    peers = [
        lax.ppermute(payload, "list", [(i, i ^ distance) for i in range(list_count)])
        for distance in range(1, list_count)
    ]

    group = 2
    near = pl.pallas_call(
        near_kernel,
        grid_spec=pltpu.PrefetchScalarGridSpec(
            num_scalar_prefetch=1,
            grid=(leaves // group,),
            in_specs=[
                pl.BlockSpec((leaves, rows, panels), lambda i, _: (0, 0, 0)),
                pl.BlockSpec((group,) + near_blocks.shape[1:], lambda i, _: (i, 0, 0, 0)),
            ],
            out_specs=pl.BlockSpec((group, rows, panels), lambda i, _: (i, 0, 0)),
        ),
        out_shape=jax.ShapeDtypeStruct((leaves, rows, panels), f32),
        compiler_params=params(16),
        cost_estimate=pl.CostEstimate(
            flops=2 * near_blocks.size * rows, bytes_accessed=2 * near_blocks.size, transcendentals=0
        ),
        name="near",
    )(near_list, panel_charges, near_blocks)

    own_node = pl.pallas_call(
        functools.partial(sum_kernel, list_count),
        out_shape=jax.ShapeDtypeStruct((rows, rank), f32),
        in_specs=[whole] * list_count,
        out_specs=whole,
        name="group_sum",
    )(payload, *peers)

    own_nodes = [own_node] + [
        lax.ppermute(own_node, "leaf", [(i, i ^ 2 * distance) for i in range(leaf_count)])
        for distance in range(1, chip_count)
    ]
    other_nodes = [
        lax.ppermute(node, "leaf", [(i, i ^ 1) for i in range(leaf_count)]) for node in own_nodes
    ]

    coupled = pl.pallas_call(
        functools.partial(far_kernel, list_count - 1),
        out_shape=jax.ShapeDtypeStruct((leaves // 2, rows, 2 * rank), f32),
        in_specs=[scalars] * 3 + [whole] * list_count,
        out_specs=whole,
        scratch_shapes=[pltpu.VMEM(((list_count - 1) * leaves, rows, 2 * rank), bf16)],
        compiler_params=params(24),
        cost_estimate=pl.CostEstimate(
            flops=2 * far_coupling.size * rows * 4,
            bytes_accessed=4 * far_coupling.size,
            transcendentals=0,
        ),
        name="far",
    )(position, far_list, far_count, *peers, far_coupling)

    return pl.pallas_call(
        functools.partial(down_kernel, chip_count),
        out_shape=jax.ShapeDtypeStruct((leaves, rows, panels), bf16),
        in_specs=[scalars] + [whole] * (2 * chip_count + 7),
        out_specs=whole,
        scratch_shapes=[pltpu.VMEM((leaf_count, rows, 2 * rank), f32)],
        compiler_params=params(32),
        name="down",
    )(
        position,
        *own_nodes,
        *other_nodes,
        tree_transfer,
        level_coupling,
        device_matrix,
        leaf_transfer,
        leaf_basis,
        coupled,
        near,
    )


def solution(mesh):
    in_specs = (
        P(("leaf", "list"), None, None),
        P(("leaf", "list"), None, None),
        P(("leaf", "list"), None, None, None),
        P(("leaf", "list"), None),
        P(("leaf", "list"), None),
        P(("leaf", "list")),
        P(("leaf", "list"), None, None, None),
        P(("leaf", "list"), None, None),
        P("leaf", "list", None, None),
        P(),
        P(),
    )
    out_specs = P(("leaf", "list"), None, None)
    return jax.shard_map(
        on_device, mesh=mesh, in_specs=in_specs, out_specs=out_specs, check_vma=False
    )
```

time: 84.8 us -> 44.8 us (0.53)
  blocking collectives: 26.9 us -> 0 us
  matrix products: 26.5 us -> 0 us
  Pallas kernels: 0 us -> 15.3 us
  starting transfers between devices: 22.8 us -> 10 us
  waiting for transfers between devices: 0.02 us -> 5.82 us
  local copies, waits for them, and re-layouts: 7.07 us -> 12.7 us
    dot_general x19 -> x0, matrix products: 26.5 us -> none  [the longest x8 7.6 us: upper_exchange(): contribution = jnp.dot(source, matrices[slot_index].T, precision=highest)]
    psum x1 -> x0, blocking collectives: 17.8 us -> none  [on_device(): group_node = lax.psum(device_term, 'list')]
    pallas_call x0 -> x5, Pallas kernels: none -> 15.3 us  [the longest x1 5.04 us: on_device(): pl.pallas_call(functools.partial(down_kernel, chip_count), out_shape=jax....]
    ppermute x9 -> x10, starting transfers between devices: 22.8 us -> 10 us  [the longest x3 4.58 us: on_device(): lax.ppermute(payload, 'list', [(i, i ^ distance) for i in range(list_coun...]
    unnamed x18 -> x44, local copies, waits for them, and re-layouts: 0.19 us -> 12.7 us
    all_gather x1 -> x0, blocking collectives: 9.12 us -> none  [on_device(): piece = lax.all_gather(flattened, 'list', axis=0, tiled=True)]
    ppermute x9 -> x10, waiting for transfers between devices: 0.02 us -> 5.82 us  [the longest x3 5.81 us: on_device(): lax.ppermute(payload, 'list', [(i, i ^ distance) for i in range(list_coun...]
    reshape x3 -> x0, local copies, waits for them, and re-layouts: 4.59 us -> none  [the longest x1 4.24 us: on_device(): selected.reshape(leaf_local, far_slots, skeleton.shape[1], skeleton.shape...]
  transfers between devices with their start and end apart: 9 -> 10, of which waited for: 0 -> 3; matrix products, arithmetic and copies ran while one was open for 30% -> 4% of each run, Pallas kernels for 0% -> 17%
where the time goes in v1:
time: 44.8 us; the launch traced here: 44.2 us
  Pallas kernels  15.3 us (34%)
  local copies, waits for them, and re-layouts  12.7 us (28%)
  starting transfers between devices  10 us (22%)
  waiting for transfers between devices  5.82 us (13%)
    unnamed x44, local copies, waits for them, and re-layouts  12.7 us
    ppermute x3, waiting for transfers between devices, on_device(): lax.ppermute(payload, 'list', [(i, i ^ distance) for i in range(list_coun...  5.81 us
    pallas_call x1, Pallas kernels, on_device(): pl.pallas_call(functools.partial(down_kernel, chip_count), out_shape=jax....  5.04 us
    ppermute x3, starting transfers between devices, on_device(): lax.ppermute(payload, 'list', [(i, i ^ distance) for i in range(list_coun...  4.58 us
    ppermute x3, starting transfers between devices, on_device(): lax.ppermute(own_node, 'leaf', [(i, i ^ 2 * distance) for i in range(leaf...  4.39 us
    pallas_call x1, Pallas kernels, on_device(): pl.pallas_call(near_kernel, grid_spec=pltpu.PrefetchScalarGridSpec(num_sc...  4.19 us
    pallas_call x1, Pallas kernels, on_device(): pl.pallas_call(functools.partial(far_kernel, list_count - 1), out_shape=j...  3.48 us
    pallas_call x1, Pallas kernels, on_device(): pl.pallas_call(functools.partial(sum_kernel, list_count), out_shape=jax.S...  1.83 us
  transfers between devices with their start and end apart: 10, of which 3 were waited for; matrix products, arithmetic and copies ran while one was open for 4% of the time, Pallas kernels for 17%

profile of v1, /device:TPU:0, one launch (start us, length us, event | category | flops | bytes accessed | tf_op | source)
XLA Modules:
  0.0 44.2 jit_solution(326547864279442441)
XLA Ops:
  0.0 1.0 %copy-done.2 = bf16[16,64,256]{2,1,0:T(8,128)(2,1)S(1)} copy-done((bf16[16,64,256]{2,1,0:T(8,128)(2,1)S(1)}, bf16[16,64,256]{2,1,0:T(8,128)(2,1)}, u32[]{:S(2)}) %copy-start.2) | copy-done | bytes 524312
  1.0 1.0 %copy-done.4 = bf16[16,64,256]{2,1,0:T(8,128)(2,1)S(1)} copy-done((bf16[16,64,256]{2,1,0:T(8,128)(2,1)S(1)}, bf16[16,64,256]{2,1,0:T(8,128)(2,1)}, u32[]{:S(2)}) %copy-start.4) | copy-done | bytes 524312
  2.1 1.0 %copy-done.6 = f32[16,64,64]{2,1,0:T(8,128)S(1)} copy-done((f32[16,64,64]{2,1,0:T(8,128)S(1)}, f32[16,64,64]{2,1,0:T(8,128)}, u32[]{:S(2)}) %copy-start.6) | copy-done | bytes 262168
  3.1 0.8 %copy-done.17 = f32[1,1,64,64]{3,2,1,0:T(8,128)S(1)} copy-done((f32[1,1,64,64]{3,2,1,0:T(8,128)S(1)}, f32[1,1,64,64]{3,2,1,0:T(8,128)}, u32[]{:S(2)}) %copy-start.17) | copy-done | bytes 16408
  3.9 0.8 %upward.1.refs_0_ = bf16[9,64,128]{2,1,0:T(8,128)(2,1)S(1)} custom-call(bf16[16,64,256]{2,1,0:T(8,128)(2,1)S(1)} %copy-done.2, bf16[16,64,256]{2,1,0:T(8,128)(2,1)S(1)} %copy-done.4, f32[16,64,64]{2,1,0:T(8,128)S(1)} %copy-done.6, f32[64,64]{1,0:T(8,128)S(1)} %bitcast.3), custom_call_target="tpu_custom_call" | custom-call | tf_op jit(solution)/shard_map/upward/pallas_call | solution.py:212
  4.7 3.9 %collective-permute-start.2 = (bf16[9,64,128]{2,1,0:T(8,128)(2,1)S(1)}, bf16[9,64,128]{2,1,0:T(8,128)(2,1)S(1)}, u32[]{:S(2)}, u32[]{:S(2)}) collective-permute-start(bf16[9,64,128]{2,1,0:T(8,128)(2,1)S(1)} %upward.1.refs_0_), channel_id=1, source_target_pairs={{0,3},{1,2},{2,1},{3,0},{4,7},{5,6},{6,5},{7,4},{8,11},{9,10},{10,... | collective-permute-start | bytes 442376 | tf_op jit(solution)/shard_map/ppermute | solution.py:222
  8.6 0.5 %collective-permute-start.1 = (bf16[9,64,128]{2,1,0:T(8,128)(2,1)S(1)}, bf16[9,64,128]{2,1,0:T(8,128)(2,1)S(1)}, u32[]{:S(2)}, u32[]{:S(2)}) collective-permute-start(bf16[9,64,128]{2,1,0:T(8,128)(2,1)S(1)} %upward.1.refs_0_), channel_id=1, source_target_pairs={{0,2},{1,3},{2,0},{3,1},{4,6},{5,7},{6,4},{7,5},{8,10},{9,11},{10,... | collective-permute-start | bytes 442376 | tf_op jit(solution)/shard_map/ppermute | solution.py:222
  9.3 0.8 %copy.13.near_list = s32[16,4]{1,0:T(8,128)S(1)} copy(s32[16,4]{0,1:T(4,128)} %param.14) | data formatting | bytes 512 | tf_op args[3]
  10.1 2.8 %collective-permute-done.2.refs_3_.refs_2_ = bf16[9,64,128]{2,1,0:T(8,128)(2,1)S(1)} collective-permute-done((bf16[9,64,128]{2,1,0:T(8,128)(2,1)S(1)}, bf16[9,64,128]{2,1,0:T(8,128)(2,1)S(1)}, u32[]{:S(2)}, u32[]{:S(2)}) %collective-permute-start.2) | collective-permute-done | bytes 147488 | tf_op jit(solution)/shard_map/ppermute | solution.py:222
  12.9 2.7 %collective-permute-done.1.refs_2_.refs_1_ = bf16[9,64,128]{2,1,0:T(8,128)(2,1)S(1)} collective-permute-done((bf16[9,64,128]{2,1,0:T(8,128)(2,1)S(1)}, bf16[9,64,128]{2,1,0:T(8,128)(2,1)S(1)}, u32[]{:S(2)}, u32[]{:S(2)}) %collective-permute-start.1) | collective-permute-done | bytes 147488 | tf_op jit(solution)/shard_map/ppermute | solution.py:222
  16.3 0.7 %copy-done.13 = bf16[9,64,128]{2,1,0:T(8,128)(2,1)} copy-done((bf16[9,64,128]{2,1,0:T(8,128)(2,1)}, bf16[9,64,128]{2,1,0:T(8,128)(2,1)S(1)}, u32[]{:S(2)}) %copy-start.13) | copy-done | bytes 147480
  16.9 1.8 %group_sum.1.refs_0_ = f32[64,64]{1,0:T(8,128)} custom-call(bf16[9,64,128]{2,1,0:T(8,128)(2,1)} %copy-done.15, bf16[9,64,128]{2,1,0:T(8,128)(2,1)} %copy-done.13, bf16[9,64,128]{2,1,0:T(8,128)(2,1)} %copy-done.11, bf16[9,64,128]{2,1,0:T(8,128)(2,1)} %copy-done.9), custom_call_target="tpu_custom_call" | custom-call | tf_op jit(solution)/shard_map/group_sum/pallas_call | solution.py:246
  18.8 3.8 %collective-permute-start.5 = (f32[64,64]{1,0:T(8,128)}, f32[64,64]{1,0:T(8,128)S(1)}, u32[]{:S(2)}, u32[]{:S(2)}) collective-permute-start(f32[64,64]{1,0:T(8,128)} %group_sum.1.refs_0_), channel_id=1, source_target_pairs={{0,24},{4,28},{8,16},{12,20},{16,8},{20,12},{24,0},{28,4},{1,25},{... | collective-permute-start | bytes 49160 | tf_op jit(solution)/shard_map/ppermute | solution.py:255
  22.6 0.6 %collective-permute-start.3 = (f32[64,64]{1,0:T(8,128)}, f32[64,64]{1,0:T(8,128)}, u32[]{:S(2)}, u32[]{:S(2)}) collective-permute-start(f32[64,64]{1,0:T(8,128)} %group_sum.1.refs_0_), channel_id=1, source_target_pairs={{0,8},{4,12},{8,0},{12,4},{16,24},{20,28},{24,16},{28,20},{1,9},{5... | collective-permute-start | bytes 49160 | tf_op jit(solution)/shard_map/ppermute | solution.py:255
  23.2 3.4 %copy-done = bf16[16,4,256,256]{3,2,1,0:T(8,128)(2,1)S(1)} copy-done((bf16[16,4,256,256]{3,2,1,0:T(8,128)(2,1)S(1)}, bf16[16,4,256,256]{3,2,1,0:T(8,128)(2,1)}, u32[]{:S(2)}) %copy-start) | copy-done | bytes 8388632
  26.5 1.0 %copy-done.3 = bf16[16,64,256]{2,1,0:T(8,128)(2,1)S(1)} copy-done((bf16[16,64,256]{2,1,0:T(8,128)(2,1)S(1)}, bf16[16,64,256]{2,1,0:T(8,128)(2,1)}, u32[]{:S(2)}) %copy-start.3) | copy-done | bytes 524312
  27.6 4.2 %near.1.refs_14_ = f32[16,64,256]{2,1,0:T(8,128)S(1)} custom-call(s32[16,4]{1,0:T(8,128)S(1)} %copy.13.near_list, bf16[16,64,256]{2,1,0:T(8,128)(2,1)S(1)} %copy-done.3, bf16[16,4,256,256]{3,2,1,0:T(8,128)(2,1)S(1)} %copy-done), custom_call_target="tpu_custom_call" | custom-call | flops 536870912 | bytes 8388608 | tf_op jit(solution)/shard_map/near/pallas_call | solution.py:227
  31.8 0.8 %copy.12.far_list = s32[16,8]{1,0:T(8,128)S(1)} copy(s32[16,8]{0,1:T(8,128)} %param.15) | data formatting | bytes 1024 | tf_op args[4]
  32.7 0.5 %collective-permute-start.9 = (f32[64,64]{1,0:T(8,128)S(1)}, f32[64,64]{1,0:T(8,128)S(1)}, u32[]{:S(2)}, u32[]{:S(2)}) collective-permute-start(f32[64,64]{1,0:T(8,128)S(1)} %collective-permute-done.5.refs_3_), channel_id=1, source_target_pairs={{0,4},{4,0},{8,12},{12,8},{16,20},{20,16},{24,28},{28,24},{1,5},{5... | collective-permute-start | bytes 49160 | tf_op jit(solution)/shard_map/ppermute | solution.py:259
  33.2 0.4 collective-permute-start.7
  33.7 0.9 %copy-done.14 = bf16[9,64,128]{2,1,0:T(8,128)(2,1)S(1)} copy-done((bf16[9,64,128]{2,1,0:T(8,128)(2,1)S(1)}, bf16[9,64,128]{2,1,0:T(8,128)(2,1)}, u32[]{:S(2)}) %copy-start.14) | copy-done | bytes 147480
  34.6 3.5 %far.1.refs_13_ = f32[8,64,128]{2,1,0:T(8,128)S(1)} custom-call(s32[2]{0:T(128)S(1)} %pad_add_fusion.position, s32[16,8]{1,0:T(8,128)S(1)} %copy.12.far_list, s32[16]{0:T(128)S(1)} %copy-done.20, bf16[9,64,128]{2,1,0:T(8,128)(2,1)S(1)} %copy-done.14, bf16[9,64,128]{2,1,0:T(8,128)(2,1)S(1)} %copy-done.12, bf16[9,64,128]{2,1,0:T(8,128)(2,1)S(1)} %copy-done.10, ...), custom_call_target="tpu_custom_call" | custom-call | flops 268435456 | bytes 2097152 | tf_op jit(solution)/shard_map/far/pallas_call | solution.py:262
  38.2 0.9 %copy-done.16 = f32[8,64,64]{2,1,0:T(8,128)S(1)} copy-done((f32[8,64,64]{2,1,0:T(8,128)S(1)}, f32[8,64,64]{2,1,0:T(8,128)}, u32[]{:S(2)}) %copy-start.16) | copy-done | bytes 131096
  39.1 5.0 %down.1 = bf16[16,64,256]{2,1,0:T(8,128)(2,1)} custom-call(s32[2]{0:T(128)S(1)} %pad_add_fusion.position, f32[64,64]{1,0:T(8,128)S(1)} %copy-done.19, f32[64,64]{1,0:T(8,128)} %collective-permute-done.3.refs_1_, f32[64,64]{1,0:T(8,128)} %collective-permute-done.4.refs_2_, f32[64,64]{1,0:T(8,128)S(1)} %collective-permute-done.5.refs_3_, ...), custom_call_target="tpu_custom_call" | custom-call | tf_op jit(solution)/shard_map/down/pallas_call | solution.py:277
  (46 shorter events, 1.1 us)
Async XLA Ops:
  0.0 1.0 %copy-start.2 = (bf16[16,64,256]{2,1,0:T(8,128)(2,1)S(1)}, bf16[16,64,256]{2,1,0:T(8,128)(2,1)}, u32[]{:S(2)}) copy-start(bf16[16,64,256]{2,1,0:T(8,128)(2,1)} %charges.3) | copy-start | bytes 1572868
  1.0 1.0 %copy-start.4 = (bf16[16,64,256]{2,1,0:T(8,128)(2,1)S(1)}, bf16[16,64,256]{2,1,0:T(8,128)(2,1)}, u32[]{:S(2)}) copy-start(bf16[16,64,256]{2,1,0:T(8,128)(2,1)} %refs_12_.1) | copy-start | bytes 1572868
  4.7 11.2 %copy-start.15 = (bf16[9,64,128]{2,1,0:T(8,128)(2,1)}, bf16[9,64,128]{2,1,0:T(8,128)(2,1)S(1)}, u32[]{:S(2)}) copy-start(bf16[9,64,128]{2,1,0:T(8,128)(2,1)S(1)} %upward.1.refs_0_) | copy-start | bytes 442372
  4.7 8.2 %collective-permute-start.2 = (bf16[9,64,128]{2,1,0:T(8,128)(2,1)S(1)}, bf16[9,64,128]{2,1,0:T(8,128)(2,1)S(1)}, u32[]{:S(2)}, u32[]{:S(2)}) collective-permute-start(bf16[9,64,128]{2,1,0:T(8,128)(2,1)S(1)} %upward.1.refs_0_), channel_id=1, source_target_pairs={{0,3},{1,2},{2,1},{3,0},{4,7},{5,6},{6,5},{7,4},{8,11},{9,10},{10,... | collective-permute-start | bytes 442376 | tf_op jit(solution)/shard_map/ppermute | solution.py:222
  8.6 7.0 %collective-permute-start.1 = (bf16[9,64,128]{2,1,0:T(8,128)(2,1)S(1)}, bf16[9,64,128]{2,1,0:T(8,128)(2,1)S(1)}, u32[]{:S(2)}, u32[]{:S(2)}) collective-permute-start(bf16[9,64,128]{2,1,0:T(8,128)(2,1)S(1)} %upward.1.refs_0_), channel_id=1, source_target_pairs={{0,2},{1,3},{2,0},{3,1},{4,6},{5,7},{6,4},{7,5},{8,10},{9,11},{10,... | collective-permute-start | bytes 442376 | tf_op jit(solution)/shard_map/ppermute | solution.py:222
  9.1 6.8 %collective-permute-start = (bf16[9,64,128]{2,1,0:T(8,128)(2,1)S(1)}, bf16[9,64,128]{2,1,0:T(8,128)(2,1)S(1)}, u32[]{:S(2)}, u32[]{:S(2)}) collective-permute-start(bf16[9,64,128]{2,1,0:T(8,128)(2,1)S(1)} %upward.1.refs_0_), channel_id=1, source_target_pairs={{0,1},{1,0},{2,3},{3,2},{4,5},{5,4},{6,7},{7,6},{8,9},{9,8},{10,11... | collective-permute-start | bytes 442376 | tf_op jit(solution)/shard_map/ppermute | solution.py:222
  12.9 3.0 %copy-start.9 = (bf16[9,64,128]{2,1,0:T(8,128)(2,1)}, bf16[9,64,128]{2,1,0:T(8,128)(2,1)S(1)}, u32[]{:S(2)}) copy-start(bf16[9,64,128]{2,1,0:T(8,128)(2,1)S(1)} %collective-permute-done.2.refs_3_.refs_2_) | copy-start | bytes 442372
  16.9 16.7 %copy-start.20 = (s32[16]{0:T(128)S(1)}, s32[16]{0:T(128)}, u32[]{:S(2)}) copy-start(s32[16]{0:T(128)} %far_count.1) | copy-start | bytes 196
  18.8 13.9 %collective-permute-start.5 = (f32[64,64]{1,0:T(8,128)}, f32[64,64]{1,0:T(8,128)S(1)}, u32[]{:S(2)}, u32[]{:S(2)}) collective-permute-start(f32[64,64]{1,0:T(8,128)} %group_sum.1.refs_0_), channel_id=1, source_target_pairs={{0,24},{4,28},{8,16},{12,20},{16,8},{20,12},{24,0},{28,4},{1,25},{... | collective-permute-start | bytes 49160 | tf_op jit(solution)/shard_map/ppermute | solution.py:255
  22.6 10.6 %collective-permute-start.4 = (f32[64,64]{1,0:T(8,128)}, f32[64,64]{1,0:T(8,128)}, u32[]{:S(2)}, u32[]{:S(2)}) collective-permute-start(f32[64,64]{1,0:T(8,128)} %group_sum.1.refs_0_), channel_id=1, source_target_pairs={{0,16},{4,20},{8,24},{12,28},{16,0},{20,4},{24,8},{28,12},{1,17},{... | collective-permute-start | bytes 49160 | tf_op jit(solution)/shard_map/ppermute | solution.py:255
  22.6 10.7 %collective-permute-start.3 = (f32[64,64]{1,0:T(8,128)}, f32[64,64]{1,0:T(8,128)}, u32[]{:S(2)}, u32[]{:S(2)}) collective-permute-start(f32[64,64]{1,0:T(8,128)} %group_sum.1.refs_0_), channel_id=1, source_target_pairs={{0,8},{4,12},{8,0},{12,4},{16,24},{20,28},{24,16},{28,20},{1,9},{5... | collective-permute-start | bytes 49160 | tf_op jit(solution)/shard_map/ppermute | solution.py:255
  23.2 3.4 %copy-start = (bf16[16,4,256,256]{3,2,1,0:T(8,128)(2,1)S(1)}, bf16[16,4,256,256]{3,2,1,0:T(8,128)(2,1)}, u32[]{:S(2)}) copy-start(bf16[16,4,256,256]{3,2,1,0:T(8,128)(2,1)} %blocks.1) | copy-start | bytes 25165828
  27.6 5.0 %copy-start.19 = (f32[64,64]{1,0:T(8,128)S(1)}, f32[64,64]{1,0:T(8,128)}, u32[]{:S(2)}) copy-start(f32[64,64]{1,0:T(8,128)} %group_sum.1.refs_0_) | copy-start | bytes 49156
  27.6 6.1 %copy-start.1 = (bf16[16,8,64,64]{3,2,1,0:T(8,128)(2,1)S(1)}, bf16[16,8,64,64]{3,2,1,0:T(8,128)(2,1)}, u32[]{:S(2)}) copy-start(bf16[16,8,64,64]{3,2,1,0:T(8,128)(2,1)} %refs_3_.1) | copy-start | bytes 3145732
  27.6 6.1 %copy-start.10 = (bf16[9,64,128]{2,1,0:T(8,128)(2,1)S(1)}, bf16[9,64,128]{2,1,0:T(8,128)(2,1)}, u32[]{:S(2)}) copy-start(bf16[9,64,128]{2,1,0:T(8,128)(2,1)} %copy-done.9) | copy-start | bytes 442372
  27.6 6.1 %copy-start.12 = (bf16[9,64,128]{2,1,0:T(8,128)(2,1)S(1)}, bf16[9,64,128]{2,1,0:T(8,128)(2,1)}, u32[]{:S(2)}) copy-start(bf16[9,64,128]{2,1,0:T(8,128)(2,1)} %copy-done.11) | copy-start | bytes 442372
  27.6 10.5 %copy-start.18 = (f32[1,1,64,64]{3,2,1,0:T(8,128)S(1)}, f32[1,1,64,64]{3,2,1,0:T(8,128)}, u32[]{:S(2)}) copy-start(f32[1,1,64,64]{3,2,1,0:T(8,128)} %param.19) | copy-start | bytes 49156
  32.6 5.6 %copy-start.5 = (bf16[16,64,256]{2,1,0:T(8,128)(2,1)S(1)}, bf16[16,64,256]{2,1,0:T(8,128)(2,1)}, u32[]{:S(2)}) copy-start(bf16[16,64,256]{2,1,0:T(8,128)(2,1)} %refs_12_.1) | copy-start | bytes 1572868
  32.6 5.6 %copy-start.7 = (f32[16,64,64]{2,1,0:T(8,128)S(1)}, f32[16,64,64]{2,1,0:T(8,128)}, u32[]{:S(2)}) copy-start(f32[16,64,64]{2,1,0:T(8,128)} %refs_11_.1) | copy-start | bytes 786436
  32.6 5.6 %copy-start.8 = (f32[12,4,64,64]{3,2,1,0:T(8,128)S(1)}, f32[12,4,64,64]{3,2,1,0:T(8,128)}, u32[]{:S(2)}) copy-start(f32[12,4,64,64]{3,2,1,0:T(8,128)} %refs_9_.1) | copy-start | bytes 2359300
  32.6 5.5 %collective-permute-start.6 = (f32[64,64]{1,0:T(8,128)S(1)}, f32[64,64]{1,0:T(8,128)S(1)}, u32[]{:S(2)}, u32[]{:S(2)}) collective-permute-start(f32[64,64]{1,0:T(8,128)S(1)} %copy-done.19), channel_id=1, source_target_pairs={{0,4},{4,0},{8,12},{12,8},{16,20},{20,16},{24,28},{28,24},{1,5},{5... | collective-permute-start | bytes 49160 | tf_op jit(solution)/shard_map/ppermute | solution.py:259
  32.7 5.4 %collective-permute-start.9 = (f32[64,64]{1,0:T(8,128)S(1)}, f32[64,64]{1,0:T(8,128)S(1)}, u32[]{:S(2)}, u32[]{:S(2)}) collective-permute-start(f32[64,64]{1,0:T(8,128)S(1)} %collective-permute-done.5.refs_3_), channel_id=1, source_target_pairs={{0,4},{4,0},{8,12},{12,8},{16,20},{20,16},{24,28},{28,24},{1,5},{5... | collective-permute-start | bytes 49160 | tf_op jit(solution)/shard_map/ppermute | solution.py:259
  33.2 4.9 %collective-permute-start.8 = (f32[64,64]{1,0:T(8,128)}, f32[64,64]{1,0:T(8,128)S(1)}, u32[]{:S(2)}, u32[]{:S(2)}) collective-permute-start(f32[64,64]{1,0:T(8,128)} %collective-permute-done.4.refs_2_), channel_id=1, source_target_pairs={{0,4},{4,0},{8,12},{12,8},{16,20},{20,16},{24,28},{28,24},{1,5},{5... | collective-permute-start | bytes 49160 | tf_op jit(solution)/shard_map/ppermute | solution.py:259
  33.2 4.9 %collective-permute-start.7 = (f32[64,64]{1,0:T(8,128)}, f32[64,64]{1,0:T(8,128)S(1)}, u32[]{:S(2)}, u32[]{:S(2)}) collective-permute-start(f32[64,64]{1,0:T(8,128)} %collective-permute-done.3.refs_1_), channel_id=1, source_target_pairs={{0,4},{4,0},{8,12},{12,8},{16,20},{20,16},{24,28},{28,24},{1,5},{5... | collective-permute-start | bytes 49160 | tf_op jit(solution)/shard_map/ppermute | solution.py:259
  (7 other events, 6.0 us)

commit v2 on v0

v2 whole, which is shorter than its diff:
```python
import functools

import jax
import jax.numpy as jnp
from jax import lax
from jax.experimental import pallas as pl
from jax.experimental.pallas import tpu as pltpu
from jax.sharding import PartitionSpec as P

offsets = (-3, -2, 2, 3)
f32 = jnp.float32
bf16 = jnp.bfloat16
whole = pl.BlockSpec(memory_space=pltpu.VMEM)
scalars = pl.BlockSpec(memory_space=pltpu.SMEM)
anywhere = pl.BlockSpec(memory_space=pl.ANY)


def params(mebibytes):
    return pltpu.CompilerParams(vmem_limit_bytes=mebibytes << 20)


def times(left, right):
    return lax.dot_general(left, right, (((1,), (0,)), ((), ())), preferred_element_type=f32)


def times_transposed(left, right):
    return lax.dot_general(left, right, (((1,), (1,)), ((), ())), preferred_element_type=f32)


def split(array):
    high = array.astype(bf16)
    return high, (array - high.astype(f32)).astype(bf16)


def exact(product, left, right):
    left_high, left_low = split(left)
    right_high, right_low = split(right)
    return product(left_high, right_high) + (
        product(left_low, right_high) + product(left_high, right_low)
    )


def upward_kernel(count, *refs):
    sources, blocks_in = refs[:count], refs[count]
    payload, term_parts = refs[count + 1 : count + 3]
    kept, blocks = refs[count + 3 : count + 7], refs[count + 7]
    basis, transfer, matrix, sem = refs[count + 8 :]
    charges = kept[0]
    targets = (charges, basis, transfer, matrix) + kept[1:]
    copies = [
        pltpu.make_async_copy(source, target, sem.at[i])
        for i, (source, target) in enumerate(zip(sources, targets))
    ]
    for copy in copies:
        copy.start()
    ahead = pltpu.make_async_copy(blocks_in.at[pl.ds(0, blocks.shape[0])], blocks, sem.at[count])
    ahead.start()
    for copy in copies:
        copy.wait()
    pair_count = charges.shape[0] // 2
    rank = basis.shape[1]
    node = jnp.zeros((charges.shape[1], rank), f32)
    for pair in range(pair_count):
        halves = [
            times_transposed(charges[leaf], basis[leaf]).astype(bf16)
            for leaf in (2 * pair, 2 * pair + 1)
        ]
        skeleton = jnp.concatenate(halves, axis=1)
        payload[pair] = skeleton
        block = transfer[pl.ds(2 * pair, 2)].reshape(2 * rank, rank)
        high, low = split(block)
        node = node + (times(skeleton, high) + times(skeleton, low))
    term = exact(times, node, matrix[...])
    both = jnp.concatenate(split(term), axis=1)
    term_parts[...] = both
    payload[pair_count] = both
    ahead.wait()


def near_leaf(near_list, charges, blocks, row, leaf):
    total = None
    for slot in range(blocks.shape[1]):
        part = times_transposed(charges[near_list[slot, leaf]], blocks[row, slot])
        total = part if total is None else total + part
    return total


def near_begin_kernel(near_list, charges, blocks, near):
    for leaf in range(near.shape[0]):
        near[leaf] = near_leaf(near_list, charges, blocks, leaf, leaf)


def near_rest_kernel(sizes, near_list, charges, blocks_in, near, buffer, sem):
    count = near.shape[0]
    first = charges.shape[0] - count
    begins = [sum(sizes[:i]) for i in range(len(sizes))]
    copies = [
        pltpu.make_async_copy(
            blocks_in.at[pl.ds(first + begin, size)], buffer.at[pl.ds(begin, size)], sem.at[i]
        )
        for i, (begin, size) in enumerate(zip(begins, sizes))
    ]
    for copy in copies:
        copy.start()
    for copy, begin, size in zip(copies, begins, sizes):
        copy.wait()
        for row in range(begin, begin + size):
            near[row] = near_leaf(near_list, charges, buffer, row, first + row)


def pack_kernel(term_parts, near, payload_in, payload, terms):
    place = payload.shape[0] - 1
    payload[place] = term_parts[...]
    terms[0] = payload_in[place - 1]
    terms[1] = term_parts[...]


def sum_kernel(count, bases, *refs):
    arrays, (pair, *copies) = refs[:count], refs[count + 1 :]
    rank = pair.shape[1] // 2
    totals = [None, None]
    for array in arrays:
        for side in range(2):
            both = array[array.shape[0] - 2 + side].astype(f32)
            part = both[:, :rank] + both[:, rank:]
            totals[side] = part if totals[side] is None else totals[side] + part
    pair[...] = jnp.concatenate(totals, axis=1)
    for base, copy in zip(bases, copies):
        copy[...] = arrays[base][pl.ds(0, copy.shape[0])]


def tree_kernel(
    leaf_count,
    position,
    tree_in,
    couplings_in,
    matrix_in,
    transfer_in,
    basis_in,
    near,
    down_high,
    down_low,
    above,
    basis,
    tree,
    couplings,
    matrix,
    transfer,
    down,
    sem,
):
    rank = matrix.shape[0]
    depth = leaf_count.bit_length() - 2
    place = position[0]
    begins = [2 * leaf_count - 2 * (leaf_count >> height) for height in range(depth)]
    copies = [
        pltpu.make_async_copy(source, target, sem.at[i])
        for i, (source, target) in enumerate(
            [(matrix_in, matrix), (tree_in, tree)]
            + [
                (couplings_in.at[begins[height] + (place >> height)], couplings.at[height])
                for height in range(depth)
            ]
            + [(transfer_in, transfer), (basis_in, basis)]
        )
    ]
    for copy in copies:
        copy.start()
    down[...] = jnp.zeros_like(down)
    for copy in copies[:-2]:
        copy.wait()
    back = matrix[...]
    for height in range(depth):
        members = leaf_count >> height
        spot = place >> height
        for slot, offset in enumerate(offsets):
            source = spot + offset
            usable = jnp.logical_and(source >= 0, source < members)
            if abs(offset) == 3:
                usable = jnp.logical_and(usable, spot % 2 == (0 if offset > 0 else 1))
            entry = begins[height] + jnp.clip(source, 0, members - 1)
            part = exact(times, back, couplings[height, slot])
            down[entry] += jnp.where(usable, part, jnp.zeros_like(part))
        if height < depth - 1:
            back = exact(times, back, tree[begins[height] + spot])
    for height in reversed(range(depth - 1)):
        for parent in range(leaf_count >> (height + 1)):
            for child in (2 * parent, 2 * parent + 1):
                down[begins[height] + child] += exact(
                    times_transposed, down[begins[height + 1] + parent], tree[begins[height] + child]
                )
    for node in range(leaf_count):
        high, low = split(down[node])
        down_high[node] = high
        down_low[node] = low
    copies[-2].wait()
    for leaf in range(transfer.shape[0]):
        high, low = split(transfer[leaf])
        above[leaf] = jnp.concatenate([high, high, low], axis=1)
    copies[-1].wait()


def relay_kernel(count, *refs):
    out = refs[count + 1]
    for i in range(count):
        out[i] = refs[i][...]


def far_kernel(peer_count, position, far_list, far_count, *refs):
    peers = refs[:peer_count]
    coupling, coupled, table = refs[peer_count:]
    leaves, slots, rank = coupling.shape[0], coupling.shape[1], coupling.shape[2]
    rows = table.shape[1]
    pair_count = leaves // 2
    empty = peer_count * leaves
    table[empty] = jnp.zeros(table.shape[1:], bf16)
    for peer in range(peer_count):
        for pair in range(pair_count):
            block = peers[peer][pair]
            first, second = block[:, :rank], block[:, rank:]
            table[peer * leaves + 2 * pair] = jnp.concatenate([first, first], axis=1)
            table[peer * leaves + 2 * pair + 1] = jnp.concatenate([second, second], axis=1)
    own = position[1]
    lower = lax.broadcasted_iota(jnp.int32, (rows, 2 * rank), 1) < rank

    def entry(leaf, slot):
        source = far_list[slot, leaf]
        device = source // leaves
        place = ((device ^ own) - 1) * leaves + (source - device * leaves)
        return jnp.where(slot < far_count[0, leaf], place, empty)

    def one(leaf):
        lefts, rights = [], []
        for slot in range(0, slots, 2):
            lefts.append(
                jnp.where(lower, table[entry(leaf, slot)], table[entry(leaf, slot + 1)])
            )
            rights.append(
                jnp.concatenate([coupling[leaf, slot], coupling[leaf, slot + 1]], axis=1)
            )
        return times_transposed(
            jnp.concatenate(lefts, axis=1), jnp.concatenate(rights, axis=1)
        )

    for pair in range(pair_count):
        coupled[pair] = jnp.concatenate([one(2 * pair), one(2 * pair + 1)], axis=1)


def down_kernel(distances, position, *refs):
    steps = len(distances[0])
    own_pair, received, swapped = refs[0], refs[1 : 1 + steps], refs[1 + steps]
    down_high, down_low, above, basis, coupled, near_begin, near_rest, out, buffer, sem = refs[
        2 + steps :
    ]
    rank = basis.shape[1]
    place = position[0]
    chip, core = place // 2, place % 2

    def product(both, chip_at, flipped):
        first = 2 * chip_at + (core ^ flipped)
        second = 2 * chip_at + (1 - (core ^ flipped))
        high = jnp.concatenate([down_high[first], down_high[second]], axis=1)
        low = jnp.concatenate([down_low[first], down_low[second]], axis=1)
        both_high, both_low = split(both)
        return times_transposed(
            jnp.concatenate([both_high, both_low, both_high], axis=1),
            jnp.concatenate([high, high, low], axis=1),
        )

    total = product(own_pair[...], chip, 0)
    for step in range(steps):
        for flipped in range(2):
            both = swapped[step] if flipped else received[step][...]
            apart = [distances[core_at ^ flipped] for core_at in range(2)]
            fresh = [apart[core_at].index(apart[core_at][step]) == step for core_at in range(2)]
            if not all(fresh):
                usable = core == fresh.index(True)
                both = jnp.where(usable, both, jnp.zeros_like(both))
            at = chip ^ jnp.where(core == 0, apart[0][step], apart[1][step])
            total = total + product(both, at, flipped)
    high, low = split(total)
    wide = jnp.concatenate([high, low, high], axis=1)
    copies = []
    group = 4
    for begin in range(0, basis.shape[0], group):
        for pair in range(begin // 2, (begin + group) // 2):
            matrix = above[pl.ds(2 * pair, 2)].reshape(2 * rank, 3 * rank)
            coefficients = (coupled[pair] + times_transposed(wide, matrix)).astype(bf16)
            for half in range(2):
                leaf = 2 * pair + half
                count = near_begin.shape[0]
                near = near_begin[leaf] if leaf < count else near_rest[leaf - count]
                far = times(coefficients[:, half * rank : (half + 1) * rank], basis[leaf])
                buffer[leaf] = (far + near).astype(bf16)
        rows = pl.ds(begin, group)
        copy = pltpu.make_async_copy(buffer.at[rows], out.at[rows], sem.at[begin // group])
        copy.start()
        copies.append(copy)
    for copy in copies:
        copy.wait()


def on_device(
    panel_charges,
    leaf_basis,
    near_blocks,
    near_list,
    far_list,
    far_count,
    far_coupling,
    leaf_transfer,
    device_transfer,
    tree_transfer,
    level_coupling,
):
    leaves, rows, panels = panel_charges.shape
    rank = leaf_basis.shape[1]
    list_count, leaf_count = lax.axis_size("list"), lax.axis_size("leaf")
    chip_count = leaf_count // 2
    position = jnp.stack([lax.axis_index("leaf"), lax.axis_index("list")]).astype(jnp.int32)

    def like(array, dtype=None):
        return jax.ShapeDtypeStruct(array.shape, dtype or array.dtype)

    def shape(*dims, dtype=bf16):
        return jax.ShapeDtypeStruct(dims, dtype)

    def stay(array):
        return pltpu.with_memory_space_constraint(array, pltpu.HBM)

    def exchange(array, axis, distance):
        pairs = [(i, i ^ distance) for i in range(lax.axis_size(axis))]
        return lax.ppermute(array, axis, pairs)

    ahead = leaves // 8
    inputs = [stay(panel_charges), stay(leaf_basis), stay(leaf_transfer)]
    inputs += [stay(device_transfer[0, 0]), near_list.T, far_list.T, far_count[None]]
    blocks_in = stay(near_blocks)
    count = len(inputs)
    payload, term_parts, charges, near_list, far_list, far_count, blocks_ahead = pl.pallas_call(
        functools.partial(upward_kernel, count),
        out_shape=[
            shape(leaves // 2 + 2, rows, 2 * rank),
            shape(rows, 2 * rank),
            like(panel_charges),
            *[like(array) for array in inputs[4:]],
            shape(ahead, *near_blocks.shape[1:]),
        ],
        in_specs=[anywhere] * (count + 1),
        out_specs=[whole] * 7,
        scratch_shapes=[
            pltpu.VMEM(leaf_basis.shape, bf16),
            pltpu.VMEM(leaf_transfer.shape, f32),
            pltpu.VMEM((rank, rank), f32),
            pltpu.SemaphoreType.DMA((count + 1,)),
        ],
        compiler_params=params(8),
        name="upward",
    )(*inputs[:4], *[stay(array) for array in inputs[4:]], blocks_in)

    other_parts = exchange(term_parts, "leaf", 1)

    near_begin = pl.pallas_call(
        near_begin_kernel,
        out_shape=shape(ahead, rows, panels, dtype=f32),
        in_specs=[scalars, whole, whole],
        out_specs=whole,
        compiler_params=params(4),
        name="near_begin",
    )(near_list, charges, blocks_ahead)

    payload, terms = pl.pallas_call(
        pack_kernel,
        out_shape=[like(payload), shape(2, rows, 2 * rank)],
        in_specs=[whole, anywhere, whole],
        out_specs=[whole, whole],
        input_output_aliases={2: 0},
        compiler_params=params(2),
        name="pack",
    )(other_parts, near_begin, payload)

    direct = [distance for distance in range(1, list_count) if distance & (distance - 1) == 0]
    arrived = {
        distance: exchange(payload if distance in direct else terms, "list", distance)
        for distance in range(1, list_count)
    }

    sizes = (2, 4, 4, 4)
    near_rest = pl.pallas_call(
        functools.partial(near_rest_kernel, sizes),
        out_shape=shape(leaves - ahead, rows, panels, dtype=f32),
        in_specs=[scalars, whole, anywhere],
        out_specs=whole,
        scratch_shapes=[
            pltpu.VMEM((leaves - ahead,) + near_blocks.shape[1:], bf16),
            pltpu.SemaphoreType.DMA((len(sizes),)),
        ],
        compiler_params=params(12),
        cost_estimate=pl.CostEstimate(
            flops=2 * near_blocks.size * rows,
            bytes_accessed=2 * near_blocks.size,
            transcendentals=0,
        ),
        name="near_rest",
    )(near_list, charges, blocks_in)

    bases = direct[:-1]
    own_pair, *copied = pl.pallas_call(
        functools.partial(sum_kernel, list_count, bases),
        out_shape=[shape(rows, 2 * rank, dtype=f32)]
        + [shape(leaves // 2, rows, 2 * rank) for _ in bases],
        in_specs=[whole] * list_count + [anywhere],
        out_specs=[whole] * (1 + len(bases)),
        compiler_params=params(4),
        name="group_sum",
    )(payload, *[arrived[distance] for distance in range(1, list_count)], near_rest)

    steps = chip_count // 2
    apart = list(range(1, chip_count))
    near_chips, far_chips = apart[: chip_count - 1 - steps], apart[chip_count - 1 - steps :]
    distances = (near_chips + near_chips[: steps - len(near_chips)], far_chips)
    received = [
        lax.ppermute(
            own_pair, "leaf", [(i, i ^ 2 * distances[i % 2][step]) for i in range(leaf_count)]
        )
        for step in range(steps)
    ]

    skeletons = {distance: arrived[distance] for distance in direct}
    forward = dict(zip(bases, copied))
    for distance in range(1, list_count):
        if distance not in direct:
            top = 1 << (distance.bit_length() - 1)
            forward[distance] = exchange(forward[distance ^ top], "list", top)
            skeletons[distance] = forward[distance]

    depth = leaf_count.bit_length() - 2
    down_high, down_low, above, basis = pl.pallas_call(
        functools.partial(tree_kernel, leaf_count),
        out_shape=[
            shape(leaf_count, rank, rank),
            shape(leaf_count, rank, rank),
            shape(leaves, rank, 3 * rank),
            like(leaf_basis),
        ],
        in_specs=[scalars] + [anywhere] * 6,
        out_specs=[whole] * 4,
        scratch_shapes=[
            pltpu.VMEM(tree_transfer.shape, f32),
            pltpu.VMEM((depth,) + level_coupling.shape[1:], f32),
            pltpu.VMEM((rank, rank), f32),
            pltpu.VMEM(leaf_transfer.shape, f32),
            pltpu.VMEM((2 * leaf_count, rank, rank), f32),
            pltpu.SemaphoreType.DMA((depth + 4,)),
        ],
        compiler_params=params(8),
        cost_estimate=pl.CostEstimate(
            flops=near_blocks.size * rows, bytes_accessed=near_blocks.size, transcendentals=0
        ),
        name="tree",
    )(
        position,
        stay(tree_transfer),
        stay(level_coupling),
        stay(device_transfer[0, 0]),
        stay(leaf_transfer),
        stay(leaf_basis),
        own_pair,
    )

    relayed = pl.pallas_call(
        functools.partial(relay_kernel, steps),
        out_shape=shape(steps, rows, 2 * rank, dtype=f32),
        in_specs=[whole] * steps + [anywhere],
        out_specs=whole,
        compiler_params=params(2),
        name="relay",
    )(*received, down_high)
    swapped = exchange(relayed, "leaf", 1)

    coupled = pl.pallas_call(
        functools.partial(far_kernel, list_count - 1),
        out_shape=shape(leaves // 2, rows, 2 * rank, dtype=f32),
        in_specs=[scalars] * 3 + [whole] * list_count,
        out_specs=whole,
        scratch_shapes=[pltpu.VMEM(((list_count - 1) * leaves + 1, rows, 2 * rank), bf16)],
        compiler_params=params(8),
        cost_estimate=pl.CostEstimate(
            flops=2 * far_coupling.size * rows * 4,
            bytes_accessed=4 * far_coupling.size,
            transcendentals=0,
        ),
        name="far",
    )(
        position,
        far_list,
        far_count,
        *[skeletons[distance] for distance in range(1, list_count)],
        far_coupling,
    )

    return pl.pallas_call(
        functools.partial(down_kernel, distances),
        out_shape=shape(leaves, rows, panels),
        in_specs=[scalars] + [whole] * (steps + 9),
        out_specs=anywhere,
        scratch_shapes=[
            pltpu.VMEM((leaves, rows, panels), bf16),
            pltpu.SemaphoreType.DMA((leaves // 4,)),
        ],
        compiler_params=params(4),
        name="down",
    )(
        position,
        own_pair,
        *received,
        swapped,
        down_high,
        down_low,
        above,
        basis,
        coupled,
        near_begin,
        near_rest,
    )


def solution(mesh):
    in_specs = (
        P(("leaf", "list"), None, None),
        P(("leaf", "list"), None, None),
        P(("leaf", "list"), None, None, None),
        P(("leaf", "list"), None),
        P(("leaf", "list"), None),
        P(("leaf", "list")),
        P(("leaf", "list"), None, None, None),
        P(("leaf", "list"), None, None),
        P("leaf", "list", None, None),
        P(),
        P(),
    )
    out_specs = P(("leaf", "list"), None, None)
    return jax.shard_map(
        on_device, mesh=mesh, in_specs=in_specs, out_specs=out_specs, check_vma=False
    )
```

time: 84.8 us -> 26.1 us (0.31); the launches traced: 83.7 us -> 26 us
  blocking collectives: 26.9 us -> 0 us
  matrix products: 26.5 us -> 0 us
  Pallas kernels: 0 us -> 14.9 us
  starting transfers between devices: 22.8 us -> 9.09 us
  local copies, waits for them, and re-layouts: 7.07 us -> 0.01 us
  waiting for transfers between devices: 0.02 us -> 1.79 us
    dot_general x19 -> x0, matrix products: 26.5 us -> none  [the longest x8 7.6 us: upper_exchange(): contribution = jnp.dot(source, matrices[slot_index].T, precision=highest)]
    psum x1 -> x0, blocking collectives: 17.8 us -> none  [on_device(): group_node = lax.psum(device_term, 'list')]
    pallas_call x0 -> x9, Pallas kernels: none -> 14.9 us  [the longest x1 4.77 us: on_device(): pl.pallas_call(functools.partial(near_rest_kernel, sizes), out_shape=shap...]
    ppermute x9 -> x8, starting transfers between devices: 22.8 us -> 9.09 us  [the longest x6 7.03 us: exchange(): return lax.ppermute(array, axis, pairs)]
    all_gather x1 -> x0, blocking collectives: 9.12 us -> none  [on_device(): piece = lax.all_gather(flattened, 'list', axis=0, tiled=True)]
    reshape x3 -> x0, local copies, waits for them, and re-layouts: 4.59 us -> none  [the longest x1 4.24 us: on_device(): selected.reshape(leaf_local, far_slots, skeleton.shape[1], skeleton.shape...]
    gather x1 -> x0, local copies, waits for them, and re-layouts: 2 us -> none  [on_device(): neighbours = jnp.take(panel_charges, near_list.reshape(-1), axis=0)]
    ppermute x9 -> x8, waiting for transfers between devices: 0.02 us -> 1.79 us  [the longest x6 1.79 us: exchange(): return lax.ppermute(array, axis, pairs)]
  transfers between devices with their start and end apart: 9 -> 8, of which waited for: 0 -> 2; matrix products, arithmetic and copies ran while one was open for 30% -> 0% of each run, Pallas kernels for 0% -> 39%
where the time goes in v2:
time: 26.1 us; the launch traced here: 26 us
  Pallas kernels  14.9 us (57%)
  starting transfers between devices  9.09 us (35%)
  waiting for transfers between devices  1.79 us (7%)
    ppermute x6, starting transfers between devices, exchange(): return lax.ppermute(array, axis, pairs)  7.03 us
    pallas_call x1, Pallas kernels, on_device(): pl.pallas_call(functools.partial(near_rest_kernel, sizes), out_shape=shap...  4.77 us
    pallas_call x1, Pallas kernels, on_device(): pl.pallas_call(functools.partial(tree_kernel, leaf_count), out_shape=[sha...  2.54 us
    pallas_call x1, Pallas kernels, on_device(): pl.pallas_call(functools.partial(down_kernel, distances), out_shape=shape...  2.38 us
    pallas_call x1, Pallas kernels, on_device(): pl.pallas_call(functools.partial(upward_kernel, count), out_shape=[shape(...  2.23 us
    ppermute x2, starting transfers between devices, on_device(): lax.ppermute(own_pair, 'leaf', [(i, i ^ 2 * distances[i % 2][step]) for i...  2.06 us
    pallas_call x1, Pallas kernels, on_device(): pl.pallas_call(functools.partial(far_kernel, list_count - 1), out_shape=s...  1.79 us
    ppermute x6, waiting for transfers between devices, exchange(): return lax.ppermute(array, axis, pairs)  1.79 us
  transfers between devices with their start and end apart: 8, of which 2 were waited for; matrix products, arithmetic and copies ran while one was open for 0% of the time, Pallas kernels for 39%

profile of v2, /device:TPU:0, one launch (start us, length us, event | category | flops | bytes accessed | tf_op | source)
XLA Modules:
  0.0 26.0 jit_solution(13167441931371034215)
XLA Ops:
  0.0 2.2 %upward.1 = (bf16[10,64,128]{2,1,0:T(8,128)(2,1)S(1)}, bf16[64,128]{1,0:T(8,128)(2,1)S(1)}, bf16[16,64,256]{2,1,0:T(8,128)(2,1)S(1)}, s32[4,16]{1,0:T(4,128)S(1)...) custom-call(bf16[16,64,256]{2,1,0:T(8,128)(2,1)} %refs_0_.1, ...), custom_call_target="tpu_custom_call" | custom-call | tf_op jit(solution)/shard_map/upward/pallas_call | solution.py:340
  2.2 0.5 %collective-permute-start = (bf16[64,128]{1,0:T(8,128)(2,1)S(1)}, bf16[64,128]{1,0:T(8,128)(2,1)S(1)}, u32[]{:S(2)}, u32[]{:S(2)}) collective-permute-start(bf16[64,128]{1,0:T(8,128)(2,1)S(1)} %get-tuple-element.20), channel_id=1, source_target_pairs={{0,4},{4,0},{8,12},{12,8},{16,20},{20,16},{24,28},{28,24},{1,5},{5... | collective-permute-start | bytes 49160 | tf_op jit(solution)/shard_map/ppermute | solution.py:333
  2.8 1.0 %near_begin.1.near.refs_9_ = f32[2,64,256]{2,1,0:T(8,128)S(1)} custom-call(s32[4,16]{1,0:T(4,128)S(1)} %get-tuple-element.21.near_list, bf16[16,64,256]{2,1,0:T(8,128)(2,1)S(1)} %get-tuple-element.22.charges, bf16[2,4,256,256]{3,2,1,0:T(8,128)(2,1)S(1)} %get-tuple-element.23.blocks), custom_call_target="tpu_custom_call" | custom-call | tf_op jit(solution)/shard_map/near_begin/pallas_call | solution.py:363
  3.8 0.0 collective-permute-done.term_parts
  3.8 2.8 %collective-permute-start.2 = (bf16[10,64,128]{2,1,0:T(8,128)(2,1)S(1)}, bf16[10,64,128]{2,1,0:T(8,128)(2,1)S(1)}, u32[]{:S(2)}, u32[]{:S(2)}) collective-permute-start(bf16[10,64,128]{2,1,0:T(8,128)(2,1)S(1)} %get-tuple-element.25.refs_0_), channel_id=1, source_target_pairs={{0,2},{1,3},{2,0},{3,1},{4,6},{5,7},{6,4},{7,5},{8,10},{9,11},{10,... | collective-permute-start | bytes 491528 | tf_op jit(solution)/shard_map/ppermute | solution.py:333
  6.5 1.5 %collective-permute-start.1 = (bf16[10,64,128]{2,1,0:T(8,128)(2,1)S(1)}, bf16[10,64,128]{2,1,0:T(8,128)(2,1)S(1)}, u32[]{:S(2)}, u32[]{:S(2)}) collective-permute-start(bf16[10,64,128]{2,1,0:T(8,128)(2,1)S(1)} %get-tuple-element.25.refs_0_), channel_id=1, source_target_pairs={{0,1},{1,0},{2,3},{3,2},{4,5},{5,4},{6,7},{7,6},{8,9},{9,8},{10,11... | collective-permute-start | bytes 491528 | tf_op jit(solution)/shard_map/ppermute | solution.py:333
  8.0 0.0 collective-permute-start.3
  8.1 4.8 %near_rest.1.refs_4_.refs_10_ = f32[14,64,256]{2,1,0:T(8,128)S(1)} custom-call(s32[4,16]{1,0:T(4,128)S(1)} %get-tuple-element.21.near_list, bf16[16,64,256]{2,1,0:T(8,128)(2,1)S(1)} %get-tuple-element.22.charges, bf16[16,4,256,256]{3,2,1,0:T(8,128)(2,1)} %blocks_in.1), custom_call_target="tpu_custom_call" | custom-call | flops 536870912 | bytes 8388608 | tf_op jit(solution)/shard_map/near_rest/pallas_call | solution.py:389
  12.9 0.0 copy-start
  12.9 0.3 %collective-permute-done.3.refs_3_ = bf16[2,64,128]{2,1,0:T(8,128)(2,1)S(1)} collective-permute-done((bf16[2,64,128]{2,1,0:T(8,128)(2,1)S(1)}, bf16[2,64,128]{2,1,0:T(8,128)(2,1)S(1)}, u32[]{:S(2)}, u32[]{:S(2)}) %collective-permute-start.3) | collective-permute-done | bytes 32800 | tf_op jit(solution)/shard_map/ppermute | solution.py:333
  13.2 0.0 collective-permute-done.2.refs_2_.refs_1_
  13.2 0.0 collective-permute-done.1.refs_1_.refs_0_
  13.2 0.2 group_sum.1
  13.4 1.8 %collective-permute-start.5 = (f32[64,128]{1,0:T(8,128)S(1)}, f32[64,128]{1,0:T(8,128)S(1)}, u32[]{:S(2)}, u32[]{:S(2)}) collective-permute-start(f32[64,128]{1,0:T(8,128)S(1)} %get-tuple-element.27.near.refs_0_), channel_id=1, source_target_pairs={{0,8},{4,28},{8,0},{12,20},{16,24},{20,12},{24,16},{28,4},{1,9},{5... | collective-permute-start | bytes 98312 | tf_op jit(solution)/shard_map/ppermute | solution.py:423
  15.1 0.3 %collective-permute-start.4 = (f32[64,128]{1,0:T(8,128)S(1)}, f32[64,128]{1,0:T(8,128)S(1)}, u32[]{:S(2)}, u32[]{:S(2)}) collective-permute-start(f32[64,128]{1,0:T(8,128)S(1)} %get-tuple-element.27.near.refs_0_), channel_id=1, source_target_pairs={{0,8},{4,20},{8,0},{12,28},{16,24},{20,4},{24,16},{28,12},{1,9},{5... | collective-permute-start | bytes 98312 | tf_op jit(solution)/shard_map/ppermute | solution.py:423
  15.4 1.7 %collective-permute-start.7 = (bf16[8,64,128]{2,1,0:T(8,128)(2,1)S(1)}, bf16[8,64,128]{2,1,0:T(8,128)(2,1)S(1)}, u32[]{:S(2)}, u32[]{:S(2)}) collective-permute-start(bf16[8,64,128]{2,1,0:T(8,128)(2,1)S(1)} %get-tuple-element.34), channel_id=1, source_target_pairs={{0,2},{1,3},{2,0},{3,1},{4,6},{5,7},{6,4},{7,5},{8,10},{9,11},{10,... | collective-permute-start | bytes 393224 | tf_op jit(solution)/shard_map/ppermute | solution.py:333
  17.1 0.1 pad_add_fusion.position
  17.2 2.5 %tree.1 = (bf16[8,64,64]{2,1,0:T(8,128)(2,1)S(1)}, bf16[8,64,64]{2,1,0:T(8,128)(2,1)S(1)}, bf16[16,64,192]{2,1,0:T(8,128)(2,1)S(1)}, bf16[16,64,256]{2,1,0:T(8,128)(2,1)S(1)}) custom-call(s32[2]{0:T(128)S(1)} %pad_add_fusion.position, f32[8,64,64]{2,1,0:T(8,128)} %tree_in.1, f32[12,4,64,64]{3,2,1,0:T(8,128)} %couplings_in.1, f32[64,64]{1,0:T(8,128)} %bitcast.7, ...), custom_call_target="tpu_custom_call" | custom-call | flops 268435456 | bytes 4194304 | tf_op jit(solution)/shard_map/tree/pallas_call | solution.py:438
  19.7 0.0 collective-permute-done.5.refs_1_.refs_2_
  19.8 0.6 %collective-permute-start.6 = (f32[2,64,128]{2,1,0:T(8,128)S(1)}, f32[2,64,128]{2,1,0:T(8,128)S(1)}, u32[]{:S(2)}, u32[]{:S(2)}) collective-permute-start(f32[2,64,128]{2,1,0:T(8,128)S(1)} %relay.1), channel_id=1, source_target_pairs={{0,4},{4,0},{8,12},{12,8},{16,20},{20,16},{24,28},{28,24},{1,5},{5... | collective-permute-start | bytes 196616 | tf_op jit(solution)/shard_map/ppermute | solution.py:333
  20.3 1.4 %collective-permute-done.7.refs_2_ = bf16[8,64,128]{2,1,0:T(8,128)(2,1)S(1)} collective-permute-done((bf16[8,64,128]{2,1,0:T(8,128)(2,1)S(1)}, bf16[8,64,128]{2,1,0:T(8,128)(2,1)S(1)}, u32[]{:S(2)}, u32[]{:S(2)}) %collective-permute-start.7) | collective-permute-done | bytes 131104 | tf_op jit(solution)/shard_map/ppermute | solution.py:333
  21.8 1.8 %far.1.refs_8_ = f32[8,64,128]{2,1,0:T(8,128)S(1)} custom-call(s32[2]{0:T(128)S(1)} %pad_add_fusion.position, s32[8,16]{1,0:T(8,128)S(1)} %get-tuple-element.32.far_list, s32[1,16]{1,0:T(1,128)S(1)} %get-tuple-element.33.far_count, bf16[10,64,128]{2,1,0:T(8,128)(2,1)S(1)} %collective-permute-done.1.refs_1_.refs_0_, ...), custom_call_target="tpu_custom_call" | custom-call | flops 268435456 | bytes 2097152 | tf_op jit(solution)/shard_map/far/pallas_call | solution.py:481
  23.6 0.0 collective-permute-done.6.refs_3_
  23.6 2.4 %down.1 = bf16[16,64,256]{2,1,0:T(8,128)(2,1)} custom-call(s32[2]{0:T(128)S(1)} %pad_add_fusion.position, f32[64,128]{1,0:T(8,128)S(1)} %get-tuple-element.27.near.refs_0_, f32[64,128]{1,0:T(8,128)S(1)} %collective-permute-done.4.refs_0_.refs_1_, f32[64,128]{1,0:T(8,128)S(1)} %collective-permute-done.5.refs_1_.refs_2_, ...), custom_call_target="tpu_custom_call" | custom-call | tf_op jit(solution)/shard_map/down/pallas_call | solution.py:502
  (4 shorter events, 0.0 us)
Async XLA Ops:
  2.2 1.5 %collective-permute-start = (bf16[64,128]{1,0:T(8,128)(2,1)S(1)}, bf16[64,128]{1,0:T(8,128)(2,1)S(1)}, u32[]{:S(2)}, u32[]{:S(2)}) collective-permute-start(bf16[64,128]{1,0:T(8,128)(2,1)S(1)} %get-tuple-element.20), channel_id=1, source_target_pairs={{0,4},{4,0},{8,12},{12,8},{16,20},{20,16},{24,28},{28,24},{1,5},{5... | collective-permute-start | bytes 49160 | tf_op jit(solution)/shard_map/ppermute | solution.py:333
  3.8 9.4 %collective-permute-start.2 = (bf16[10,64,128]{2,1,0:T(8,128)(2,1)S(1)}, bf16[10,64,128]{2,1,0:T(8,128)(2,1)S(1)}, u32[]{:S(2)}, u32[]{:S(2)}) collective-permute-start(bf16[10,64,128]{2,1,0:T(8,128)(2,1)S(1)} %get-tuple-element.25.refs_0_), channel_id=1, source_target_pairs={{0,2},{1,3},{2,0},{3,1},{4,6},{5,7},{6,4},{7,5},{8,10},{9,11},{10,... | collective-permute-start | bytes 491528 | tf_op jit(solution)/shard_map/ppermute | solution.py:333
  6.5 6.7 %collective-permute-start.1 = (bf16[10,64,128]{2,1,0:T(8,128)(2,1)S(1)}, bf16[10,64,128]{2,1,0:T(8,128)(2,1)S(1)}, u32[]{:S(2)}, u32[]{:S(2)}) collective-permute-start(bf16[10,64,128]{2,1,0:T(8,128)(2,1)S(1)} %get-tuple-element.25.refs_0_), channel_id=1, source_target_pairs={{0,1},{1,0},{2,3},{3,2},{4,5},{5,4},{6,7},{7,6},{8,9},{9,8},{10,11... | collective-permute-start | bytes 491528 | tf_op jit(solution)/shard_map/ppermute | solution.py:333
  8.0 5.2 %collective-permute-start.3 = (bf16[2,64,128]{2,1,0:T(8,128)(2,1)S(1)}, bf16[2,64,128]{2,1,0:T(8,128)(2,1)S(1)}, u32[]{:S(2)}, u32[]{:S(2)}) collective-permute-start(bf16[2,64,128]{2,1,0:T(8,128)(2,1)S(1)} %get-tuple-element.26), channel_id=1, source_target_pairs={{0,3},{1,2},{2,1},{3,0},{4,7},{5,6},{6,5},{7,4},{8,11},{9,10},{10,... | collective-permute-start | bytes 98312 | tf_op jit(solution)/shard_map/ppermute | solution.py:333
  12.9 8.9 %copy-start = (bf16[16,8,64,64]{3,2,1,0:T(8,128)(2,1)S(1)}, bf16[16,8,64,64]{3,2,1,0:T(8,128)(2,1)}, u32[]{:S(2)}) copy-start(bf16[16,8,64,64]{3,2,1,0:T(8,128)(2,1)} %refs_3_.1) | copy-start | bytes 3145732
  13.4 6.4 %collective-permute-start.5 = (f32[64,128]{1,0:T(8,128)S(1)}, f32[64,128]{1,0:T(8,128)S(1)}, u32[]{:S(2)}, u32[]{:S(2)}) collective-permute-start(f32[64,128]{1,0:T(8,128)S(1)} %get-tuple-element.27.near.refs_0_), channel_id=1, source_target_pairs={{0,8},{4,28},{8,0},{12,20},{16,24},{20,12},{24,16},{28,4},{1,9},{5... | collective-permute-start | bytes 98312 | tf_op jit(solution)/shard_map/ppermute | solution.py:423
  15.1 4.6 %collective-permute-start.4 = (f32[64,128]{1,0:T(8,128)S(1)}, f32[64,128]{1,0:T(8,128)S(1)}, u32[]{:S(2)}, u32[]{:S(2)}) collective-permute-start(f32[64,128]{1,0:T(8,128)S(1)} %get-tuple-element.27.near.refs_0_), channel_id=1, source_target_pairs={{0,8},{4,20},{8,0},{12,28},{16,24},{20,4},{24,16},{28,12},{1,9},{5... | collective-permute-start | bytes 98312 | tf_op jit(solution)/shard_map/ppermute | solution.py:423
  15.4 6.3 %collective-permute-start.7 = (bf16[8,64,128]{2,1,0:T(8,128)(2,1)S(1)}, bf16[8,64,128]{2,1,0:T(8,128)(2,1)S(1)}, u32[]{:S(2)}, u32[]{:S(2)}) collective-permute-start(bf16[8,64,128]{2,1,0:T(8,128)(2,1)S(1)} %get-tuple-element.34), channel_id=1, source_target_pairs={{0,2},{1,3},{2,0},{3,1},{4,6},{5,7},{6,4},{7,5},{8,10},{9,11},{10,... | collective-permute-start | bytes 393224 | tf_op jit(solution)/shard_map/ppermute | solution.py:333
  19.8 3.8 %collective-permute-start.6 = (f32[2,64,128]{2,1,0:T(8,128)S(1)}, f32[2,64,128]{2,1,0:T(8,128)S(1)}, u32[]{:S(2)}, u32[]{:S(2)}) collective-permute-start(f32[2,64,128]{2,1,0:T(8,128)S(1)} %relay.1), channel_id=1, source_target_pairs={{0,4},{4,0},{8,12},{12,8},{16,20},{20,16},{24,28},{28,24},{1,5},{5... | collective-permute-start | bytes 196616 | tf_op jit(solution)/shard_map/ppermute | solution.py:333

commit v3 on v2

v3 whole, which is shorter than its diff:
```python
import functools

import jax
import jax.numpy as jnp
from jax import lax
from jax.experimental import pallas as pl
from jax.experimental.pallas import tpu as pltpu
from jax.sharding import PartitionSpec as P

offsets = (-3, -2, 2, 3)
f32 = jnp.float32
bf16 = jnp.bfloat16
whole = pl.BlockSpec(memory_space=pltpu.VMEM)
anywhere = pl.BlockSpec(memory_space=pl.ANY)


def params(mebibytes):
    return pltpu.CompilerParams(vmem_limit_bytes=mebibytes << 20)


def times(left, right):
    return lax.dot_general(left, right, (((1,), (0,)), ((), ())), preferred_element_type=f32)


def times_transposed(left, right):
    return lax.dot_general(left, right, (((1,), (1,)), ((), ())), preferred_element_type=f32)


def split(array):
    high = array.astype(bf16)
    return high, (array - high.astype(f32)).astype(bf16)


def exact(product, left, right):
    left_high, left_low = split(left)
    right_high, right_low = split(right)
    return product(left_high, right_high) + (
        product(left_low, right_high) + product(left_high, right_low)
    )


def upward_kernel(count, *refs):
    sources = refs[:count]
    payload, terms = refs[count : count + 2]
    kept = refs[count + 2 : count + 6]
    basis, transfer, matrix, sem = refs[count + 6 :]
    charges = kept[0]
    targets = (charges, basis, transfer, matrix) + kept[1:]
    copies = [
        pltpu.make_async_copy(source, target, sem.at[i])
        for i, (source, target) in enumerate(zip(sources, targets))
    ]
    for copy in copies:
        copy.start()
    for copy in copies:
        copy.wait()
    pair_count = charges.shape[0] // 2
    rank = basis.shape[1]
    node = jnp.zeros((charges.shape[1], rank), f32)
    for pair in range(pair_count):
        halves = [
            times_transposed(charges[leaf], basis[leaf]).astype(bf16)
            for leaf in (2 * pair, 2 * pair + 1)
        ]
        skeleton = jnp.concatenate(halves, axis=1)
        payload[pair] = skeleton
        block = transfer[pl.ds(2 * pair, 2)].reshape(2 * rank, rank)
        high, low = split(block)
        node = node + (times(skeleton, high) + times(skeleton, low))
    term = exact(times, node, matrix[...])
    both = jnp.concatenate(split(term), axis=1)
    terms[0] = both
    payload[pair_count] = both


def near_leaf(near_list, charges, blocks, row, leaf):
    total = None
    for slot in range(blocks.shape[1]):
        part = times_transposed(charges[near_list[slot, leaf]], blocks[row, slot])
        total = part if total is None else total + part
    return total


def near_kernel(first, list_in, charges, blocks, after, near, near_list, sem):
    listed = pltpu.make_async_copy(list_in, near_list, sem)
    listed.start()
    listed.wait()
    for row in range(near.shape[0]):
        near[row] = near_leaf(near_list, charges, blocks, first + row, first + row)


def pair_kernel(own, other, after, pair):
    pair[...] = jnp.concatenate([own[...], other[...]], axis=1)


def forward_kernel(payload, near, terms, copy):
    copy[...] = payload[pl.ds(0, copy.shape[0])]


def sum_kernel(count, *refs):
    arrays, node = refs[:count], refs[-1]
    rank = node.shape[1]
    total = None
    for array in arrays:
        both = array[array.shape[0] - 1].astype(f32)
        part = both[:, :rank] + both[:, rank:]
        total = part if total is None else total + part
    node[...] = total


def tree_kernel(
    leaf_count, tree, couplings, matrix, own_node, down_high, down_low, down
):
    rank = matrix.shape[0]
    depth = leaf_count.bit_length() - 2
    place = lax.axis_index("leaf")
    begins = [2 * leaf_count - 2 * (leaf_count >> height) for height in range(depth)]
    down[...] = jnp.zeros_like(down)
    back = matrix[...]
    for height in range(depth):
        members = leaf_count >> height
        spot = place >> height
        for slot, offset in enumerate(offsets):
            source = spot + offset
            usable = jnp.logical_and(source >= 0, source < members)
            if abs(offset) == 3:
                usable = jnp.logical_and(usable, spot % 2 == (0 if offset > 0 else 1))
            entry = begins[height] + jnp.clip(source, 0, members - 1)
            part = exact(times, back, couplings[begins[height] + spot, slot])
            down[entry] += jnp.where(usable, part, jnp.zeros_like(part))
        if height < depth - 1:
            back = exact(times, back, tree[begins[height] + spot])
    for height in reversed(range(depth - 1)):
        for parent in range(leaf_count >> (height + 1)):
            for child in (2 * parent, 2 * parent + 1):
                down[begins[height] + child] += exact(
                    times_transposed, down[begins[height + 1] + parent], tree[begins[height] + child]
                )
    for node in range(leaf_count):
        high, low = split(down[node])
        down_high[node] = high
        down_low[node] = low


def weights_kernel(transfer, basis, after, weights):
    for leaf in range(transfer.shape[0]):
        high, low = split(transfer[leaf])
        full = times(high.T, basis[leaf]) + times(low.T, basis[leaf])
        full_high, full_low = split(full)
        weights[leaf] = jnp.concatenate([full_high, full_high, full_low], axis=0)


def base_kernel(coupled, basis, near, base):
    rank = basis.shape[1]
    for pair in range(coupled.shape[0]):
        both = coupled[pair].astype(bf16)
        for half in range(2):
            leaf = 2 * pair + half
            far = times(both[:, half * rank : (half + 1) * rank], basis[leaf])
            base[leaf] = far + near[leaf]


def relay_kernel(count, *refs):
    out = refs[-1]
    for i in range(count):
        out[i] = refs[i][...]


def far_kernel(peer_count, list_in, count_in, *refs):
    peers = refs[:peer_count]
    coupling, after, coupled, table, far_list, far_count, sem = refs[peer_count:]
    copies = [
        pltpu.make_async_copy(list_in, far_list, sem.at[0]),
        pltpu.make_async_copy(count_in, far_count, sem.at[1]),
    ]
    for copy in copies:
        copy.start()
    leaves, slots, rank = coupling.shape[0], coupling.shape[1], coupling.shape[2]
    rows = table.shape[1]
    pair_count = leaves // 2
    empty = peer_count * leaves
    table[empty] = jnp.zeros(table.shape[1:], bf16)
    for peer in range(peer_count):
        for pair in range(pair_count):
            block = peers[peer][pair]
            first, second = block[:, :rank], block[:, rank:]
            table[peer * leaves + 2 * pair] = jnp.concatenate([first, first], axis=1)
            table[peer * leaves + 2 * pair + 1] = jnp.concatenate([second, second], axis=1)
    for copy in copies:
        copy.wait()
    own = lax.axis_index("list")
    lower = lax.broadcasted_iota(jnp.int32, (rows, 2 * rank), 1) < rank

    def entry(leaf, slot):
        source = far_list[slot, leaf]
        device = source // leaves
        place = ((device ^ own) - 1) * leaves + (source - device * leaves)
        return jnp.where(slot < far_count[0, leaf], place, empty)

    def one(leaf):
        lefts, rights = [], []
        for slot in range(0, slots, 2):
            lefts.append(
                jnp.where(lower, table[entry(leaf, slot)], table[entry(leaf, slot + 1)])
            )
            rights.append(
                jnp.concatenate([coupling[leaf, slot], coupling[leaf, slot + 1]], axis=1)
            )
        return times_transposed(
            jnp.concatenate(lefts, axis=1), jnp.concatenate(rights, axis=1)
        )

    for pair in range(pair_count):
        coupled[pair] = jnp.concatenate([one(2 * pair), one(2 * pair + 1)], axis=1)


def down_kernel(distances, *refs):
    steps = len(distances[0])
    own_pair, received, swapped = refs[0], refs[1 : 1 + steps], refs[1 + steps]
    down_high, down_low, weights, base, out, buffer, sem = refs[2 + steps :]
    place = lax.axis_index("leaf")
    chip, core = place // 2, place % 2

    def product(both, chip_at, flipped):
        first = 2 * chip_at + (core ^ flipped)
        second = 2 * chip_at + (1 - (core ^ flipped))
        high = jnp.concatenate([down_high[first], down_high[second]], axis=1)
        low = jnp.concatenate([down_low[first], down_low[second]], axis=1)
        both_high, both_low = split(both)
        return times_transposed(
            jnp.concatenate([both_high, both_low, both_high], axis=1),
            jnp.concatenate([high, high, low], axis=1),
        )

    total = product(own_pair[...], chip, 0)
    for step in range(steps):
        for flipped in range(2):
            both = swapped[step] if flipped else received[step][...]
            apart = [distances[core_at ^ flipped] for core_at in range(2)]
            fresh = [apart[core_at].index(apart[core_at][step]) == step for core_at in range(2)]
            if not all(fresh):
                usable = core == fresh.index(True)
                both = jnp.where(usable, both, jnp.zeros_like(both))
            at = chip ^ jnp.where(core == 0, apart[0][step], apart[1][step])
            total = total + product(both, at, flipped)
    high, low = split(total)
    wide = jnp.concatenate([high, low, high], axis=1)
    copies = []
    group = 4
    for begin in range(0, base.shape[0], group):
        for leaf in range(begin, begin + group):
            buffer[leaf] = (base[leaf] + times(wide, weights[leaf])).astype(bf16)
        rows = pl.ds(begin, group)
        copy = pltpu.make_async_copy(buffer.at[rows], out.at[rows], sem.at[begin // group])
        copy.start()
        copies.append(copy)
    for copy in copies:
        copy.wait()


def on_device(
    panel_charges,
    leaf_basis,
    near_blocks,
    near_list,
    far_list,
    far_count,
    far_coupling,
    leaf_transfer,
    device_transfer,
    tree_transfer,
    level_coupling,
):
    leaves, rows, panels = panel_charges.shape
    rank = leaf_basis.shape[1]
    list_count, leaf_count = lax.axis_size("list"), lax.axis_size("leaf")
    chip_count = leaf_count // 2

    def like(array, dtype=None):
        return jax.ShapeDtypeStruct(array.shape, dtype or array.dtype)

    def shape(*dims, dtype=bf16):
        return jax.ShapeDtypeStruct(dims, dtype)

    def stay(array):
        return pltpu.with_memory_space_constraint(array, pltpu.HBM)

    def exchange(array, axis, distance):
        pairs = [(i, i ^ distance) for i in range(lax.axis_size(axis))]
        return lax.ppermute(array, axis, pairs)

    inputs = [stay(panel_charges), stay(leaf_basis), stay(leaf_transfer)]
    inputs += [stay(device_transfer[0, 0]), near_list.T, far_list.T, far_count[None]]
    count = len(inputs)
    payload, terms, charges, near_list, far_list, far_count = pl.pallas_call(
        functools.partial(upward_kernel, count),
        out_shape=[
            shape(leaves // 2 + 1, rows, 2 * rank),
            shape(1, rows, 2 * rank),
            like(panel_charges),
            *[like(array) for array in inputs[4:]],
        ],
        in_specs=[anywhere] * count,
        out_specs=[whole] * 6,
        scratch_shapes=[
            pltpu.VMEM(leaf_basis.shape, bf16),
            pltpu.VMEM(leaf_transfer.shape, f32),
            pltpu.VMEM((rank, rank), f32),
            pltpu.SemaphoreType.DMA((count,)),
        ],
        compiler_params=params(4),
        cost_estimate=pl.CostEstimate(
            flops=64 * near_blocks.size * rows,
            bytes_accessed=64 * near_blocks.size,
            transcendentals=0,
        ),
        name="upward",
    )(*inputs[:4], *[stay(array) for array in inputs[4:]])

    direct = [distance for distance in range(1, list_count) if distance & (distance - 1) == 0]
    arrived = {
        distance: exchange(payload if distance in direct else terms, "list", distance)
        for distance in range(1, list_count)
    }

    def near_part(first, count, after):
        return pl.pallas_call(
            functools.partial(near_kernel, first),
            out_shape=shape(count, rows, panels, dtype=f32),
            in_specs=[anywhere, whole, whole, anywhere],
            out_specs=whole,
            scratch_shapes=[pltpu.SMEM(near_list.shape, jnp.int32), pltpu.SemaphoreType.DMA],
            compiler_params=params(4),
            cost_estimate=pl.CostEstimate(
                flops=2 * near_blocks.size * rows,
                bytes_accessed=2 * near_blocks.size,
                transcendentals=0,
            ),
            name="near",
        )(near_list, charges, near_blocks, after)

    near = near_part(0, leaves, terms)

    bases = direct[:-1]
    forward = {}
    for base in bases:
        forward[base] = pl.pallas_call(
            forward_kernel,
            out_shape=shape(leaves // 2, rows, 2 * rank),
            in_specs=[whole, anywhere, anywhere],
            out_specs=whole,
            compiler_params=params(2),
            name="forward",
        )(arrived[base], near, arrived[list_count - 1])

    own_node = pl.pallas_call(
        functools.partial(sum_kernel, list_count),
        out_shape=shape(rows, rank, dtype=f32),
        in_specs=[whole] * list_count + [anywhere],
        out_specs=whole,
        compiler_params=params(4),
        name="group_sum",
    )(payload, *[arrived[distance] for distance in range(1, list_count)], near)
    other_node = exchange(own_node, "leaf", 1)

    down_high, down_low = pl.pallas_call(
        functools.partial(tree_kernel, leaf_count),
        out_shape=[
            shape(leaf_count, rank, rank),
            shape(leaf_count, rank, rank),
        ],
        in_specs=[whole] * 3 + [anywhere],
        out_specs=[whole] * 2,
        scratch_shapes=[pltpu.VMEM((2 * leaf_count, rank, rank), f32)],
        compiler_params=params(4),
        name="tree",
    )(tree_transfer, level_coupling, device_transfer[0, 0], own_node)

    own_pair = pl.pallas_call(
        pair_kernel,
        out_shape=shape(rows, 2 * rank, dtype=f32),
        in_specs=[whole] * 2 + [anywhere],
        out_specs=whole,
        compiler_params=params(2),
        name="pair",
    )(own_node, other_node, down_high)

    steps = chip_count // 2
    apart = list(range(1, chip_count))
    near_chips, far_chips = apart[: chip_count - 1 - steps], apart[chip_count - 1 - steps :]
    distances = (near_chips + near_chips[: steps - len(near_chips)], far_chips)
    received = [
        lax.ppermute(
            own_pair, "leaf", [(i, i ^ 2 * distances[i % 2][step]) for i in range(leaf_count)]
        )
        for step in range(steps)
    ]

    skeletons = {distance: arrived[distance] for distance in direct}
    for distance in range(1, list_count):
        if distance not in direct:
            top = 1 << (distance.bit_length() - 1)
            forward[distance] = exchange(forward[distance ^ top], "list", top)
            skeletons[distance] = forward[distance]

    coupled = pl.pallas_call(
        functools.partial(far_kernel, list_count - 1),
        out_shape=shape(leaves // 2, rows, 2 * rank, dtype=f32),
        in_specs=[anywhere] * 2 + [whole] * list_count + [anywhere],
        out_specs=whole,
        scratch_shapes=[
            pltpu.VMEM(((list_count - 1) * leaves + 1, rows, 2 * rank), bf16),
            pltpu.SMEM(far_list.shape, jnp.int32),
            pltpu.SMEM(far_count.shape, jnp.int32),
            pltpu.SemaphoreType.DMA((2,)),
        ],
        compiler_params=params(8),
        cost_estimate=pl.CostEstimate(
            flops=2 * far_coupling.size * rows * 4,
            bytes_accessed=4 * far_coupling.size,
            transcendentals=0,
        ),
        name="far",
    )(
        far_list,
        far_count,
        *[skeletons[distance] for distance in range(1, list_count)],
        far_coupling,
        own_pair,
    )

    weights = pl.pallas_call(
        weights_kernel,
        out_shape=shape(leaves, 3 * rank, panels),
        in_specs=[whole] * 2 + [anywhere],
        out_specs=whole,
        compiler_params=params(4),
        name="weights",
    )(leaf_transfer, leaf_basis, own_pair)

    relayed = pl.pallas_call(
        functools.partial(relay_kernel, steps),
        out_shape=shape(steps, rows, 2 * rank, dtype=f32),
        in_specs=[whole] * steps + [anywhere] * 2,
        out_specs=whole,
        compiler_params=params(2),
        name="relay",
    )(*received, coupled, weights)
    swapped = exchange(relayed, "leaf", 1)

    base = pl.pallas_call(
        base_kernel,
        out_shape=shape(leaves, rows, panels, dtype=f32),
        in_specs=[whole] * 3,
        out_specs=whole,
        compiler_params=params(4),
        name="base",
    )(coupled, leaf_basis, near)

    return pl.pallas_call(
        functools.partial(down_kernel, distances),
        out_shape=shape(leaves, rows, panels),
        in_specs=[whole] * (steps + 6),
        out_specs=anywhere,
        scratch_shapes=[
            pltpu.VMEM((leaves, rows, panels), bf16),
            pltpu.SemaphoreType.DMA((leaves // 4,)),
        ],
        compiler_params=params(4),
        name="down",
    )(
        own_pair,
        *received,
        swapped,
        down_high,
        down_low,
        weights,
        base,
    )


def solution(mesh):
    in_specs = (
        P(("leaf", "list"), None, None),
        P(("leaf", "list"), None, None),
        P(("leaf", "list"), None, None, None),
        P(("leaf", "list"), None),
        P(("leaf", "list"), None),
        P(("leaf", "list")),
        P(("leaf", "list"), None, None, None),
        P(("leaf", "list"), None, None),
        P("leaf", "list", None, None),
        P(),
        P(),
    )
    out_specs = P(("leaf", "list"), None, None)
    return jax.shard_map(
        on_device, mesh=mesh, in_specs=in_specs, out_specs=out_specs, check_vma=False
    )
```

time: 26.1 us -> 23.4 us (0.90)
  Pallas kernels: 14.9 us -> 10.5 us
  waiting for transfers between devices: 1.79 us -> 3.56 us
    pallas_call x1, Pallas kernels: 2.54 us -> 0.76 us  [on_device(): pl.pallas_call(functools.partial(tree_kernel, leaf_count), out_shape=[sha...]
    pallas_call x4 -> x6, Pallas kernels: 5.94 us -> 4.18 us  [the longest x1 3.21 us: near_part(): pl.pallas_call(functools.partial(near_kernel, first), out_shape=shape(cou...]
    pallas_call x1, Pallas kernels: 2.38 us -> 1.46 us  [on_device(): pl.pallas_call(functools.partial(down_kernel, distances), out_shape=shape...]
    ppermute x6, waiting for transfers between devices: 1.79 us -> 2.68 us  [exchange(): return lax.ppermute(array, axis, pairs)]
    ppermute x2, waiting for transfers between devices: 0.01 us -> 0.88 us  [on_device(): lax.ppermute(own_pair, 'leaf', [(i, i ^ 2 * distances[i % 2][step]) for i...]
  transfers between devices with their start and end apart: 8 -> 8, of which waited for: 2 -> 5; matrix products, arithmetic and copies ran while one was open for 0% -> 0% of each run, Pallas kernels for 39% -> 29%
where the time goes in v3:
time: 23.4 us; the launch traced here: 23.3 us
  Pallas kernels  10.5 us (45%)
  starting transfers between devices  9.01 us (39%)
  waiting for transfers between devices  3.56 us (15%)
    ppermute x6, starting transfers between devices, exchange(): return lax.ppermute(array, axis, pairs)  6.98 us
    pallas_call x1, Pallas kernels, near_part(): pl.pallas_call(functools.partial(near_kernel, first), out_shape=shape(cou...  3.21 us
    ppermute x6, waiting for transfers between devices, exchange(): return lax.ppermute(array, axis, pairs)  2.68 us
    pallas_call x1, Pallas kernels, on_device(): pl.pallas_call(functools.partial(upward_kernel, count), out_shape=[shape(...  2.38 us
    ppermute x2, starting transfers between devices, on_device(): lax.ppermute(own_pair, 'leaf', [(i, i ^ 2 * distances[i % 2][step]) for i...  2.03 us
    pallas_call x1, Pallas kernels, on_device(): pl.pallas_call(functools.partial(far_kernel, list_count - 1), out_shape=s...  1.72 us
    pallas_call x1, Pallas kernels, on_device(): pl.pallas_call(functools.partial(down_kernel, distances), out_shape=shape...  1.46 us
    ppermute x2, waiting for transfers between devices, on_device(): lax.ppermute(own_pair, 'leaf', [(i, i ^ 2 * distances[i % 2][step]) for i...  0.88 us
  transfers between devices with their start and end apart: 8, of which 5 were waited for; matrix products, arithmetic and copies ran while one was open for 0% of the time, Pallas kernels for 29%

profile of v3, /device:TPU:0, one launch (start us, length us, event | category | flops | bytes accessed | tf_op | source)
XLA Modules:
  0.0 23.3 jit_solution(13897122440041482599)
XLA Ops:
  0.0 2.4 %upward.1 = (bf16[9,64,128]{2,1,0:T(8,128)(2,1)S(1)}, bf16[1,64,128]{2,1,0:T(8,128)(2,1)S(1)}, bf16[16,64,256]{2,1,0:T(8,128)(2,1)S(1)}, s32[4,16]{1,0:T(4,128)S...) custom-call(bf16[16,64,256]{2,1,0:T(8,128)(2,1)} %refs_0_.1, bf16[16,64,256]{2,1,0:T(8,128)(2,1)} %basis.3, ...), custom_call_target="tpu_custom_call" | custom-call | flops 17179869184 | bytes 268435456 | tf_op jit(solution)/shard_map/upward/pallas_call | solution.py:295
  2.4 3.0 %collective-permute-start = (bf16[9,64,128]{2,1,0:T(8,128)(2,1)S(1)}, bf16[9,64,128]{2,1,0:T(8,128)(2,1)S(1)}, u32[]{:S(2)}, u32[]{:S(2)}) collective-permute-start(bf16[9,64,128]{2,1,0:T(8,128)(2,1)S(1)} %get-tuple-element.13.refs_0_), channel_id=1, source_target_pairs={{0,1},{1,0},{2,3},{3,2},{4,5},{5,4},{6,7},{7,6},{8,9},{9,8},{10,11... | collective-permute-start | bytes 442376 | tf_op jit(solution)/shard_map/ppermute | solution.py:290
  5.4 1.5 %collective-permute-start.1 = (bf16[9,64,128]{2,1,0:T(8,128)(2,1)S(1)}, bf16[9,64,128]{2,1,0:T(8,128)(2,1)S(1)}, u32[]{:S(2)}, u32[]{:S(2)}) collective-permute-start(bf16[9,64,128]{2,1,0:T(8,128)(2,1)S(1)} %get-tuple-element.13.refs_0_), channel_id=1, source_target_pairs={{0,2},{1,3},{2,0},{3,1},{4,6},{5,7},{6,4},{7,5},{8,10},{9,11},{10,... | collective-permute-start | bytes 442376 | tf_op jit(solution)/shard_map/ppermute | solution.py:290
  6.9 0.0 collective-permute-start.2
  6.9 3.2 %near.1.refs_4_ = f32[16,64,256]{2,1,0:T(8,128)S(1)} custom-call(s32[4,16]{1,0:T(4,128)S(1)} %get-tuple-element.15.list_in, bf16[16,64,256]{2,1,0:T(8,128)(2,1)S(1)} %get-tuple-element.16.charges, bf16[16,4,256,256]{3,2,1,0:T(8,128)(2,1)S(1)} %bitcast.5, bf16[1,64,128]{2,1,0:T(8,128)(2,1)S(1)} %get-tuple-element.14.after), custom_call_target="tpu_custom_call" | custom-call | flops 536870912 | bytes 8388608 | tf_op jit(solution)/shard_map/near/pallas_call | solution.py:327
  10.2 0.0 copy-start.2
  10.2 1.4 %collective-permute-done.2.refs_3_.terms = bf16[1,64,128]{2,1,0:T(8,128)(2,1)S(1)} collective-permute-done((bf16[1,64,128]{2,1,0:T(8,128)(2,1)S(1)}, bf16[1,64,128]{2,1,0:T(8,128)(2,1)S(1)}, u32[]{:S(2)}, u32[]{:S(2)}) %collective-permute-start.2) | collective-permute-done | bytes 16416 | tf_op jit(solution)/shard_map/ppermute | solution.py:290
  11.6 0.0 copy-start.3
  11.6 0.7 %collective-permute-start.6 = (bf16[8,64,128]{2,1,0:T(8,128)(2,1)S(1)}, bf16[8,64,128]{2,1,0:T(8,128)(2,1)S(1)}, u32[]{:S(2)}, u32[]{:S(2)}) collective-permute-start(bf16[8,64,128]{2,1,0:T(8,128)(2,1)S(1)} %forward.1), channel_id=1, source_target_pairs={{0,2},{1,3},{2,0},{3,1},{4,6},{5,7},{6,4},{7,5},{8,10},{9,11},{10,... | collective-permute-start | bytes 393224 | tf_op jit(solution)/shard_map/ppermute | solution.py:290
  12.3 0.1 group_sum.1.own_node.own
  12.4 0.1 collective-permute-start.3
  12.5 0.8 %tree.2 = (bf16[8,64,64]{2,1,0:T(8,128)(2,1)S(1)}, bf16[8,64,64]{2,1,0:T(8,128)(2,1)S(1)}) custom-call(f32[8,64,64]{2,1,0:T(8,128)S(1)} %copy-done.4, f32[12,4,64,64]{3,2,1,0:T(8,128)S(1)} %copy-done.2, f32[64,64]{1,0:T(8,128)S(1)} %bitcast.7, f32[64,64]{1,0:T(8,128)S(1)} %group_sum.1.own_node.own), custom_call_target="tpu_custom_call" | custom-call | tf_op jit(solution)/shard_map/tree/pallas_call | solution.py:366
  13.3 0.4 %collective-permute-done.3.other = f32[64,64]{1,0:T(8,128)S(1)} collective-permute-done((f32[64,64]{1,0:T(8,128)S(1)}, f32[64,64]{1,0:T(8,128)S(1)}, u32[]{:S(2)}, u32[]{:S(2)}) %collective-permute-start.3) | collective-permute-done | bytes 16416 | tf_op jit(solution)/shard_map/ppermute | solution.py:290
  13.7 0.1 pair.1.refs_4_.after.refs_0_
  13.8 1.6 %collective-permute-start.5 = (f32[64,128]{1,0:T(8,128)S(1)}, f32[64,128]{1,0:T(8,128)S(1)}, u32[]{:S(2)}, u32[]{:S(2)}) collective-permute-start(f32[64,128]{1,0:T(8,128)S(1)} %pair.1.refs_4_.after.refs_0_), channel_id=1, source_target_pairs={{0,8},{4,28},{8,0},{12,20},{16,24},{20,12},{24,16},{28,4},{1,9},{5... | collective-permute-start | bytes 98312 | tf_op jit(solution)/shard_map/ppermute | solution.py:393
  15.3 0.4 %collective-permute-start.4 = (f32[64,128]{1,0:T(8,128)S(1)}, f32[64,128]{1,0:T(8,128)S(1)}, u32[]{:S(2)}, u32[]{:S(2)}) collective-permute-start(f32[64,128]{1,0:T(8,128)S(1)} %pair.1.refs_4_.after.refs_0_), channel_id=1, source_target_pairs={{0,8},{4,20},{8,0},{12,28},{16,24},{20,4},{24,16},{28,12},{1,9},{5... | collective-permute-start | bytes 98312 | tf_op jit(solution)/shard_map/ppermute | solution.py:393
  15.8 0.5 %weights.1.refs_3_.refs_6_ = bf16[16,192,256]{2,1,0:T(8,128)(2,1)S(1)} custom-call(f32[16,64,64]{2,1,0:T(8,128)S(1)} %copy-done.3, bf16[16,64,256]{2,1,0:T(8,128)(2,1)S(1)} %copy-done.1, f32[64,128]{1,0:T(8,128)S(1)} %pair.1.refs_4_.after.refs_0_), custom_call_target="tpu_custom_call" | custom-call | tf_op jit(solution)/shard_map/weights/pallas_call | solution.py:432
  16.3 0.3 %collective-permute-done.6.refs_2_ = bf16[8,64,128]{2,1,0:T(8,128)(2,1)S(1)} collective-permute-done((bf16[8,64,128]{2,1,0:T(8,128)(2,1)S(1)}, bf16[8,64,128]{2,1,0:T(8,128)(2,1)S(1)}, u32[]{:S(2)}, u32[]{:S(2)}) %collective-permute-start.6) | collective-permute-done | bytes 131104 | tf_op jit(solution)/shard_map/ppermute | solution.py:290
  16.6 1.7 %far.1.refs_2_.coupled = f32[8,64,128]{2,1,0:T(8,128)S(1)} custom-call(s32[8,16]{1,0:T(8,128)S(1)} %get-tuple-element.18.list_in, s32[1,16]{1,0:T(1,128)S(1)} %get-tuple-element.19.count_in, bf16[9,64,128]{2,1,0:T(8,128)(2,1)S(1)} %collective-permute-done.refs_1_.payload.refs_0_, bf16[9,64,128]{2,1,0:T(8,128)(2,1)S(1)} %collective-permute-done.1.refs_2_.refs_1_, ...), custom_call_target="tpu_custom_call" | custom-call | flops 268435456 | bytes 2097152 | tf_op jit(solution)/shard_map/far/pallas_call | solution.py:406
  18.4 0.9 %collective-permute-done.4.refs_0_.refs_1_ = f32[64,128]{1,0:T(8,128)S(1)} collective-permute-done((f32[64,128]{1,0:T(8,128)S(1)}, f32[64,128]{1,0:T(8,128)S(1)}, u32[]{:S(2)}, u32[]{:S(2)}) %collective-permute-start.4) | collective-permute-done | bytes 32800 | tf_op jit(solution)/shard_map/ppermute | solution.py:393
  19.3 1.7 %collective-permute-start.7 = (f32[2,64,128]{2,1,0:T(8,128)S(1)}, f32[2,64,128]{2,1,0:T(8,128)S(1)}, u32[]{:S(2)}, u32[]{:S(2)}) collective-permute-start(f32[2,64,128]{2,1,0:T(8,128)S(1)} %relay.1), channel_id=1, source_target_pairs={{0,4},{4,0},{8,12},{12,8},{16,20},{20,16},{24,28},{28,24},{1,5},{5... | collective-permute-start | bytes 196616 | tf_op jit(solution)/shard_map/ppermute | solution.py:290
  20.9 0.3 %base.1.refs_7_ = f32[16,64,256]{2,1,0:T(8,128)S(1)} custom-call(f32[8,64,128]{2,1,0:T(8,128)S(1)} %far.1.refs_2_.coupled, bf16[16,64,256]{2,1,0:T(8,128)(2,1)S(1)} %copy-done.1, f32[16,64,256]{2,1,0:T(8,128)S(1)} %near.1.refs_4_), custom_call_target="tpu_custom_call" | custom-call | tf_op jit(solution)/shard_map/base/pallas_call | solution.py:451
  21.3 0.6 %collective-permute-done.7.refs_3_ = f32[2,64,128]{2,1,0:T(8,128)S(1)} collective-permute-done((f32[2,64,128]{2,1,0:T(8,128)S(1)}, f32[2,64,128]{2,1,0:T(8,128)S(1)}, u32[]{:S(2)}, u32[]{:S(2)}) %collective-permute-start.7) | collective-permute-done | bytes 65568 | tf_op jit(solution)/shard_map/ppermute | solution.py:290
  21.8 1.5 %down.1 = bf16[16,64,256]{2,1,0:T(8,128)(2,1)} custom-call(f32[64,128]{1,0:T(8,128)S(1)} %pair.1.refs_4_.after.refs_0_, f32[64,128]{1,0:T(8,128)S(1)} %collective-permute-done.4.refs_0_.refs_1_, f32[64,128]{1,0:T(8,128)S(1)} %collective-permute-done.5.refs_1_.refs_2_, f32[2,64,128]{2,1,0:T(8,128)S(1)} %collective-permute-done.7.refs_3_, ...), custom_call_target="tpu_custom_call" | custom-call | tf_op jit(solution)/shard_map/down/pallas_call | solution.py:460
  (20 shorter events, 0.1 us)
Async XLA Ops:
  0.0 6.9 %slice-start = ((s8[8388608]{0:T(1024)(128)(4,1)}), s8[4194304]{0:T(1024)(128)(4,1)S(1)}, s32[]{:S(2)}) async-start(s8[8388608]{0:T(1024)(128)(4,1)} %bitcast.4), calls=%async_computation | async-start | bytes 8388608
  0.0 6.9 %slice-start.1 = ((s8[8388608]{0:T(1024)(128)(4,1)}), s8[4194304]{0:T(1024)(128)(4,1)S(1)}, s32[]{:S(2)}) async-start(s8[8388608]{0:T(1024)(128)(4,1)} %bitcast.4), calls=%async_computation.1 | async-start | bytes 8388608
  2.4 9.2 %collective-permute-start = (bf16[9,64,128]{2,1,0:T(8,128)(2,1)S(1)}, bf16[9,64,128]{2,1,0:T(8,128)(2,1)S(1)}, u32[]{:S(2)}, u32[]{:S(2)}) collective-permute-start(bf16[9,64,128]{2,1,0:T(8,128)(2,1)S(1)} %get-tuple-element.13.refs_0_), channel_id=1, source_target_pairs={{0,1},{1,0},{2,3},{3,2},{4,5},{5,4},{6,7},{7,6},{8,9},{9,8},{10,11... | collective-permute-start | bytes 442376 | tf_op jit(solution)/shard_map/ppermute | solution.py:290
  5.4 6.9 %collective-permute-start.1 = (bf16[9,64,128]{2,1,0:T(8,128)(2,1)S(1)}, bf16[9,64,128]{2,1,0:T(8,128)(2,1)S(1)}, u32[]{:S(2)}, u32[]{:S(2)}) collective-permute-start(bf16[9,64,128]{2,1,0:T(8,128)(2,1)S(1)} %get-tuple-element.13.refs_0_), channel_id=1, source_target_pairs={{0,2},{1,3},{2,0},{3,1},{4,6},{5,7},{6,4},{7,5},{8,10},{9,11},{10,... | collective-permute-start | bytes 442376 | tf_op jit(solution)/shard_map/ppermute | solution.py:290
  6.9 4.6 %collective-permute-start.2 = (bf16[1,64,128]{2,1,0:T(8,128)(2,1)S(1)}, bf16[1,64,128]{2,1,0:T(8,128)(2,1)S(1)}, u32[]{:S(2)}, u32[]{:S(2)}) collective-permute-start(bf16[1,64,128]{2,1,0:T(8,128)(2,1)S(1)} %get-tuple-element.14.after), channel_id=1, source_target_pairs={{0,3},{1,2},{2,1},{3,0},{4,7},{5,6},{6,5},{7,4},{8,11},{9,10},{10,... | collective-permute-start | bytes 49160 | tf_op jit(solution)/shard_map/ppermute | solution.py:290
  10.2 2.3 %copy-start.2 = (f32[12,4,64,64]{3,2,1,0:T(8,128)S(1)}, f32[12,4,64,64]{3,2,1,0:T(8,128)}, u32[]{:S(2)}) copy-start(f32[12,4,64,64]{3,2,1,0:T(8,128)} %couplings.1) | copy-start | bytes 2359300
  10.2 2.3 %copy-start.4 = (f32[8,64,64]{2,1,0:T(8,128)S(1)}, f32[8,64,64]{2,1,0:T(8,128)}, u32[]{:S(2)}) copy-start(f32[8,64,64]{2,1,0:T(8,128)} %tree.3) | copy-start | bytes 393220
  10.2 2.3 %copy-start.5 = (f32[1,1,64,64]{3,2,1,0:T(8,128)S(1)}, f32[1,1,64,64]{3,2,1,0:T(8,128)}, u32[]{:S(2)}) copy-start(f32[1,1,64,64]{3,2,1,0:T(8,128)} %param.19) | copy-start | bytes 49156
  11.6 4.2 %copy-start.1 = (bf16[16,64,256]{2,1,0:T(8,128)(2,1)S(1)}, bf16[16,64,256]{2,1,0:T(8,128)(2,1)}, u32[]{:S(2)}) copy-start(bf16[16,64,256]{2,1,0:T(8,128)(2,1)} %basis.3) | copy-start | bytes 1572868
  11.6 4.2 %copy-start.3 = (f32[16,64,64]{2,1,0:T(8,128)S(1)}, f32[16,64,64]{2,1,0:T(8,128)}, u32[]{:S(2)}) copy-start(f32[16,64,64]{2,1,0:T(8,128)} %transfer.1) | copy-start | bytes 786436
  11.6 5.0 %collective-permute-start.6 = (bf16[8,64,128]{2,1,0:T(8,128)(2,1)S(1)}, bf16[8,64,128]{2,1,0:T(8,128)(2,1)S(1)}, u32[]{:S(2)}, u32[]{:S(2)}) collective-permute-start(bf16[8,64,128]{2,1,0:T(8,128)(2,1)S(1)} %forward.1), channel_id=1, source_target_pairs={{0,2},{1,3},{2,0},{3,1},{4,6},{5,7},{6,4},{7,5},{8,10},{9,11},{10,... | collective-permute-start | bytes 393224 | tf_op jit(solution)/shard_map/ppermute | solution.py:290
  12.4 4.2 %copy-start = (bf16[16,8,64,64]{3,2,1,0:T(8,128)(2,1)S(1)}, bf16[16,8,64,64]{3,2,1,0:T(8,128)(2,1)}, u32[]{:S(2)}) copy-start(bf16[16,8,64,64]{3,2,1,0:T(8,128)(2,1)} %refs_3_.1) | copy-start | bytes 3145732
  12.4 1.3 %collective-permute-start.3 = (f32[64,64]{1,0:T(8,128)S(1)}, f32[64,64]{1,0:T(8,128)S(1)}, u32[]{:S(2)}, u32[]{:S(2)}) collective-permute-start(f32[64,64]{1,0:T(8,128)S(1)} %group_sum.1.own_node.own), channel_id=1, source_target_pairs={{0,4},{4,0},{8,12},{12,8},{16,20},{20,16},{24,28},{28,24},{1,5},{5... | collective-permute-start | bytes 49160 | tf_op jit(solution)/shard_map/ppermute | solution.py:290
  13.8 4.6 %collective-permute-start.5 = (f32[64,128]{1,0:T(8,128)S(1)}, f32[64,128]{1,0:T(8,128)S(1)}, u32[]{:S(2)}, u32[]{:S(2)}) collective-permute-start(f32[64,128]{1,0:T(8,128)S(1)} %pair.1.refs_4_.after.refs_0_), channel_id=1, source_target_pairs={{0,8},{4,28},{8,0},{12,20},{16,24},{20,12},{24,16},{28,4},{1,9},{5... | collective-permute-start | bytes 98312 | tf_op jit(solution)/shard_map/ppermute | solution.py:393
  15.3 3.9 %collective-permute-start.4 = (f32[64,128]{1,0:T(8,128)S(1)}, f32[64,128]{1,0:T(8,128)S(1)}, u32[]{:S(2)}, u32[]{:S(2)}) collective-permute-start(f32[64,128]{1,0:T(8,128)S(1)} %pair.1.refs_4_.after.refs_0_), channel_id=1, source_target_pairs={{0,8},{4,20},{8,0},{12,28},{16,24},{20,4},{24,16},{28,12},{1,9},{5... | collective-permute-start | bytes 98312 | tf_op jit(solution)/shard_map/ppermute | solution.py:393
  19.3 2.6 %collective-permute-start.7 = (f32[2,64,128]{2,1,0:T(8,128)S(1)}, f32[2,64,128]{2,1,0:T(8,128)S(1)}, u32[]{:S(2)}, u32[]{:S(2)}) collective-permute-start(f32[2,64,128]{2,1,0:T(8,128)S(1)} %relay.1), channel_id=1, source_target_pairs={{0,4},{4,0},{8,12},{12,8},{16,20},{20,16},{24,28},{28,24},{1,5},{5... | collective-permute-start | bytes 196616 | tf_op jit(solution)/shard_map/ppermute | solution.py:290

commit v4 on v3

--- a/solution.py
+++ b/solution.py
@@ -41,9 +41,9 @@
 
 def upward_kernel(count, *refs):
     sources = refs[:count]
-    payload, terms = refs[count : count + 2]
-    kept = refs[count + 2 : count + 6]
-    basis, transfer, matrix, sem = refs[count + 6 :]
+    payload = refs[count]
+    kept = refs[count + 1 : count + 5]
+    basis, transfer, matrix, sem = refs[count + 5 :]
     charges = kept[0]
     targets = (charges, basis, transfer, matrix) + kept[1:]
     copies = [
@@ -56,21 +56,23 @@
         copy.wait()
     pair_count = charges.shape[0] // 2
     rank = basis.shape[1]
-    node = jnp.zeros((charges.shape[1], rank), f32)
+    skeletons = []
     for pair in range(pair_count):
         halves = [
             times_transposed(charges[leaf], basis[leaf]).astype(bf16)
             for leaf in (2 * pair, 2 * pair + 1)
         ]
-        skeleton = jnp.concatenate(halves, axis=1)
-        payload[pair] = skeleton
-        block = transfer[pl.ds(2 * pair, 2)].reshape(2 * rank, rank)
-        high, low = split(block)
-        node = node + (times(skeleton, high) + times(skeleton, low))
+        skeletons.append(jnp.concatenate(halves, axis=1))
+        payload[pair] = skeletons[pair]
+    high, low = split(transfer[...].reshape(2 * pair_count * rank, rank))
+    row = jnp.concatenate(skeletons, axis=1)
+    node = times(row, high) + times(row, low)
     term = exact(times, node, matrix[...])
-    both = jnp.concatenate(split(term), axis=1)
-    terms[0] = both
-    payload[pair_count] = both
+    payload[pair_count] = jnp.concatenate(split(term), axis=1)
+
+
+def mark_kernel(*refs):
+    pass
 
 
 def near_leaf(near_list, charges, blocks, row, leaf):
@@ -81,7 +83,7 @@
     return total
 
 
-def near_kernel(first, list_in, charges, blocks, after, near, near_list, sem):
+def near_rest_kernel(first, list_in, charges, blocks, after, near, near_list, sem):
     listed = pltpu.make_async_copy(list_in, near_list, sem)
     listed.start()
     listed.wait()
@@ -89,27 +91,70 @@
         near[row] = near_leaf(near_list, charges, blocks, first + row, first + row)
 
 
-def pair_kernel(own, other, after, pair):
-    pair[...] = jnp.concatenate([own[...], other[...]], axis=1)
-
-
-def forward_kernel(payload, near, terms, copy):
+def near_kernel(leaf_count, list_in, charges, blocks, after, *refs):
+    sources, couplings_in = refs[:5], refs[5]
+    near, targets, couplings = refs[6], refs[7:12], refs[12]
+    near_list, sem = refs[13:]
+    listed = pltpu.make_async_copy(list_in, near_list, sem.at[0])
+    listed.start()
+    place = lax.axis_index("leaf")
+    moves = list(zip(sources, targets))
+    for height in range(couplings.shape[0]):
+        begin = 2 * leaf_count - 2 * (leaf_count >> height)
+        moves.append((couplings_in.at[begin + (place >> height)], couplings.at[height]))
+    copies = [
+        pltpu.make_async_copy(source, target, sem.at[1 + i])
+        for i, (source, target) in enumerate(moves)
+    ]
+    for copy in copies:
+        copy.start()
+    listed.wait()
+    for leaf in range(near.shape[0]):
+        near[leaf] = near_leaf(near_list, charges, blocks, leaf, leaf)
+    for copy in copies:
+        copy.wait()
+
+
+def joined(both):
+    both = both.astype(f32)
+    rank = both.shape[1] // 2
+    return both[:, :rank] + both[:, rank:]
+
+
+def terms_kernel(own, other, terms):
+    last = own.shape[0] - 1
+    terms[...] = jnp.concatenate([joined(own[last]), joined(other[last])], axis=1)
+
+
+def pair_kernel(mine, theirs, *refs):
+    pair = refs[-1]
+    rank = pair.shape[1] // 2
+    odd = lax.axis_index("leaf") % 2 == 1
+    far = jnp.where(odd, mine[1], theirs[1])
+    flipped = jnp.concatenate([far[:, rank:], far[:, :rank]], axis=1)
+    near = jnp.concatenate([mine[0][:, :rank], theirs[0][:, :rank]], axis=1)
+    pair[...] = near + jnp.where(odd, far, flipped)
+
+
+def forward_kernel(payload, near, copy):
     copy[...] = payload[pl.ds(0, copy.shape[0])]
 
 
 def sum_kernel(count, *refs):
-    arrays, node = refs[:count], refs[-1]
-    rank = node.shape[1]
+    arrays, pairs, sums = refs[:count], refs[count:-2], refs[-1]
     total = None
     for array in arrays:
-        both = array[array.shape[0] - 1].astype(f32)
-        part = both[:, :rank] + both[:, rank:]
+        part = joined(array[array.shape[0] - 1])
         total = part if total is None else total + part
-    node[...] = total
+    sums[0] = jnp.concatenate([total, jnp.zeros_like(total)], axis=1)
+    total = jnp.zeros(sums.shape[1:], f32)
+    for pair in pairs:
+        total = total + pair[...]
+    sums[1] = total
 
 
 def tree_kernel(
-    leaf_count, tree, couplings, matrix, own_node, down_high, down_low, down
+    leaf_count, tree, couplings, matrix, sums, down_high, down_low, down
 ):
     rank = matrix.shape[0]
     depth = leaf_count.bit_length() - 2
@@ -126,7 +171,7 @@
             if abs(offset) == 3:
                 usable = jnp.logical_and(usable, spot % 2 == (0 if offset > 0 else 1))
             entry = begins[height] + jnp.clip(source, 0, members - 1)
-            part = exact(times, back, couplings[begins[height] + spot, slot])
+            part = exact(times, back, couplings[height, slot])
             down[entry] += jnp.where(usable, part, jnp.zeros_like(part))
         if height < depth - 1:
             back = exact(times, back, tree[begins[height] + spot])
@@ -150,14 +195,22 @@
         weights[leaf] = jnp.concatenate([full_high, full_high, full_low], axis=0)
 
 
-def base_kernel(coupled, basis, near, base):
+def base_kernel(distances, coupled, basis, near, near_rest, down_high, down_low, *refs):
+    pairs, base, part = refs[:-2], refs[-2], refs[-1]
     rank = basis.shape[1]
     for pair in range(coupled.shape[0]):
         both = coupled[pair].astype(bf16)
         for half in range(2):
             leaf = 2 * pair + half
             far = times(both[:, half * rank : (half + 1) * rank], basis[leaf])
-            base[leaf] = far + near[leaf]
+            count = near.shape[0]
+            base[leaf] = far + (near[leaf] if leaf < count else near_rest[leaf - count])
+    place = lax.axis_index("leaf")
+    chip, core = place // 2, place % 2
+    total = down_product(down_high, down_low, pairs[0][...], chip, core)
+    for both, at in arrivals(distances, [ref[...] for ref in pairs[1:]], chip, core, 0):
+        total = total + down_product(down_high, down_low, both, at, core)
+    part[...] = total
 
 
 def relay_kernel(count, *refs):
@@ -214,39 +267,39 @@
         coupled[pair] = jnp.concatenate([one(2 * pair), one(2 * pair + 1)], axis=1)
 
 
-def down_kernel(distances, *refs):
-    steps = len(distances[0])
-    own_pair, received, swapped = refs[0], refs[1 : 1 + steps], refs[1 + steps]
-    down_high, down_low, weights, base, out, buffer, sem = refs[2 + steps :]
+def down_product(down_high, down_low, both, chip_at, core):
+    first, second = 2 * chip_at + core, 2 * chip_at + 1 - core
+    high = jnp.concatenate([down_high[first], down_high[second]], axis=1)
+    low = jnp.concatenate([down_low[first], down_low[second]], axis=1)
+    both_high, both_low = split(both)
+    return times_transposed(
+        jnp.concatenate([both_high, both_low, both_high], axis=1),
+        jnp.concatenate([high, high, low], axis=1),
+    )
+
+
+def arrivals(distances, arrays, chip, core, flipped):
+    apart = [distances[core_at ^ flipped] for core_at in range(2)]
+    result = []
+    for step, both in enumerate(arrays):
+        fresh = [apart[core_at].index(apart[core_at][step]) == step for core_at in range(2)]
+        if not all(fresh):
+            both = jnp.where(core == fresh.index(True), both, jnp.zeros_like(both))
+        result.append((both, chip ^ jnp.where(core == 0, apart[0][step], apart[1][step])))
+    return result
+
+
+def down_kernel(distances, part, swapped, down_high, down_low, weights, base, out, buffer, sem):
     place = lax.axis_index("leaf")
     chip, core = place // 2, place % 2
-
-    def product(both, chip_at, flipped):
-        first = 2 * chip_at + (core ^ flipped)
-        second = 2 * chip_at + (1 - (core ^ flipped))
-        high = jnp.concatenate([down_high[first], down_high[second]], axis=1)
-        low = jnp.concatenate([down_low[first], down_low[second]], axis=1)
-        both_high, both_low = split(both)
-        return times_transposed(
-            jnp.concatenate([both_high, both_low, both_high], axis=1),
-            jnp.concatenate([high, high, low], axis=1),
-        )
-
-    total = product(own_pair[...], chip, 0)
-    for step in range(steps):
-        for flipped in range(2):
-            both = swapped[step] if flipped else received[step][...]
-            apart = [distances[core_at ^ flipped] for core_at in range(2)]
-            fresh = [apart[core_at].index(apart[core_at][step]) == step for core_at in range(2)]
-            if not all(fresh):
-                usable = core == fresh.index(True)
-                both = jnp.where(usable, both, jnp.zeros_like(both))
-            at = chip ^ jnp.where(core == 0, apart[0][step], apart[1][step])
-            total = total + product(both, at, flipped)
+    total = part[...]
+    arrays = [swapped[step] for step in range(swapped.shape[0])]
+    for both, at in arrivals(distances, arrays, chip, core, 1):
+        total = total + down_product(down_high, down_low, both, at, 1 - core)
     high, low = split(total)
     wide = jnp.concatenate([high, low, high], axis=1)
     copies = []
-    group = 4
+    group = 2
     for begin in range(0, base.shape[0], group):
         for leaf in range(begin, begin + group):
             buffer[leaf] = (base[leaf] + times(wide, weights[leaf])).astype(bf16)
@@ -292,89 +345,133 @@
     inputs = [stay(panel_charges), stay(leaf_basis), stay(leaf_transfer)]
     inputs += [stay(device_transfer[0, 0]), near_list.T, far_list.T, far_count[None]]
     count = len(inputs)
-    payload, terms, charges, near_list, far_list, far_count = pl.pallas_call(
+    payload, charges, near_list, far_list, far_count = pl.pallas_call(
         functools.partial(upward_kernel, count),
         out_shape=[
             shape(leaves // 2 + 1, rows, 2 * rank),
-            shape(1, rows, 2 * rank),
             like(panel_charges),
             *[like(array) for array in inputs[4:]],
         ],
         in_specs=[anywhere] * count,
-        out_specs=[whole] * 6,
+        out_specs=[whole] * 5,
         scratch_shapes=[
             pltpu.VMEM(leaf_basis.shape, bf16),
             pltpu.VMEM(leaf_transfer.shape, f32),
             pltpu.VMEM((rank, rank), f32),
             pltpu.SemaphoreType.DMA((count,)),
         ],
+        compiler_params=params(4),
+        name="upward",
+    )(*inputs[:4], *[stay(array) for array in inputs[4:]])
+
+    payload = pl.pallas_call(
+        mark_kernel,
+        out_shape=like(payload),
+        in_specs=[anywhere],
+        out_specs=anywhere,
+        input_output_aliases={0: 0},
+        compiler_params=params(1),
+        cost_estimate=pl.CostEstimate(
+            flops=64 * near_blocks.size * rows,
+            bytes_accessed=64 * near_blocks.size,
+            transcendentals=0,
+        ),
+        name="mark",
+    )(payload)
+
+    other_payload = exchange(payload, "leaf", 1)
+    direct = [distance for distance in range(1, list_count) if distance & (distance - 1) == 0]
+    arrived = {distance: exchange(payload, "list", distance) for distance in direct}
+
+    terms = pl.pallas_call(
+        terms_kernel,
+        out_shape=shape(rows, 2 * rank, dtype=f32),
+        in_specs=[whole] * 2,
+        out_specs=whole,
+        compiler_params=params(2),
+        name="terms",
+    )(payload, other_payload)
+
+    def send_pairs(distance):
+        places = [(l, j) for l in range(leaf_count) for j in range(list_count)]
+        ends = [l * list_count + (j ^ (distance if l % 2 else direct[0])) for l, j in places]
+        return lax.ppermute(terms, ("leaf", "list"), list(enumerate(ends)))
+
+    far_terms = [
+        send_pairs(distance) for distance in range(1, list_count) if distance not in direct
+    ]
+
+    early = leaves * 14 // 16
+    depth = leaf_count.bit_length() - 2
+    fetched = [tree_transfer, device_transfer[0, 0], leaf_transfer, leaf_basis, far_coupling]
+    near, tree_matrices, device_matrix, transfer, basis, coupling, couplings = pl.pallas_call(
+        functools.partial(near_kernel, leaf_count),
+        out_shape=[
+            shape(early, rows, panels, dtype=f32),
+            *[like(array) for array in fetched],
+            shape(depth, *level_coupling.shape[1:], dtype=f32),
+        ],
+        in_specs=[anywhere, whole, whole] + [anywhere] * (2 + len(fetched)),
+        out_specs=[whole] * (2 + len(fetched)),
+        scratch_shapes=[
+            pltpu.SMEM(near_list.shape, jnp.int32),
+            pltpu.SemaphoreType.DMA((1 + len(fetched) + depth,)),
+        ],
+        compiler_params=params(12),
+        cost_estimate=pl.CostEstimate(
+            flops=2 * near_blocks.size * rows,
+            bytes_accessed=2 * near_blocks.size,
+            transcendentals=0,
+        ),
+        name="near",
+    )(
+        near_list,
+        charges,
+        near_blocks,
+        terms,
+        *[stay(array) for array in fetched],
+        stay(level_coupling),
+    )
+
+    sums = pl.pallas_call(
+        functools.partial(sum_kernel, 1 + len(direct)),
+        out_shape=shape(2, rows, 2 * rank, dtype=f32),
+        in_specs=[whole] * (1 + len(direct) + len(far_terms)) + [anywhere],
+        out_specs=whole,
+        compiler_params=params(4),
+        name="group_sum",
+    )(payload, *[arrived[distance] for distance in direct], *far_terms, near)
+    other_sums = exchange(sums, "leaf", 1)
+
+    bases = direct[:-1]
+    forward = {}
+    for base in bases:
+        forward[base] = pl.pallas_call(
+            forward_kernel,
+            out_shape=shape(leaves // 2, rows, 2 * rank),
+            in_specs=[whole, anywhere],
+            out_specs=whole,
+            compiler_params=params(2),
+            name="forward",
+        )(arrived[base], near)
+
+    down_high, down_low = pl.pallas_call(
+        functools.partial(tree_kernel, leaf_count),
+        out_shape=[
+            shape(leaf_count, rank, rank),
+            shape(leaf_count, rank, rank),
+        ],
+        in_specs=[whole] * 3 + [anywhere],
+        out_specs=[whole] * 2,
+        scratch_shapes=[pltpu.VMEM((2 * leaf_count, rank, rank), f32)],
         compiler_params=params(4),
         cost_estimate=pl.CostEstimate(
             flops=64 * near_blocks.size * rows,
             bytes_accessed=64 * near_blocks.size,
             transcendentals=0,
         ),
-        name="upward",
-    )(*inputs[:4], *[stay(array) for array in inputs[4:]])
-
-    direct = [distance for distance in range(1, list_count) if distance & (distance - 1) == 0]
-    arrived = {
-        distance: exchange(payload if distance in direct else terms, "list", distance)
-        for distance in range(1, list_count)
-    }
-
-    def near_part(first, count, after):
-        return pl.pallas_call(
-            functools.partial(near_kernel, first),
-            out_shape=shape(count, rows, panels, dtype=f32),
-            in_specs=[anywhere, whole, whole, anywhere],
-            out_specs=whole,
-            scratch_shapes=[pltpu.SMEM(near_list.shape, jnp.int32), pltpu.SemaphoreType.DMA],
-            compiler_params=params(4),
-            cost_estimate=pl.CostEstimate(
-                flops=2 * near_blocks.size * rows,
-                bytes_accessed=2 * near_blocks.size,
-                transcendentals=0,
-            ),
-            name="near",
-        )(near_list, charges, near_blocks, after)
-
-    near = near_part(0, leaves, terms)
-
-    bases = direct[:-1]
-    forward = {}
-    for base in bases:
-        forward[base] = pl.pallas_call(
-            forward_kernel,
-            out_shape=shape(leaves // 2, rows, 2 * rank),
-            in_specs=[whole, anywhere, anywhere],
-            out_specs=whole,
-            compiler_params=params(2),
-            name="forward",
-        )(arrived[base], near, arrived[list_count - 1])
-
-    own_node = pl.pallas_call(
-        functools.partial(sum_kernel, list_count),
-        out_shape=shape(rows, rank, dtype=f32),
-        in_specs=[whole] * list_count + [anywhere],
-        out_specs=whole,
-        compiler_params=params(4),
-        name="group_sum",
-    )(payload, *[arrived[distance] for distance in range(1, list_count)], near)
-    other_node = exchange(own_node, "leaf", 1)
-
-    down_high, down_low = pl.pallas_call(
-        functools.partial(tree_kernel, leaf_count),
-        out_shape=[
-            shape(leaf_count, rank, rank),
-            shape(leaf_count, rank, rank),
-        ],
-        in_specs=[whole] * 3 + [anywhere],
-        out_specs=[whole] * 2,
-        scratch_shapes=[pltpu.VMEM((2 * leaf_count, rank, rank), f32)],
-        compiler_params=params(4),
         name="tree",
-    )(tree_transfer, level_coupling, device_transfer[0, 0], own_node)
+    )(tree_matrices, couplings, device_matrix, sums)
 
     own_pair = pl.pallas_call(
         pair_kernel,
@@ -383,7 +480,7 @@
         out_specs=whole,
         compiler_params=params(2),
         name="pair",
-    )(own_node, other_node, down_high)
+    )(sums, other_sums, down_high)
 
     steps = chip_count // 2
     apart = list(range(1, chip_count))
@@ -395,6 +492,16 @@
         )
         for step in range(steps)
     ]
+
+    near_rest = pl.pallas_call(
+        functools.partial(near_rest_kernel, early),
+        out_shape=shape(leaves - early, rows, panels, dtype=f32),
+        in_specs=[anywhere, whole, whole, anywhere],
+        out_specs=whole,
+        scratch_shapes=[pltpu.SMEM(near_list.shape, jnp.int32), pltpu.SemaphoreType.DMA],
+        compiler_params=params(4),
+        name="near_rest",
+    )(near_list, charges, near_blocks, own_pair)
 
     skeletons = {distance: arrived[distance] for distance in direct}
     for distance in range(1, list_count):
@@ -425,9 +532,19 @@
         far_list,
         far_count,
         *[skeletons[distance] for distance in range(1, list_count)],
-        far_coupling,
-        own_pair,
+        coupling,
+        near_rest,
     )
+
+    relayed = pl.pallas_call(
+        functools.partial(relay_kernel, steps),
+        out_shape=shape(steps, rows, 2 * rank, dtype=f32),
+        in_specs=[whole] * steps + [anywhere],
+        out_specs=whole,
+        compiler_params=params(2),
+        name="relay",
+    )(*received, coupled)
+    swapped = exchange(relayed, "leaf", 1)
 
     weights = pl.pallas_call(
         weights_kernel,
@@ -436,47 +553,33 @@
         out_specs=whole,
         compiler_params=params(4),
         name="weights",
-    )(leaf_transfer, leaf_basis, own_pair)
-
-    relayed = pl.pallas_call(
-        functools.partial(relay_kernel, steps),
-        out_shape=shape(steps, rows, 2 * rank, dtype=f32),
-        in_specs=[whole] * steps + [anywhere] * 2,
-        out_specs=whole,
-        compiler_params=params(2),
-        name="relay",
-    )(*received, coupled, weights)
-    swapped = exchange(relayed, "leaf", 1)
-
-    base = pl.pallas_call(
-        base_kernel,
-        out_shape=shape(leaves, rows, panels, dtype=f32),
-        in_specs=[whole] * 3,
-        out_specs=whole,
+    )(transfer, basis, relayed)
+
+
+    base, part = pl.pallas_call(
+        functools.partial(base_kernel, distances),
+        out_shape=[
+            shape(leaves, rows, panels, dtype=f32),
+            shape(rows, rank, dtype=f32),
+        ],
+        in_specs=[whole] * (7 + steps),
+        out_specs=[whole] * 2,
         compiler_params=params(4),
         name="base",
-    )(coupled, leaf_basis, near)
+    )(coupled, basis, near, near_rest, down_high, down_low, own_pair, *received)
 
     return pl.pallas_call(
         functools.partial(down_kernel, distances),
         out_shape=shape(leaves, rows, panels),
-        in_specs=[whole] * (steps + 6),
+        in_specs=[whole] * 6,
         out_specs=anywhere,
         scratch_shapes=[
             pltpu.VMEM((leaves, rows, panels), bf16),
-            pltpu.SemaphoreType.DMA((leaves // 4,)),
+            pltpu.SemaphoreType.DMA((leaves // 2,)),
         ],
         compiler_params=params(4),
         name="down",
-    )(
-        own_pair,
-        *received,
-        swapped,
-        down_high,
-        down_low,
-        weights,
-        base,
-    )
+    )(part, swapped, down_high, down_low, weights, base)
 
 
 def solution(mesh):

time: 23.4 us -> 23 us (0.983)
  waiting for transfers between devices: 3.56 us -> 1.24 us
  starting transfers between devices: 9.01 us -> 10.3 us
  Pallas kernels: 10.5 us -> 11.2 us
    ppermute x6, waiting for transfers between devices: 2.68 us -> 0.54 us  [exchange(): return lax.ppermute(array, axis, pairs)]
    pallas_call x3 -> x6, Pallas kernels: 3.62 us -> 4.58 us  [the longest x1 2.97 us: on_device(): pl.pallas_call(functools.partial(near_kernel, leaf_count), out_shape=[sha...]
    ppermute x6, starting transfers between devices: 6.98 us -> 7.69 us  [exchange(): return lax.ppermute(array, axis, pairs)]
    ppermute x0 -> x1, starting transfers between devices: none -> 0.54 us  [send_pairs(): return lax.ppermute(terms, ('leaf', 'list'), list(enumerate(ends)))]
  transfers between devices with their start and end apart: 8 -> 9, of which waited for: 5 -> 2; matrix products, arithmetic and copies ran while one was open for 0% -> 0% of each run, Pallas kernels for 29% -> 33%
where the time goes in v4:
time: 23 us; the launch traced here: 22.9 us
  Pallas kernels  11.2 us (49%)
  starting transfers between devices  10.3 us (45%)
  waiting for transfers between devices  1.24 us (5%)
    ppermute x6, starting transfers between devices, exchange(): return lax.ppermute(array, axis, pairs)  7.69 us
    pallas_call x1, Pallas kernels, on_device(): pl.pallas_call(functools.partial(near_kernel, leaf_count), out_shape=[sha...  2.97 us
    pallas_call x1, Pallas kernels, on_device(): pl.pallas_call(functools.partial(upward_kernel, count), out_shape=[shape(...  2.17 us
    ppermute x2, starting transfers between devices, on_device(): lax.ppermute(own_pair, 'leaf', [(i, i ^ 2 * distances[i % 2][step]) for i...  2.09 us
    pallas_call x1, Pallas kernels, on_device(): pl.pallas_call(functools.partial(far_kernel, list_count - 1), out_shape=s...  1.73 us
    pallas_call x1, Pallas kernels, on_device(): pl.pallas_call(functools.partial(down_kernel, distances), out_shape=shape...  1.39 us
    pallas_call x1, Pallas kernels, on_device(): pl.pallas_call(functools.partial(near_rest_kernel, early), out_shape=shap...  1.01 us
    pallas_call x1, Pallas kernels, on_device(): pl.pallas_call(functools.partial(tree_kernel, leaf_count), out_shape=[sha...  0.75 us
  transfers between devices with their start and end apart: 9, of which 2 were waited for; matrix products, arithmetic and copies ran while one was open for 0% of the time, Pallas kernels for 33%

profile of v4, /device:TPU:0, one launch (start us, length us, event | category | flops | bytes accessed | tf_op | source)
XLA Modules:
  0.0 22.9 jit_solution(1236975955520617923)
XLA Ops:
  0.0 2.2 %upward.1 = (bf16[9,64,128]{2,1,0:T(8,128)(2,1)S(1)}, bf16[16,64,256]{2,1,0:T(8,128)(2,1)S(1)}, s32[4,16]{1,0:T(4,128)S(1)}, s32[8,16]{1,0:T(8,128)S(1)}, s32[1,16]{1,0:T(1,128)S(1)}) custom-call(bf16[16,64,256]{2,1,0:T(8,128)(2,1)} %refs_0_.2, bf16[16,64,256]{2,1,0:T(8,128)(2,1)} %refs_3_.1, f32[16,64,64]{2,1,0:T(8,128)} %refs_2_.3, f32[64,64]{1,0:T(8,128)} %bitcast.6, ...), custom_call_target="tpu_custom_call" | custom-call | tf_op jit(solution)/shard_map/upward/pallas_call | solution.py:348
  2.2 0.0 slice-start
  2.2 0.5 %collective-permute-start.2 = (bf16[9,64,128]{2,1,0:T(8,128)(2,1)S(1)}, bf16[9,64,128]{2,1,0:T(8,128)(2,1)S(1)}, u32[]{:S(2)}, u32[]{:S(2)}) collective-permute-start(bf16[9,64,128]{2,1,0:T(8,128)(2,1)S(1)} %mark.1.own.refs_0_), channel_id=1, source_target_pairs={{0,4},{4,0},{8,12},{12,8},{16,20},{20,16},{24,28},{28,24},{1,5},{5... | collective-permute-start | bytes 442376 | tf_op jit(solution)/shard_map/ppermute | solution.py:343
  2.7 2.6 %collective-permute-start = (bf16[9,64,128]{2,1,0:T(8,128)(2,1)S(1)}, bf16[9,64,128]{2,1,0:T(8,128)(2,1)S(1)}, u32[]{:S(2)}, u32[]{:S(2)}) collective-permute-start(bf16[9,64,128]{2,1,0:T(8,128)(2,1)S(1)} %mark.1.own.refs_0_), channel_id=1, source_target_pairs={{0,1},{1,0},{2,3},{3,2},{4,5},{5,4},{6,7},{7,6},{8,9},{9,8},{10,11... | collective-permute-start | bytes 442376 | tf_op jit(solution)/shard_map/ppermute | solution.py:343
  5.3 1.5 %collective-permute-start.1 = (bf16[9,64,128]{2,1,0:T(8,128)(2,1)S(1)}, bf16[9,64,128]{2,1,0:T(8,128)(2,1)S(1)}, u32[]{:S(2)}, u32[]{:S(2)}) collective-permute-start(bf16[9,64,128]{2,1,0:T(8,128)(2,1)S(1)} %mark.1.own.refs_0_), channel_id=1, source_target_pairs={{0,2},{1,3},{2,0},{3,1},{4,6},{5,7},{6,4},{7,5},{8,10},{9,11},{10,... | collective-permute-start | bytes 442376 | tf_op jit(solution)/shard_map/ppermute | solution.py:343
  6.8 0.1 terms.1.after
  7.0 0.5 %collective-permute-start.4 = (f32[64,128]{1,0:T(8,128)S(1)}, f32[64,128]{1,0:T(8,128)S(1)}, u32[]{:S(2)}, u32[]{:S(2)}) collective-permute-start(f32[64,128]{1,0:T(8,128)S(1)} %terms.1.after), channel_id=1, source_target_pairs={{0,1},{1,0},{2,3},{3,2},{4,7},{5,6},{6,5},{7,4},{8,9},{9,8},{10,11... | collective-permute-start | bytes 98312 | tf_op jit(solution)/shard_map/ppermute | solution.py:398
  7.5 3.0 %near.1 = (f32[14,64,256]{2,1,0:T(8,128)S(1)}, f32[8,64,64]{2,1,0:T(8,128)S(1)}, f32[64,64]{1,0:T(8,128)S(1)}, f32[16,64,64]{2,1,0:T(8,128)S(1)}, bf16[16,64,256...) custom-call(s32[4,16]{1,0:T(4,128)S(1)} %get-tuple-element.24.list_in, ...), custom_call_target="tpu_custom_call" | custom-call | flops 536870912 | bytes 8388608 | tf_op jit(solution)/shard_map/near/pallas_call | solution.py:407
  10.5 1.4 %collective-permute-start.3 = (bf16[8,64,128]{2,1,0:T(8,128)(2,1)S(1)}, bf16[8,64,128]{2,1,0:T(8,128)(2,1)S(1)}, u32[]{:S(2)}, u32[]{:S(2)}) collective-permute-start(bf16[8,64,128]{2,1,0:T(8,128)(2,1)S(1)} %forward.1), channel_id=1, source_target_pairs={{0,2},{1,3},{2,0},{3,1},{4,6},{5,7},{6,4},{7,5},{8,10},{9,11},{10,... | collective-permute-start | bytes 393224 | tf_op jit(solution)/shard_map/ppermute | solution.py:343
  12.0 0.1 group_sum.1.sums.mine
  12.0 0.1 collective-permute-start.5
  12.1 0.8 %tree.1 = (bf16[8,64,64]{2,1,0:T(8,128)(2,1)S(1)}, bf16[8,64,64]{2,1,0:T(8,128)(2,1)S(1)}) custom-call(f32[8,64,64]{2,1,0:T(8,128)S(1)} %get-tuple-element.28.tree, f32[2,4,64,64]{3,2,1,0:T(8,128)S(1)} %get-tuple-element.29.couplings, f32[64,64]{1,0:T(8,128)S(1)} %get-tuple-element.30.matrix, f32[2,64,128]{2,1,0:T(8,128)S(1)} %group_sum.1.sums.mine), custom_call_target="tpu_custom_call" | custom-call | flops 17179869184 | bytes 268435456 | tf_op jit(solution)/shard_map/tree/pallas_call | solution.py:458
  12.9 0.5 %collective-permute-done.5.theirs = f32[2,64,128]{2,1,0:T(8,128)S(1)} collective-permute-done((f32[2,64,128]{2,1,0:T(8,128)S(1)}, f32[2,64,128]{2,1,0:T(8,128)S(1)}, u32[]{:S(2)}, u32[]{:S(2)}) %collective-permute-start.5) | collective-permute-done | bytes 65568 | tf_op jit(solution)/shard_map/ppermute | solution.py:343
  13.4 0.1 pair.1.after.refs_0_
  13.5 1.6 %collective-permute-start.6 = (f32[64,128]{1,0:T(8,128)S(1)}, f32[64,128]{1,0:T(8,128)S(1)}, u32[]{:S(2)}, u32[]{:S(2)}) collective-permute-start(f32[64,128]{1,0:T(8,128)S(1)} %pair.1.after.refs_0_), channel_id=1, source_target_pairs={{0,8},{4,20},{8,0},{12,28},{16,24},{20,4},{24,16},{28,12},{1,9},{5... | collective-permute-start | bytes 98312 | tf_op jit(solution)/shard_map/ppermute | solution.py:490
  15.1 0.4 %collective-permute-start.7 = (f32[64,128]{1,0:T(8,128)S(1)}, f32[64,128]{1,0:T(8,128)S(1)}, u32[]{:S(2)}, u32[]{:S(2)}) collective-permute-start(f32[64,128]{1,0:T(8,128)S(1)} %pair.1.after.refs_0_), channel_id=1, source_target_pairs={{0,8},{4,28},{8,0},{12,20},{16,24},{20,12},{24,16},{28,4},{1,9},{5... | collective-permute-start | bytes 98312 | tf_op jit(solution)/shard_map/ppermute | solution.py:490
  15.5 1.0 %near_rest.1.refs_4_ = f32[2,64,256]{2,1,0:T(8,128)S(1)} custom-call(s32[4,16]{1,0:T(4,128)S(1)} %get-tuple-element.24.list_in, bf16[16,64,256]{2,1,0:T(8,128)(2,1)S(1)} %get-tuple-element.25.charges, bf16[16,4,256,256]{3,2,1,0:T(8,128)(2,1)S(1)} %bitcast.5, f32[64,128]{1,0:T(8,128)S(1)} %pair.1.after.refs_0_), custom_call_target="tpu_custom_call" | custom-call | tf_op jit(solution)/shard_map/near_rest/pallas_call | solution.py:496
  16.6 1.7 %far.1.coupled.refs_2_ = f32[8,64,128]{2,1,0:T(8,128)S(1)} custom-call(s32[8,16]{1,0:T(8,128)S(1)} %get-tuple-element.21.list_in, s32[1,16]{1,0:T(1,128)S(1)} %get-tuple-element.22.count_in, bf16[9,64,128]{2,1,0:T(8,128)(2,1)S(1)} %collective-permute-done.payload.refs_1_.refs_0_, bf16[9,64,128]{2,1,0:T(8,128)(2,1)S(1)} %collective-permute-done.1.refs_2_.refs_1_, ...), custom_call_target="tpu_custom_call" | custom-call | flops 268435456 | bytes 2097152 | tf_op jit(solution)/shard_map/far/pallas_call | solution.py:513
  18.3 0.7 %collective-permute-done.7.refs_2_.refs_1_ = f32[64,128]{1,0:T(8,128)S(1)} collective-permute-done((f32[64,128]{1,0:T(8,128)S(1)}, f32[64,128]{1,0:T(8,128)S(1)}, u32[]{:S(2)}, u32[]{:S(2)}) %collective-permute-start.7) | collective-permute-done | bytes 32800 | tf_op jit(solution)/shard_map/ppermute | solution.py:490
  19.0 1.6 %collective-permute-start.8 = (f32[2,64,128]{2,1,0:T(8,128)S(1)}, f32[2,64,128]{2,1,0:T(8,128)S(1)}, u32[]{:S(2)}, u32[]{:S(2)}) collective-permute-start(f32[2,64,128]{2,1,0:T(8,128)S(1)} %relay.1.after), channel_id=1, source_target_pairs={{0,4},{4,0},{8,12},{12,8},{16,20},{20,16},{24,28},{28,24},{1,5},{5... | collective-permute-start | bytes 196616 | tf_op jit(solution)/shard_map/ppermute | solution.py:343
  20.6 0.5 %weights.1 = bf16[16,192,256]{2,1,0:T(8,128)(2,1)S(1)} custom-call(f32[16,64,64]{2,1,0:T(8,128)S(1)} %get-tuple-element.35.transfer, bf16[16,64,256]{2,1,0:T(8,128)(2,1)S(1)} %get-tuple-element.32.basis, f32[2,64,128]{2,1,0:T(8,128)S(1)} %relay.1.after), custom_call_target="tpu_custom_call" | custom-call | tf_op jit(solution)/shard_map/weights/pallas_call | solution.py:549
  21.1 0.4 %base.1 = (f32[16,64,256]{2,1,0:T(8,128)S(1)}, f32[64,64]{1,0:T(8,128)S(1)}) custom-call(f32[8,64,128]{2,1,0:T(8,128)S(1)} %far.1.coupled.refs_2_, bf16[16,64,256]{2,1,0:T(8,128)(2,1)S(1)} %get-tuple-element.32.basis, f32[14,64,256]{2,1,0:T(8,128)S(1)} %get-tuple-element.26.near.refs_4_, f32[2,64,256]{2,1,0:T(8,128)S(1)} %near_rest.1.refs_4_, ...), custom_call_target="tpu_custom_call" | custom-call | tf_op jit(solution)/shard_map/base/pallas_call | solution.py:559
  21.4 0.0 collective-permute-done.8.swapped
  21.5 1.4 %down.1 = bf16[16,64,256]{2,1,0:T(8,128)(2,1)} custom-call(f32[64,64]{1,0:T(8,128)S(1)} %get-tuple-element.34.part, f32[2,64,128]{2,1,0:T(8,128)S(1)} %collective-permute-done.8.swapped, bf16[8,64,64]{2,1,0:T(8,128)(2,1)S(1)} %get-tuple-element.31.refs_0_.down_high, bf16[8,64,64]{2,1,0:T(8,128)(2,1)S(1)} %get-tuple-element.33.down_low, ...), custom_call_target="tpu_custom_call" | custom-call | tf_op jit(solution)/shard_map/down/pallas_call | solution.py:571
  (13 shorter events, 0.0 us)
Async XLA Ops:
  2.2 5.3 %slice-start = ((s8[8388608]{0:T(1024)(128)(4,1)}), s8[4194304]{0:T(1024)(128)(4,1)S(1)}, s32[]{:S(2)}) async-start(s8[8388608]{0:T(1024)(128)(4,1)} %bitcast.4), calls=%async_computation | async-start | bytes 8388608
  2.2 5.3 %slice-start.1 = ((s8[8388608]{0:T(1024)(128)(4,1)}), s8[4194304]{0:T(1024)(128)(4,1)S(1)}, s32[]{:S(2)}) async-start(s8[8388608]{0:T(1024)(128)(4,1)} %bitcast.4), calls=%async_computation.1 | async-start | bytes 8388608
  2.2 4.6 %collective-permute-start.2 = (bf16[9,64,128]{2,1,0:T(8,128)(2,1)S(1)}, bf16[9,64,128]{2,1,0:T(8,128)(2,1)S(1)}, u32[]{:S(2)}, u32[]{:S(2)}) collective-permute-start(bf16[9,64,128]{2,1,0:T(8,128)(2,1)S(1)} %mark.1.own.refs_0_), channel_id=1, source_target_pairs={{0,4},{4,0},{8,12},{12,8},{16,20},{20,16},{24,28},{28,24},{1,5},{5... | collective-permute-start | bytes 442376 | tf_op jit(solution)/shard_map/ppermute | solution.py:343
  2.7 7.8 %collective-permute-start = (bf16[9,64,128]{2,1,0:T(8,128)(2,1)S(1)}, bf16[9,64,128]{2,1,0:T(8,128)(2,1)S(1)}, u32[]{:S(2)}, u32[]{:S(2)}) collective-permute-start(bf16[9,64,128]{2,1,0:T(8,128)(2,1)S(1)} %mark.1.own.refs_0_), channel_id=1, source_target_pairs={{0,1},{1,0},{2,3},{3,2},{4,5},{5,4},{6,7},{7,6},{8,9},{9,8},{10,11... | collective-permute-start | bytes 442376 | tf_op jit(solution)/shard_map/ppermute | solution.py:343
  5.3 6.7 %collective-permute-start.1 = (bf16[9,64,128]{2,1,0:T(8,128)(2,1)S(1)}, bf16[9,64,128]{2,1,0:T(8,128)(2,1)S(1)}, u32[]{:S(2)}, u32[]{:S(2)}) collective-permute-start(bf16[9,64,128]{2,1,0:T(8,128)(2,1)S(1)} %mark.1.own.refs_0_), channel_id=1, source_target_pairs={{0,2},{1,3},{2,0},{3,1},{4,6},{5,7},{6,4},{7,5},{8,10},{9,11},{10,... | collective-permute-start | bytes 442376 | tf_op jit(solution)/shard_map/ppermute | solution.py:343
  7.0 5.0 %collective-permute-start.4 = (f32[64,128]{1,0:T(8,128)S(1)}, f32[64,128]{1,0:T(8,128)S(1)}, u32[]{:S(2)}, u32[]{:S(2)}) collective-permute-start(f32[64,128]{1,0:T(8,128)S(1)} %terms.1.after), channel_id=1, source_target_pairs={{0,1},{1,0},{2,3},{3,2},{4,7},{5,6},{6,5},{7,4},{8,9},{9,8},{10,11... | collective-permute-start | bytes 98312 | tf_op jit(solution)/shard_map/ppermute | solution.py:398
  10.5 6.0 %collective-permute-start.3 = (bf16[8,64,128]{2,1,0:T(8,128)(2,1)S(1)}, bf16[8,64,128]{2,1,0:T(8,128)(2,1)S(1)}, u32[]{:S(2)}, u32[]{:S(2)}) collective-permute-start(bf16[8,64,128]{2,1,0:T(8,128)(2,1)S(1)} %forward.1), channel_id=1, source_target_pairs={{0,2},{1,3},{2,0},{3,1},{4,6},{5,7},{6,4},{7,5},{8,10},{9,11},{10,... | collective-permute-start | bytes 393224 | tf_op jit(solution)/shard_map/ppermute | solution.py:343
  12.0 1.3 %collective-permute-start.5 = (f32[2,64,128]{2,1,0:T(8,128)S(1)}, f32[2,64,128]{2,1,0:T(8,128)S(1)}, u32[]{:S(2)}, u32[]{:S(2)}) collective-permute-start(f32[2,64,128]{2,1,0:T(8,128)S(1)} %group_sum.1.sums.mine), channel_id=1, source_target_pairs={{0,4},{4,0},{8,12},{12,8},{16,20},{20,16},{24,28},{28,24},{1,5},{5... | collective-permute-start | bytes 196616 | tf_op jit(solution)/shard_map/ppermute | solution.py:343
  13.5 4.9 %collective-permute-start.6 = (f32[64,128]{1,0:T(8,128)S(1)}, f32[64,128]{1,0:T(8,128)S(1)}, u32[]{:S(2)}, u32[]{:S(2)}) collective-permute-start(f32[64,128]{1,0:T(8,128)S(1)} %pair.1.after.refs_0_), channel_id=1, source_target_pairs={{0,8},{4,20},{8,0},{12,28},{16,24},{20,4},{24,16},{28,12},{1,9},{5... | collective-permute-start | bytes 98312 | tf_op jit(solution)/shard_map/ppermute | solution.py:490
  15.1 3.9 %collective-permute-start.7 = (f32[64,128]{1,0:T(8,128)S(1)}, f32[64,128]{1,0:T(8,128)S(1)}, u32[]{:S(2)}, u32[]{:S(2)}) collective-permute-start(f32[64,128]{1,0:T(8,128)S(1)} %pair.1.after.refs_0_), channel_id=1, source_target_pairs={{0,8},{4,28},{8,0},{12,20},{16,24},{20,12},{24,16},{28,4},{1,9},{5... | collective-permute-start | bytes 98312 | tf_op jit(solution)/shard_map/ppermute | solution.py:490
  19.0 2.5 %collective-permute-start.8 = (f32[2,64,128]{2,1,0:T(8,128)S(1)}, f32[2,64,128]{2,1,0:T(8,128)S(1)}, u32[]{:S(2)}, u32[]{:S(2)}) collective-permute-start(f32[2,64,128]{2,1,0:T(8,128)S(1)} %relay.1.after), channel_id=1, source_target_pairs={{0,4},{4,0},{8,12},{12,8},{16,20},{20,16},{24,28},{28,24},{1,5},{5... | collective-permute-start | bytes 196616 | tf_op jit(solution)/shard_map/ppermute | solution.py:343

commit v5 on v4

--- a/solution.py
+++ b/solution.py
@@ -39,13 +39,16 @@
     )
 
 
+def mirrored(distance, count):
+    bits = count.bit_length() - 1
+    return sum(((distance >> i) & 1) << (bits - 1 - i) for i in range(bits))
+
+
 def upward_kernel(count, *refs):
     sources = refs[:count]
     payload = refs[count]
-    kept = refs[count + 1 : count + 5]
-    basis, transfer, matrix, sem = refs[count + 5 :]
-    charges = kept[0]
-    targets = (charges, basis, transfer, matrix) + kept[1:]
+    charges, basis, transfer, *lists, matrix, sem = refs[count + 1 :]
+    targets = [charges, basis, transfer, matrix] + lists
     copies = [
         pltpu.make_async_copy(source, target, sem.at[i])
         for i, (source, target) in enumerate(zip(sources, targets))
@@ -75,6 +78,10 @@
     pass
 
 
+def pause_kernel(after, out):
+    out[...] = jnp.zeros_like(out)
+
+
 def near_leaf(near_list, charges, blocks, row, leaf):
     total = None
     for slot in range(blocks.shape[1]):
@@ -83,18 +90,10 @@
     return total
 
 
-def near_rest_kernel(first, list_in, charges, blocks, after, near, near_list, sem):
-    listed = pltpu.make_async_copy(list_in, near_list, sem)
-    listed.start()
-    listed.wait()
-    for row in range(near.shape[0]):
-        near[row] = near_leaf(near_list, charges, blocks, first + row, first + row)
-
-
 def near_kernel(leaf_count, list_in, charges, blocks, after, *refs):
-    sources, couplings_in = refs[:5], refs[5]
-    near, targets, couplings = refs[6], refs[7:12], refs[12]
-    near_list, sem = refs[13:]
+    sources, couplings_in = refs[:4], refs[4]
+    near, targets, couplings = refs[5], refs[6:10], refs[10]
+    near_list, sem = refs[11:]
     listed = pltpu.make_async_copy(list_in, near_list, sem.at[0])
     listed.start()
     place = lax.axis_index("leaf")
@@ -127,13 +126,15 @@
 
 
 def pair_kernel(mine, theirs, *refs):
-    pair = refs[-1]
+    pair, rounded = refs[-2:]
     rank = pair.shape[1] // 2
     odd = lax.axis_index("leaf") % 2 == 1
     far = jnp.where(odd, mine[1], theirs[1])
     flipped = jnp.concatenate([far[:, rank:], far[:, :rank]], axis=1)
     near = jnp.concatenate([mine[0][:, :rank], theirs[0][:, :rank]], axis=1)
-    pair[...] = near + jnp.where(odd, far, flipped)
+    total = near + jnp.where(odd, far, flipped)
+    pair[...] = total
+    rounded[...] = total.astype(bf16)
 
 
 def forward_kernel(payload, near, copy):
@@ -195,7 +196,7 @@
         weights[leaf] = jnp.concatenate([full_high, full_high, full_low], axis=0)
 
 
-def base_kernel(distances, coupled, basis, near, near_rest, down_high, down_low, *refs):
+def base_kernel(coupled, basis, near, down_high, down_low, own, beside, *refs):
     pairs, base, part = refs[:-2], refs[-2], refs[-1]
     rank = basis.shape[1]
     for pair in range(coupled.shape[0]):
@@ -203,13 +204,14 @@
         for half in range(2):
             leaf = 2 * pair + half
             far = times(both[:, half * rank : (half + 1) * rank], basis[leaf])
-            count = near.shape[0]
-            base[leaf] = far + (near[leaf] if leaf < count else near_rest[leaf - count])
+            base[leaf] = far + near[leaf]
     place = lax.axis_index("leaf")
     chip, core = place // 2, place % 2
-    total = down_product(down_high, down_low, pairs[0][...], chip, core)
-    for both, at in arrivals(distances, [ref[...] for ref in pairs[1:]], chip, core, 0):
-        total = total + down_product(down_high, down_low, both, at, core)
+    total = down_product(down_high, down_low, own[...], chip, core)
+    total = total + down_product(down_high, down_low, beside[...], chip ^ 1, core)
+    for step, pair in enumerate(pairs):
+        at = chip ^ (2 + step + len(pairs) * core)
+        total = total + down_product(down_high, down_low, pair[...], at, core)
     part[...] = total
 
 
@@ -233,12 +235,14 @@
     pair_count = leaves // 2
     empty = peer_count * leaves
     table[empty] = jnp.zeros(table.shape[1:], bf16)
+    odd = lax.axis_index("leaf") % 2 == 1
     for peer in range(peer_count):
+        begin = jnp.where(odd, mirrored(peer + 1, peer_count + 1) - 1, peer) * leaves
         for pair in range(pair_count):
             block = peers[peer][pair]
             first, second = block[:, :rank], block[:, rank:]
-            table[peer * leaves + 2 * pair] = jnp.concatenate([first, first], axis=1)
-            table[peer * leaves + 2 * pair + 1] = jnp.concatenate([second, second], axis=1)
+            table[begin + 2 * pair] = jnp.concatenate([first, first], axis=1)
+            table[begin + 2 * pair + 1] = jnp.concatenate([second, second], axis=1)
     for copy in copies:
         copy.wait()
     own = lax.axis_index("list")
@@ -271,6 +275,10 @@
     first, second = 2 * chip_at + core, 2 * chip_at + 1 - core
     high = jnp.concatenate([down_high[first], down_high[second]], axis=1)
     low = jnp.concatenate([down_low[first], down_low[second]], axis=1)
+    if both.dtype == bf16:
+        return times_transposed(
+            jnp.concatenate([both, both], axis=1), jnp.concatenate([high, low], axis=1)
+        )
     both_high, both_low = split(both)
     return times_transposed(
         jnp.concatenate([both_high, both_low, both_high], axis=1),
@@ -278,24 +286,14 @@
     )
 
 
-def arrivals(distances, arrays, chip, core, flipped):
-    apart = [distances[core_at ^ flipped] for core_at in range(2)]
-    result = []
-    for step, both in enumerate(arrays):
-        fresh = [apart[core_at].index(apart[core_at][step]) == step for core_at in range(2)]
-        if not all(fresh):
-            both = jnp.where(core == fresh.index(True), both, jnp.zeros_like(both))
-        result.append((both, chip ^ jnp.where(core == 0, apart[0][step], apart[1][step])))
-    return result
-
-
-def down_kernel(distances, part, swapped, down_high, down_low, weights, base, out, buffer, sem):
+def down_kernel(part, swapped, down_high, down_low, weights, base, out, buffer, sem):
     place = lax.axis_index("leaf")
-    chip, core = place // 2, place % 2
+    chip, other = place // 2, 1 - place % 2
     total = part[...]
-    arrays = [swapped[step] for step in range(swapped.shape[0])]
-    for both, at in arrivals(distances, arrays, chip, core, 1):
-        total = total + down_product(down_high, down_low, both, at, 1 - core)
+    steps = swapped.shape[0]
+    for step in range(steps):
+        at = chip ^ (2 + step + steps * other)
+        total = total + down_product(down_high, down_low, swapped[step], at, other)
     high, low = split(total)
     wide = jnp.concatenate([high, low, high], axis=1)
     copies = []
@@ -342,21 +340,29 @@
         pairs = [(i, i ^ distance) for i in range(lax.axis_size(axis))]
         return lax.ppermute(array, axis, pairs)
 
+    def spread(array, first, second):
+        places = [(l, j) for l in range(leaf_count) for j in range(list_count)]
+        ends = [l * list_count + (j ^ (second if l % 2 else first)) for l, j in places]
+        return lax.ppermute(array, ("leaf", "list"), list(enumerate(ends)))
+
+    def list_exchange(array, distance):
+        return spread(array, distance, mirrored(distance, list_count))
+
     inputs = [stay(panel_charges), stay(leaf_basis), stay(leaf_transfer)]
     inputs += [stay(device_transfer[0, 0]), near_list.T, far_list.T, far_count[None]]
     count = len(inputs)
-    payload, charges, near_list, far_list, far_count = pl.pallas_call(
+    payload, charges, basis, transfer, near_list, far_list, far_count = pl.pallas_call(
         functools.partial(upward_kernel, count),
         out_shape=[
             shape(leaves // 2 + 1, rows, 2 * rank),
             like(panel_charges),
+            like(leaf_basis),
+            like(leaf_transfer),
             *[like(array) for array in inputs[4:]],
         ],
         in_specs=[anywhere] * count,
-        out_specs=[whole] * 5,
+        out_specs=[whole] * 7,
         scratch_shapes=[
-            pltpu.VMEM(leaf_basis.shape, bf16),
-            pltpu.VMEM(leaf_transfer.shape, f32),
             pltpu.VMEM((rank, rank), f32),
             pltpu.SemaphoreType.DMA((count,)),
         ],
@@ -381,7 +387,7 @@
 
     other_payload = exchange(payload, "leaf", 1)
     direct = [distance for distance in range(1, list_count) if distance & (distance - 1) == 0]
-    arrived = {distance: exchange(payload, "list", distance) for distance in direct}
+    arrived = {distance: list_exchange(payload, distance) for distance in direct}
 
     terms = pl.pallas_call(
         terms_kernel,
@@ -392,22 +398,28 @@
         name="terms",
     )(payload, other_payload)
 
-    def send_pairs(distance):
-        places = [(l, j) for l in range(leaf_count) for j in range(list_count)]
-        ends = [l * list_count + (j ^ (distance if l % 2 else direct[0])) for l, j in places]
-        return lax.ppermute(terms, ("leaf", "list"), list(enumerate(ends)))
-
     far_terms = [
-        send_pairs(distance) for distance in range(1, list_count) if distance not in direct
+        spread(terms, direct[0], distance)
+        for distance in range(1, list_count)
+        if distance not in direct
     ]
 
-    early = leaves * 14 // 16
+    weights = pl.pallas_call(
+        weights_kernel,
+        out_shape=shape(leaves, 3 * rank, panels),
+        in_specs=[whole] * 2 + [anywhere],
+        out_specs=whole,
+        compiler_params=params(4),
+        name="weights",
+    )(transfer, basis, terms)
+
+
     depth = leaf_count.bit_length() - 2
-    fetched = [tree_transfer, device_transfer[0, 0], leaf_transfer, leaf_basis, far_coupling]
-    near, tree_matrices, device_matrix, transfer, basis, coupling, couplings = pl.pallas_call(
+    fetched = [tree_transfer, device_transfer[0, 0], leaf_basis, far_coupling]
+    near, tree_matrices, device_matrix, basis, coupling, couplings = pl.pallas_call(
         functools.partial(near_kernel, leaf_count),
         out_shape=[
-            shape(early, rows, panels, dtype=f32),
+            shape(leaves, rows, panels, dtype=f32),
             *[like(array) for array in fetched],
             shape(depth, *level_coupling.shape[1:], dtype=f32),
         ],
@@ -428,7 +440,7 @@
         near_list,
         charges,
         near_blocks,
-        terms,
+        weights,
         *[stay(array) for array in fetched],
         stay(level_coupling),
     )
@@ -453,7 +465,30 @@
             out_specs=whole,
             compiler_params=params(2),
             name="forward",
-        )(arrived[base], near)
+        )(arrived[base], sums)
+
+    passed = pl.pallas_call(
+        pause_kernel,
+        out_shape=shape(8, 128, dtype=f32),
+        in_specs=[anywhere],
+        out_specs=whole,
+        compiler_params=params(1),
+        cost_estimate=pl.CostEstimate(
+            flops=64 * near_blocks.size * rows,
+            bytes_accessed=64 * near_blocks.size,
+            transcendentals=0,
+        ),
+        name="pause",
+    )(sums)
+
+    own_pair, rounded_pair = pl.pallas_call(
+        pair_kernel,
+        out_shape=[shape(rows, 2 * rank, dtype=f32), shape(rows, 2 * rank)],
+        in_specs=[whole] * 2 + [anywhere],
+        out_specs=[whole] * 2,
+        compiler_params=params(2),
+        name="pair",
+    )(sums, other_sums, passed)
 
     down_high, down_low = pl.pallas_call(
         functools.partial(tree_kernel, leaf_count),
@@ -471,44 +506,35 @@
             transcendentals=0,
         ),
         name="tree",
-    )(tree_matrices, couplings, device_matrix, sums)
-
-    own_pair = pl.pallas_call(
-        pair_kernel,
-        out_shape=shape(rows, 2 * rank, dtype=f32),
-        in_specs=[whole] * 2 + [anywhere],
-        out_specs=whole,
-        compiler_params=params(2),
-        name="pair",
-    )(sums, other_sums, down_high)
-
-    steps = chip_count // 2
-    apart = list(range(1, chip_count))
-    near_chips, far_chips = apart[: chip_count - 1 - steps], apart[chip_count - 1 - steps :]
-    distances = (near_chips + near_chips[: steps - len(near_chips)], far_chips)
+    )(tree_matrices, couplings, device_matrix, own_pair)
+
+    steps = (chip_count - 2) // 2
     received = [
         lax.ppermute(
-            own_pair, "leaf", [(i, i ^ 2 * distances[i % 2][step]) for i in range(leaf_count)]
+            rounded_pair,
+            "leaf",
+            [(i, i ^ 2 * (2 + step + steps * (i % 2))) for i in range(leaf_count)],
         )
         for step in range(steps)
     ]
-
-    near_rest = pl.pallas_call(
-        functools.partial(near_rest_kernel, early),
-        out_shape=shape(leaves - early, rows, panels, dtype=f32),
-        in_specs=[anywhere, whole, whole, anywhere],
-        out_specs=whole,
-        scratch_shapes=[pltpu.SMEM(near_list.shape, jnp.int32), pltpu.SemaphoreType.DMA],
-        compiler_params=params(4),
-        name="near_rest",
-    )(near_list, charges, near_blocks, own_pair)
+    beside = exchange(own_pair, "leaf", 2)
 
     skeletons = {distance: arrived[distance] for distance in direct}
     for distance in range(1, list_count):
         if distance not in direct:
             top = 1 << (distance.bit_length() - 1)
-            forward[distance] = exchange(forward[distance ^ top], "list", top)
+            forward[distance] = list_exchange(forward[distance ^ top], top)
             skeletons[distance] = forward[distance]
+
+    relayed = pl.pallas_call(
+        functools.partial(relay_kernel, steps),
+        out_shape=shape(steps, rows, 2 * rank),
+        in_specs=[whole] * steps + [anywhere],
+        out_specs=whole,
+        compiler_params=params(2),
+        name="relay",
+    )(*received, down_high)
+    swapped = exchange(relayed, "leaf", 1)
 
     coupled = pl.pallas_call(
         functools.partial(far_kernel, list_count - 1),
@@ -533,31 +559,12 @@
         far_count,
         *[skeletons[distance] for distance in range(1, list_count)],
         coupling,
-        near_rest,
+        relayed,
     )
 
-    relayed = pl.pallas_call(
-        functools.partial(relay_kernel, steps),
-        out_shape=shape(steps, rows, 2 * rank, dtype=f32),
-        in_specs=[whole] * steps + [anywhere],
-        out_specs=whole,
-        compiler_params=params(2),
-        name="relay",
-    )(*received, coupled)
-    swapped = exchange(relayed, "leaf", 1)
-
-    weights = pl.pallas_call(
-        weights_kernel,
-        out_shape=shape(leaves, 3 * rank, panels),
-        in_specs=[whole] * 2 + [anywhere],
-        out_specs=whole,
-        compiler_params=params(4),
-        name="weights",
-    )(transfer, basis, relayed)
-
 
     base, part = pl.pallas_call(
-        functools.partial(base_kernel, distances),
+        base_kernel,
         out_shape=[
             shape(leaves, rows, panels, dtype=f32),
             shape(rows, rank, dtype=f32),
@@ -566,10 +573,10 @@
         out_specs=[whole] * 2,
         compiler_params=params(4),
         name="base",
-    )(coupled, basis, near, near_rest, down_high, down_low, own_pair, *received)
+    )(coupled, basis, near, down_high, down_low, own_pair, beside, *received)
 
     return pl.pallas_call(
-        functools.partial(down_kernel, distances),
+        down_kernel,
         out_shape=shape(leaves, rows, panels),
         in_specs=[whole] * 6,
         out_specs=anywhere,

time: 23 us -> 21.6 us (0.939)
  waiting for transfers between devices: 1.24 us -> 0.14 us
  Pallas kernels: 11.2 us -> 10.5 us
  starting transfers between devices: 10.3 us -> 10.6 us
    ppermute x3 -> x5, starting transfers between devices: 2.63 us -> 8.34 us  [the longest x4 5.69 us: spread(): return lax.ppermute(array, ('leaf', 'list'), list(enumerate(ends)))]
    ppermute x6 -> x4, starting transfers between devices: 7.69 us -> 2.29 us  [exchange(): return lax.ppermute(array, axis, pairs)]
    pallas_call x4, Pallas kernels: 2.86 us -> 1.85 us  [the longest x1 1.4 us: on_device(): pl.pallas_call(down_kernel, out_shape=shape(leaves, rows, panels), in_spe...]
    ppermute x3 -> x5, waiting for transfers between devices: 0.69 us -> 0.01 us  [the longest x4 0.01 us: spread(): return lax.ppermute(array, ('leaf', 'list'), list(enumerate(ends)))]
    ppermute x6 -> x4, waiting for transfers between devices: 0.54 us -> 0.13 us  [exchange(): return lax.ppermute(array, axis, pairs)]
    pallas_call x1, Pallas kernels: 2.97 us -> 3.28 us  [on_device(): pl.pallas_call(functools.partial(near_kernel, leaf_count), out_shape=[sha...]
  transfers between devices with their start and end apart: 9 -> 9, of which waited for: 2 -> 1; matrix products, arithmetic and copies ran while one was open for 0% -> 0% of each run, Pallas kernels for 33% -> 32%
where the time goes in v5:
time: 21.6 us; the launch traced here: 21.5 us
  starting transfers between devices  10.6 us (49%)
  Pallas kernels  10.5 us (49%)
    ppermute x4, starting transfers between devices, spread(): return lax.ppermute(array, ('leaf', 'list'), list(enumerate(ends)))  5.69 us
    pallas_call x1, Pallas kernels, on_device(): pl.pallas_call(functools.partial(near_kernel, leaf_count), out_shape=[sha...  3.28 us
    ppermute x1, starting transfers between devices, on_device(): lax.ppermute(rounded_pair, 'leaf', [(i, i ^ 2 * (2 + step + steps * (i %...  2.65 us
    ppermute x4, starting transfers between devices, exchange(): return lax.ppermute(array, axis, pairs)  2.29 us
    pallas_call x1, Pallas kernels, on_device(): pl.pallas_call(functools.partial(upward_kernel, count), out_shape=[shape(...  2.17 us
    pallas_call x1, Pallas kernels, on_device(): pl.pallas_call(functools.partial(far_kernel, list_count - 1), out_shape=s...  1.73 us
    pallas_call x1, Pallas kernels, on_device(): pl.pallas_call(down_kernel, out_shape=shape(leaves, rows, panels), in_spe...  1.4 us
    pallas_call x1, Pallas kernels, on_device(): pl.pallas_call(functools.partial(tree_kernel, leaf_count), out_shape=[sha...  0.75 us
  transfers between devices with their start and end apart: 9, of which 1 were waited for; matrix products, arithmetic and copies ran while one was open for 0% of the time, Pallas kernels for 32%

profile of v5, /device:TPU:0, one launch (start us, length us, event | category | flops | bytes accessed | tf_op | source)
XLA Modules:
  0.0 21.5 jit_solution(15218827494436281516)
XLA Ops:
  0.0 2.2 %upward.1 = (bf16[9,64,128]{2,1,0:T(8,128)(2,1)S(1)}, bf16[16,64,256]{2,1,0:T(8,128)(2,1)S(1)}, bf16[16,64,256]{2,1,0:T(8,128)(2,1)S(1)}, f32[16,64,64]{2,1,0:T(...) custom-call(bf16[16,64,256]{2,1,0:T(8,128)(2,1)} %refs_0_.2, ...), custom_call_target="tpu_custom_call" | custom-call | tf_op jit(solution)/shard_map/upward/pallas_call | solution.py:354
  2.2 0.0 slice-start
  2.2 0.0 slice-start.1
  2.2 0.5 %collective-permute-start.2 = (bf16[9,64,128]{2,1,0:T(8,128)(2,1)S(1)}, bf16[9,64,128]{2,1,0:T(8,128)(2,1)S(1)}, u32[]{:S(2)}, u32[]{:S(2)}) collective-permute-start(bf16[9,64,128]{2,1,0:T(8,128)(2,1)S(1)} %mark.1.own.refs_0_), channel_id=1, source_target_pairs={{0,4},{4,0},{8,12},{12,8},{16,20},{20,16},{24,28},{28,24},{1,5},{5... | collective-permute-start | bytes 442376 | tf_op jit(solution)/shard_map/ppermute | solution.py:341
  2.7 2.6 %collective-permute-start = (bf16[9,64,128]{2,1,0:T(8,128)(2,1)S(1)}, bf16[9,64,128]{2,1,0:T(8,128)(2,1)S(1)}, u32[]{:S(2)}, u32[]{:S(2)}) collective-permute-start(bf16[9,64,128]{2,1,0:T(8,128)(2,1)S(1)} %mark.1.own.refs_0_), channel_id=1, source_target_pairs={{0,1},{1,0},{2,3},{3,2},{4,6},{5,7},{6,4},{7,5},{8,9},{9,8},{10,11... | collective-permute-start | bytes 442376 | tf_op jit(solution)/shard_map/ppermute | solution.py:346
  5.3 1.5 %collective-permute-start.1 = (bf16[9,64,128]{2,1,0:T(8,128)(2,1)S(1)}, bf16[9,64,128]{2,1,0:T(8,128)(2,1)S(1)}, u32[]{:S(2)}, u32[]{:S(2)}) collective-permute-start(bf16[9,64,128]{2,1,0:T(8,128)(2,1)S(1)} %mark.1.own.refs_0_), channel_id=1, source_target_pairs={{0,2},{1,3},{2,0},{3,1},{4,5},{5,4},{6,7},{7,6},{8,10},{9,11},{10,... | collective-permute-start | bytes 442376 | tf_op jit(solution)/shard_map/ppermute | solution.py:346
  6.8 0.0 collective-permute-done.2.other
  6.8 0.1 terms.1.after
  7.0 0.5 %collective-permute-start.3 = (f32[64,128]{1,0:T(8,128)S(1)}, f32[64,128]{1,0:T(8,128)S(1)}, u32[]{:S(2)}, u32[]{:S(2)}) collective-permute-start(f32[64,128]{1,0:T(8,128)S(1)} %terms.1.after), channel_id=1, source_target_pairs={{0,1},{1,0},{2,3},{3,2},{4,7},{5,6},{6,5},{7,4},{8,9},{9,8},{10,11... | collective-permute-start | bytes 98312 | tf_op jit(solution)/shard_map/ppermute | solution.py:346
  7.5 0.5 %weights.1.after = bf16[16,192,256]{2,1,0:T(8,128)(2,1)S(1)} custom-call(f32[16,64,64]{2,1,0:T(8,128)S(1)} %get-tuple-element.29.transfer, bf16[16,64,256]{2,1,0:T(8,128)(2,1)S(1)} %get-tuple-element.30.basis, f32[64,128]{1,0:T(8,128)S(1)} %terms.1.after), custom_call_target="tpu_custom_call" | custom-call | tf_op jit(solution)/shard_map/weights/pallas_call | solution.py:407
  8.0 3.3 %near.1 = (f32[16,64,256]{2,1,0:T(8,128)S(1)}, f32[8,64,64]{2,1,0:T(8,128)S(1)}, f32[64,64]{1,0:T(8,128)S(1)}, bf16[16,64,256]{2,1,0:T(8,128)(2,1)S(1)}, bf16[16...) custom-call(s32[4,16]{1,0:T(4,128)S(1)} %get-tuple-element.27.list_in, ...), custom_call_target="tpu_custom_call" | custom-call | flops 536870912 | bytes 8388608 | tf_op jit(solution)/shard_map/near/pallas_call | solution.py:419
  11.3 0.0 collective-permute-done.1.refs_2_.refs_1_
  11.3 0.1 group_sum.1.near.after.mine
  11.4 0.1 collective-permute-start.5
  11.6 1.1 %collective-permute-start.4 = (bf16[8,64,128]{2,1,0:T(8,128)(2,1)S(1)}, bf16[8,64,128]{2,1,0:T(8,128)(2,1)S(1)}, u32[]{:S(2)}, u32[]{:S(2)}) collective-permute-start(bf16[8,64,128]{2,1,0:T(8,128)(2,1)S(1)} %forward.1), channel_id=1, source_target_pairs={{0,2},{1,3},{2,0},{3,1},{4,5},{5,4},{6,7},{7,6},{8,10},{9,11},{10,... | collective-permute-start | bytes 393224 | tf_op jit(solution)/shard_map/ppermute | solution.py:346
  12.6 0.1 collective-permute-done.5.theirs
  12.7 0.1 pair.1
  12.8 2.6 %collective-permute-start.6 = (bf16[64,128]{1,0:T(8,128)(2,1)S(1)}, bf16[64,128]{1,0:T(8,128)(2,1)S(1)}, u32[]{:S(2)}, u32[]{:S(2)}) collective-permute-start(bf16[64,128]{1,0:T(8,128)(2,1)S(1)} %get-tuple-element.33), channel_id=1, source_target_pairs={{0,16},{4,28},{8,24},{12,20},{16,0},{20,12},{24,8},{28,4},{1,17},{... | collective-permute-start | bytes 49160 | tf_op jit(solution)/shard_map/ppermute | solution.py:513
  15.5 1.6 %collective-permute-start.7 = (f32[64,128]{1,0:T(8,128)S(1)}, f32[64,128]{1,0:T(8,128)S(1)}, u32[]{:S(2)}, u32[]{:S(2)}) collective-permute-start(f32[64,128]{1,0:T(8,128)S(1)} %get-tuple-element.37.sums.own), channel_id=1, source_target_pairs={{0,8},{4,12},{8,0},{12,4},{16,24},{20,28},{24,16},{28,20},{1,9},{5... | collective-permute-start | bytes 98312 | tf_op jit(solution)/shard_map/ppermute | solution.py:341
  17.1 0.8 %tree.1 = (bf16[8,64,64]{2,1,0:T(8,128)(2,1)S(1)}, bf16[8,64,64]{2,1,0:T(8,128)(2,1)S(1)}) custom-call(f32[8,64,64]{2,1,0:T(8,128)S(1)} %get-tuple-element.34.tree, f32[2,4,64,64]{3,2,1,0:T(8,128)S(1)} %get-tuple-element.35.couplings, f32[64,64]{1,0:T(8,128)S(1)} %get-tuple-element.36.matrix, f32[64,128]{1,0:T(8,128)S(1)} %get-tuple-element.37.sums.own), custom_call_target="tpu_custom_call" | custom-call | flops 17179869184 | bytes 268435456 | tf_op jit(solution)/shard_map/tree/pallas_call | solution.py:493
  17.8 0.1 collective-permute-start.8
  17.9 1.7 %far.1.coupled = f32[8,64,128]{2,1,0:T(8,128)S(1)} custom-call(s32[8,16]{1,0:T(8,128)S(1)} %get-tuple-element.24.list_in, s32[1,16]{1,0:T(1,128)S(1)} %get-tuple-element.25.count_in, bf16[9,64,128]{2,1,0:T(8,128)(2,1)S(1)} %collective-permute-done.refs_1_.payload.refs_0_, bf16[9,64,128]{2,1,0:T(8,128)(2,1)S(1)} %collective-permute-done.1.refs_2_.refs_1_, ...), custom_call_target="tpu_custom_call" | custom-call | flops 268435456 | bytes 2097152 | tf_op jit(solution)/shard_map/far/pallas_call | solution.py:539
  19.7 0.4 %base.1 = (f32[16,64,256]{2,1,0:T(8,128)S(1)}, f32[64,64]{1,0:T(8,128)S(1)}) custom-call(f32[8,64,128]{2,1,0:T(8,128)S(1)} %far.1.coupled, bf16[16,64,256]{2,1,0:T(8,128)(2,1)S(1)} %get-tuple-element.39.basis, f32[16,64,256]{2,1,0:T(8,128)S(1)} %get-tuple-element.31.refs_4_.near, bf16[8,64,64]{2,1,0:T(8,128)(2,1)S(1)} %get-tuple-element.38.refs_1_.down_high, ...), custom_call_target="tpu_custom_call" | custom-call | tf_op jit(solution)/shard_map/base/pallas_call | solution.py:566
  20.0 1.4 %down.1 = bf16[16,64,256]{2,1,0:T(8,128)(2,1)} custom-call(f32[64,64]{1,0:T(8,128)S(1)} %get-tuple-element.41.part, bf16[1,64,128]{2,1,0:T(8,128)(2,1)S(1)} %collective-permute-done.8.swapped, bf16[8,64,64]{2,1,0:T(8,128)(2,1)S(1)} %get-tuple-element.38.refs_1_.down_high, bf16[8,64,64]{2,1,0:T(8,128)(2,1)S(1)} %get-tuple-element.40.down_low, ...), custom_call_target="tpu_custom_call" | custom-call | tf_op jit(solution)/shard_map/down/pallas_call | solution.py:578
  (13 shorter events, 0.0 us)
Async XLA Ops:
  2.2 5.8 %slice-start = ((s8[8388608]{0:T(1024)(128)(4,1)}), s8[4194304]{0:T(1024)(128)(4,1)S(1)}, s32[]{:S(2)}) async-start(s8[8388608]{0:T(1024)(128)(4,1)} %bitcast.4), calls=%async_computation | async-start | bytes 8388608
  2.2 5.8 %slice-start.1 = ((s8[8388608]{0:T(1024)(128)(4,1)}), s8[4194304]{0:T(1024)(128)(4,1)S(1)}, s32[]{:S(2)}) async-start(s8[8388608]{0:T(1024)(128)(4,1)} %bitcast.4), calls=%async_computation.1 | async-start | bytes 8388608
  2.2 4.6 %collective-permute-start.2 = (bf16[9,64,128]{2,1,0:T(8,128)(2,1)S(1)}, bf16[9,64,128]{2,1,0:T(8,128)(2,1)S(1)}, u32[]{:S(2)}, u32[]{:S(2)}) collective-permute-start(bf16[9,64,128]{2,1,0:T(8,128)(2,1)S(1)} %mark.1.own.refs_0_), channel_id=1, source_target_pairs={{0,4},{4,0},{8,12},{12,8},{16,20},{20,16},{24,28},{28,24},{1,5},{5... | collective-permute-start | bytes 442376 | tf_op jit(solution)/shard_map/ppermute | solution.py:341
  2.7 8.6 %collective-permute-start = (bf16[9,64,128]{2,1,0:T(8,128)(2,1)S(1)}, bf16[9,64,128]{2,1,0:T(8,128)(2,1)S(1)}, u32[]{:S(2)}, u32[]{:S(2)}) collective-permute-start(bf16[9,64,128]{2,1,0:T(8,128)(2,1)S(1)} %mark.1.own.refs_0_), channel_id=1, source_target_pairs={{0,1},{1,0},{2,3},{3,2},{4,6},{5,7},{6,4},{7,5},{8,9},{9,8},{10,11... | collective-permute-start | bytes 442376 | tf_op jit(solution)/shard_map/ppermute | solution.py:346
  5.3 6.0 %collective-permute-start.1 = (bf16[9,64,128]{2,1,0:T(8,128)(2,1)S(1)}, bf16[9,64,128]{2,1,0:T(8,128)(2,1)S(1)}, u32[]{:S(2)}, u32[]{:S(2)}) collective-permute-start(bf16[9,64,128]{2,1,0:T(8,128)(2,1)S(1)} %mark.1.own.refs_0_), channel_id=1, source_target_pairs={{0,2},{1,3},{2,0},{3,1},{4,5},{5,4},{6,7},{7,6},{8,10},{9,11},{10,... | collective-permute-start | bytes 442376 | tf_op jit(solution)/shard_map/ppermute | solution.py:346
  7.0 4.4 %collective-permute-start.3 = (f32[64,128]{1,0:T(8,128)S(1)}, f32[64,128]{1,0:T(8,128)S(1)}, u32[]{:S(2)}, u32[]{:S(2)}) collective-permute-start(f32[64,128]{1,0:T(8,128)S(1)} %terms.1.after), channel_id=1, source_target_pairs={{0,1},{1,0},{2,3},{3,2},{4,7},{5,6},{6,5},{7,4},{8,9},{9,8},{10,11... | collective-permute-start | bytes 98312 | tf_op jit(solution)/shard_map/ppermute | solution.py:346
  11.4 1.3 %collective-permute-start.5 = (f32[2,64,128]{2,1,0:T(8,128)S(1)}, f32[2,64,128]{2,1,0:T(8,128)S(1)}, u32[]{:S(2)}, u32[]{:S(2)}) collective-permute-start(f32[2,64,128]{2,1,0:T(8,128)S(1)} %group_sum.1.near.after.mine), channel_id=1, source_target_pairs={{0,4},{4,0},{8,12},{12,8},{16,20},{20,16},{24,28},{28,24},{1,5},{5... | collective-permute-start | bytes 196616 | tf_op jit(solution)/shard_map/ppermute | solution.py:341
  11.6 6.4 %collective-permute-start.4 = (bf16[8,64,128]{2,1,0:T(8,128)(2,1)S(1)}, bf16[8,64,128]{2,1,0:T(8,128)(2,1)S(1)}, u32[]{:S(2)}, u32[]{:S(2)}) collective-permute-start(bf16[8,64,128]{2,1,0:T(8,128)(2,1)S(1)} %forward.1), channel_id=1, source_target_pairs={{0,2},{1,3},{2,0},{3,1},{4,5},{5,4},{6,7},{7,6},{8,10},{9,11},{10,... | collective-permute-start | bytes 393224 | tf_op jit(solution)/shard_map/ppermute | solution.py:346
  12.8 5.0 %collective-permute-start.6 = (bf16[64,128]{1,0:T(8,128)(2,1)S(1)}, bf16[64,128]{1,0:T(8,128)(2,1)S(1)}, u32[]{:S(2)}, u32[]{:S(2)}) collective-permute-start(bf16[64,128]{1,0:T(8,128)(2,1)S(1)} %get-tuple-element.33), channel_id=1, source_target_pairs={{0,16},{4,28},{8,24},{12,20},{16,0},{20,12},{24,8},{28,4},{1,17},{... | collective-permute-start | bytes 49160 | tf_op jit(solution)/shard_map/ppermute | solution.py:513
  15.5 4.2 %collective-permute-start.7 = (f32[64,128]{1,0:T(8,128)S(1)}, f32[64,128]{1,0:T(8,128)S(1)}, u32[]{:S(2)}, u32[]{:S(2)}) collective-permute-start(f32[64,128]{1,0:T(8,128)S(1)} %get-tuple-element.37.sums.own), channel_id=1, source_target_pairs={{0,8},{4,12},{8,0},{12,4},{16,24},{20,28},{24,16},{28,20},{1,9},{5... | collective-permute-start | bytes 98312 | tf_op jit(solution)/shard_map/ppermute | solution.py:341
  17.8 2.2 %collective-permute-start.8 = (bf16[1,64,128]{2,1,0:T(8,128)(2,1)S(1)}, bf16[1,64,128]{2,1,0:T(8,128)(2,1)S(1)}, u32[]{:S(2)}, u32[]{:S(2)}) collective-permute-start(bf16[1,64,128]{2,1,0:T(8,128)(2,1)S(1)} %relay.1.refs_4_), channel_id=1, source_target_pairs={{0,4},{4,0},{8,12},{12,8},{16,20},{20,16},{24,28},{28,24},{1,5},{5... | collective-permute-start | bytes 49160 | tf_op jit(solution)/shard_map/ppermute | solution.py:341

commit v6 on v5

--- a/solution.py
+++ b/solution.py
@@ -55,7 +55,7 @@
     ]
     for copy in copies:
         copy.start()
-    for copy in copies:
+    for copy in copies[:2]:
         copy.wait()
     pair_count = charges.shape[0] // 2
     rank = basis.shape[1]
@@ -67,6 +67,8 @@
         ]
         skeletons.append(jnp.concatenate(halves, axis=1))
         payload[pair] = skeletons[pair]
+    for copy in copies[2:]:
+        copy.wait()
     high, low = split(transfer[...].reshape(2 * pair_count * rank, rank))
     row = jnp.concatenate(skeletons, axis=1)
     node = times(row, high) + times(row, low)
@@ -90,10 +92,10 @@
     return total
 
 
-def near_kernel(leaf_count, list_in, charges, blocks, after, *refs):
+def near_kernel(leaf_count, list_in, charges, blocks, after, transfer, basis_ready, *refs):
     sources, couplings_in = refs[:4], refs[4]
     near, targets, couplings = refs[5], refs[6:10], refs[10]
-    near_list, sem = refs[11:]
+    weights, near_list, sem = refs[11:]
     listed = pltpu.make_async_copy(list_in, near_list, sem.at[0])
     listed.start()
     place = lax.axis_index("leaf")
@@ -107,6 +109,7 @@
     ]
     for copy in copies:
         copy.start()
+    weigh(transfer, basis_ready, weights)
     listed.wait()
     for leaf in range(near.shape[0]):
         near[leaf] = near_leaf(near_list, charges, blocks, leaf, leaf)
@@ -122,7 +125,8 @@
 
 def terms_kernel(own, other, terms):
     last = own.shape[0] - 1
-    terms[...] = jnp.concatenate([joined(own[last]), joined(other[last])], axis=1)
+    both = jnp.concatenate([joined(own[last]), joined(other[last])], axis=1)
+    terms[...] = both.astype(bf16)
 
 
 def pair_kernel(mine, theirs, *refs):
@@ -188,7 +192,7 @@
         down_low[node] = low
 
 
-def weights_kernel(transfer, basis, after, weights):
+def weigh(transfer, basis, weights):
     for leaf in range(transfer.shape[0]):
         high, low = split(transfer[leaf])
         full = times(high.T, basis[leaf]) + times(low.T, basis[leaf])
@@ -223,7 +227,7 @@
 
 def far_kernel(peer_count, list_in, count_in, *refs):
     peers = refs[:peer_count]
-    coupling, after, coupled, table, far_list, far_count, sem = refs[peer_count:]
+    coupling, after, coupled, table, rights, far_list, far_count, sem = refs[peer_count:]
     copies = [
         pltpu.make_async_copy(list_in, far_list, sem.at[0]),
         pltpu.make_async_copy(count_in, far_count, sem.at[1]),
@@ -232,21 +236,25 @@
         copy.start()
     leaves, slots, rank = coupling.shape[0], coupling.shape[1], coupling.shape[2]
     rows = table.shape[1]
-    pair_count = leaves // 2
     empty = peer_count * leaves
     table[empty] = jnp.zeros(table.shape[1:], bf16)
     odd = lax.axis_index("leaf") % 2 == 1
     for peer in range(peer_count):
         begin = jnp.where(odd, mirrored(peer + 1, peer_count + 1) - 1, peer) * leaves
-        for pair in range(pair_count):
+        for pair in range(leaves // 2):
             block = peers[peer][pair]
             first, second = block[:, :rank], block[:, rank:]
             table[begin + 2 * pair] = jnp.concatenate([first, first], axis=1)
             table[begin + 2 * pair + 1] = jnp.concatenate([second, second], axis=1)
+    for leaf in range(leaves // 2):
+        for slot in range(0, slots, 2):
+            rights[leaf, :, rank * slot : rank * (slot + 2)] = jnp.concatenate(
+                [coupling[leaf, slot], coupling[leaf, slot + 1]], axis=1
+            )
+    own = lax.axis_index("list")
+    lower = lax.broadcasted_iota(jnp.int32, (rows, 2 * rank), 1) < rank
     for copy in copies:
         copy.wait()
-    own = lax.axis_index("list")
-    lower = lax.broadcasted_iota(jnp.int32, (rows, 2 * rank), 1) < rank
 
     def entry(leaf, slot):
         source = far_list[slot, leaf]
@@ -255,19 +263,23 @@
         return jnp.where(slot < far_count[0, leaf], place, empty)
 
     def one(leaf):
-        lefts, rights = [], []
-        for slot in range(0, slots, 2):
-            lefts.append(
-                jnp.where(lower, table[entry(leaf, slot)], table[entry(leaf, slot + 1)])
+        lefts = [
+            jnp.where(lower, table[entry(leaf, slot)], table[entry(leaf, slot + 1)])
+            for slot in range(0, slots, 2)
+        ]
+        if leaf < leaves // 2:
+            right = rights[leaf]
+        else:
+            right = jnp.concatenate(
+                [
+                    jnp.concatenate([coupling[leaf, slot], coupling[leaf, slot + 1]], axis=1)
+                    for slot in range(0, slots, 2)
+                ],
+                axis=1,
             )
-            rights.append(
-                jnp.concatenate([coupling[leaf, slot], coupling[leaf, slot + 1]], axis=1)
-            )
-        return times_transposed(
-            jnp.concatenate(lefts, axis=1), jnp.concatenate(rights, axis=1)
-        )
-
-    for pair in range(pair_count):
+        return times_transposed(jnp.concatenate(lefts, axis=1), right)
+
+    for pair in range(leaves // 2):
         coupled[pair] = jnp.concatenate([one(2 * pair), one(2 * pair + 1)], axis=1)
 
 
@@ -391,7 +403,7 @@
 
     terms = pl.pallas_call(
         terms_kernel,
-        out_shape=shape(rows, 2 * rank, dtype=f32),
+        out_shape=shape(rows, 2 * rank),
         in_specs=[whole] * 2,
         out_specs=whole,
         compiler_params=params(2),
@@ -404,27 +416,18 @@
         if distance not in direct
     ]
 
-    weights = pl.pallas_call(
-        weights_kernel,
-        out_shape=shape(leaves, 3 * rank, panels),
-        in_specs=[whole] * 2 + [anywhere],
-        out_specs=whole,
-        compiler_params=params(4),
-        name="weights",
-    )(transfer, basis, terms)
-
-
     depth = leaf_count.bit_length() - 2
     fetched = [tree_transfer, device_transfer[0, 0], leaf_basis, far_coupling]
-    near, tree_matrices, device_matrix, basis, coupling, couplings = pl.pallas_call(
+    near, tree_matrices, device_matrix, basis_later, coupling, couplings, weights = pl.pallas_call(
         functools.partial(near_kernel, leaf_count),
         out_shape=[
             shape(leaves, rows, panels, dtype=f32),
             *[like(array) for array in fetched],
             shape(depth, *level_coupling.shape[1:], dtype=f32),
-        ],
-        in_specs=[anywhere, whole, whole] + [anywhere] * (2 + len(fetched)),
-        out_specs=[whole] * (2 + len(fetched)),
+            shape(leaves, 3 * rank, panels),
+        ],
+        in_specs=[anywhere, whole, whole, anywhere, whole, whole] + [anywhere] * (1 + len(fetched)),
+        out_specs=[whole] * (3 + len(fetched)),
         scratch_shapes=[
             pltpu.SMEM(near_list.shape, jnp.int32),
             pltpu.SemaphoreType.DMA((1 + len(fetched) + depth,)),
@@ -440,7 +443,9 @@
         near_list,
         charges,
         near_blocks,
-        weights,
+        terms,
+        transfer,
+        basis,
         *[stay(array) for array in fetched],
         stay(level_coupling),
     )
@@ -543,6 +548,7 @@
         out_specs=whole,
         scratch_shapes=[
             pltpu.VMEM(((list_count - 1) * leaves + 1, rows, 2 * rank), bf16),
+            pltpu.VMEM((leaves, rank, far_list.shape[0] * rank), bf16),
             pltpu.SMEM(far_list.shape, jnp.int32),
             pltpu.SMEM(far_count.shape, jnp.int32),
             pltpu.SemaphoreType.DMA((2,)),
@@ -573,7 +579,7 @@
         out_specs=[whole] * 2,
         compiler_params=params(4),
         name="base",
-    )(coupled, basis, near, down_high, down_low, own_pair, beside, *received)
+    )(coupled, basis_later, near, down_high, down_low, own_pair, beside, *received)
 
     return pl.pallas_call(
         down_kernel,

time: 21.6 us -> 21.3 us (0.986)
  Pallas kernels: 10.5 us -> 10.2 us
    pallas_call x2 -> x1, Pallas kernels: 0.62 us -> 0.14 us  [on_device(): pl.pallas_call(terms_kernel, out_shape=shape(rows, 2 * rank), in_specs=[w...]
    pallas_call x1, Pallas kernels: 3.28 us -> 3.59 us  [on_device(): pl.pallas_call(functools.partial(near_kernel, leaf_count), out_shape=[sha...]
  transfers between devices with their start and end apart: 9 -> 9, of which waited for: 1 -> 0; matrix products, arithmetic and copies ran while one was open for 0% -> 0% of each run, Pallas kernels for 32% -> 31%
where the time goes in v6:
time: 21.3 us; the launch traced here: 21.1 us
  starting transfers between devices  10.7 us (50%)
  Pallas kernels  10.2 us (48%)
    ppermute x4, starting transfers between devices, spread(): return lax.ppermute(array, ('leaf', 'list'), list(enumerate(ends)))  5.76 us
    pallas_call x1, Pallas kernels, on_device(): pl.pallas_call(functools.partial(near_kernel, leaf_count), out_shape=[sha...  3.59 us
    ppermute x1, starting transfers between devices, on_device(): lax.ppermute(rounded_pair, 'leaf', [(i, i ^ 2 * (2 + step + steps * (i %...  2.65 us
    ppermute x4, starting transfers between devices, exchange(): return lax.ppermute(array, axis, pairs)  2.29 us
    pallas_call x1, Pallas kernels, on_device(): pl.pallas_call(functools.partial(upward_kernel, count), out_shape=[shape(...  2.09 us
    pallas_call x1, Pallas kernels, on_device(): pl.pallas_call(functools.partial(far_kernel, list_count - 1), out_shape=s...  1.69 us
    pallas_call x1, Pallas kernels, on_device(): pl.pallas_call(down_kernel, out_shape=shape(leaves, rows, panels), in_spe...  1.41 us
    pallas_call x1, Pallas kernels, on_device(): pl.pallas_call(functools.partial(tree_kernel, leaf_count), out_shape=[sha...  0.75 us
  transfers between devices with their start and end apart: 9, of which 0 were waited for; matrix products, arithmetic and copies ran while one was open for 0% of the time, Pallas kernels for 31%

profile of v6, /device:TPU:0, one launch (start us, length us, event | category | flops | bytes accessed | tf_op | source)
XLA Modules:
  0.0 21.1 jit_solution(11394909718178455702)
XLA Ops:
  0.0 2.1 %upward.1 = (bf16[9,64,128]{2,1,0:T(8,128)(2,1)S(1)}, bf16[16,64,256]{2,1,0:T(8,128)(2,1)S(1)}, bf16[16,64,256]{2,1,0:T(8,128)(2,1)S(1)}, f32[16,64,64]{2,1,0:T(...) custom-call(bf16[16,64,256]{2,1,0:T(8,128)(2,1)} %refs_0_.2, ...), custom_call_target="tpu_custom_call" | custom-call | tf_op jit(solution)/shard_map/upward/pallas_call | solution.py:366
  2.1 0.0 slice-start
  2.1 0.0 slice-start.1
  2.1 0.5 %collective-permute-start.2 = (bf16[9,64,128]{2,1,0:T(8,128)(2,1)S(1)}, bf16[9,64,128]{2,1,0:T(8,128)(2,1)S(1)}, u32[]{:S(2)}, u32[]{:S(2)}) collective-permute-start(bf16[9,64,128]{2,1,0:T(8,128)(2,1)S(1)} %mark.1.own.refs_0_), channel_id=1, source_target_pairs={{0,4},{4,0},{8,12},{12,8},{16,20},{20,16},{24,28},{28,24},{1,5},{5... | collective-permute-start | bytes 442376 | tf_op jit(solution)/shard_map/ppermute | solution.py:353
  2.6 2.6 %collective-permute-start = (bf16[9,64,128]{2,1,0:T(8,128)(2,1)S(1)}, bf16[9,64,128]{2,1,0:T(8,128)(2,1)S(1)}, u32[]{:S(2)}, u32[]{:S(2)}) collective-permute-start(bf16[9,64,128]{2,1,0:T(8,128)(2,1)S(1)} %mark.1.own.refs_0_), channel_id=1, source_target_pairs={{0,1},{1,0},{2,3},{3,2},{4,6},{5,7},{6,4},{7,5},{8,9},{9,8},{10,11... | collective-permute-start | bytes 442376 | tf_op jit(solution)/shard_map/ppermute | solution.py:358
  5.2 1.5 %collective-permute-start.1 = (bf16[9,64,128]{2,1,0:T(8,128)(2,1)S(1)}, bf16[9,64,128]{2,1,0:T(8,128)(2,1)S(1)}, u32[]{:S(2)}, u32[]{:S(2)}) collective-permute-start(bf16[9,64,128]{2,1,0:T(8,128)(2,1)S(1)} %mark.1.own.refs_0_), channel_id=1, source_target_pairs={{0,2},{1,3},{2,0},{3,1},{4,5},{5,4},{6,7},{7,6},{8,10},{9,11},{10,... | collective-permute-start | bytes 442376 | tf_op jit(solution)/shard_map/ppermute | solution.py:358
  6.7 0.1 terms.1.after
  6.9 0.5 %collective-permute-start.3 = (bf16[64,128]{1,0:T(8,128)(2,1)S(1)}, bf16[64,128]{1,0:T(8,128)(2,1)S(1)}, u32[]{:S(2)}, u32[]{:S(2)}) collective-permute-start(bf16[64,128]{1,0:T(8,128)(2,1)S(1)} %terms.1.after), channel_id=1, source_target_pairs={{0,1},{1,0},{2,3},{3,2},{4,7},{5,6},{6,5},{7,4},{8,9},{9,8},{10,11... | collective-permute-start | bytes 49160 | tf_op jit(solution)/shard_map/ppermute | solution.py:358
  7.4 3.6 %near.1 = (f32[16,64,256]{2,1,0:T(8,128)S(1)}, f32[8,64,64]{2,1,0:T(8,128)S(1)}, f32[64,64]{1,0:T(8,128)S(1)}, bf16[16,64,256]{2,1,0:T(8,128)(2,1)S(1)}, bf16[16...) custom-call(s32[4,16]{1,0:T(4,128)S(1)} %get-tuple-element.28.list_in, ...), custom_call_target="tpu_custom_call" | custom-call | flops 536870912 | bytes 8388608 | tf_op jit(solution)/shard_map/near/pallas_call | solution.py:421
  11.0 0.0 collective-permute-done.1.refs_2_.refs_1_
  11.0 0.0 collective-permute-done.3.refs_3_
  11.1 0.1 group_sum.1.near.after.mine
  11.1 0.1 collective-permute-start.5
  11.3 1.1 %collective-permute-start.4 = (bf16[8,64,128]{2,1,0:T(8,128)(2,1)S(1)}, bf16[8,64,128]{2,1,0:T(8,128)(2,1)S(1)}, u32[]{:S(2)}, u32[]{:S(2)}) collective-permute-start(bf16[8,64,128]{2,1,0:T(8,128)(2,1)S(1)} %forward.1), channel_id=1, source_target_pairs={{0,2},{1,3},{2,0},{3,1},{4,5},{5,4},{6,7},{7,6},{8,10},{9,11},{10,... | collective-permute-start | bytes 393224 | tf_op jit(solution)/shard_map/ppermute | solution.py:358
  12.4 0.0 collective-permute-done.5.theirs
  12.5 0.1 pair.1
  12.6 2.6 %collective-permute-start.6 = (bf16[64,128]{1,0:T(8,128)(2,1)S(1)}, bf16[64,128]{1,0:T(8,128)(2,1)S(1)}, u32[]{:S(2)}, u32[]{:S(2)}) collective-permute-start(bf16[64,128]{1,0:T(8,128)(2,1)S(1)} %get-tuple-element.34), channel_id=1, source_target_pairs={{0,16},{4,28},{8,24},{12,20},{16,0},{20,12},{24,8},{28,4},{1,17},{... | collective-permute-start | bytes 49160 | tf_op jit(solution)/shard_map/ppermute | solution.py:518
  15.2 1.6 %collective-permute-start.7 = (f32[64,128]{1,0:T(8,128)S(1)}, f32[64,128]{1,0:T(8,128)S(1)}, u32[]{:S(2)}, u32[]{:S(2)}) collective-permute-start(f32[64,128]{1,0:T(8,128)S(1)} %get-tuple-element.38.sums.own), channel_id=1, source_target_pairs={{0,8},{4,12},{8,0},{12,4},{16,24},{20,28},{24,16},{28,20},{1,9},{5... | collective-permute-start | bytes 98312 | tf_op jit(solution)/shard_map/ppermute | solution.py:353
  16.8 0.8 %tree.1 = (bf16[8,64,64]{2,1,0:T(8,128)(2,1)S(1)}, bf16[8,64,64]{2,1,0:T(8,128)(2,1)S(1)}) custom-call(f32[8,64,64]{2,1,0:T(8,128)S(1)} %get-tuple-element.35.tree, f32[2,4,64,64]{3,2,1,0:T(8,128)S(1)} %get-tuple-element.36.couplings, f32[64,64]{1,0:T(8,128)S(1)} %get-tuple-element.37.matrix, f32[64,128]{1,0:T(8,128)S(1)} %get-tuple-element.38.sums.own), custom_call_target="tpu_custom_call" | custom-call | flops 17179869184 | bytes 268435456 | tf_op jit(solution)/shard_map/tree/pallas_call | solution.py:498
  17.5 0.0 collective-permute-done.6.refs_0_
  17.6 0.1 collective-permute-start.8
  17.7 1.7 %far.1.coupled = f32[8,64,128]{2,1,0:T(8,128)S(1)} custom-call(s32[8,16]{1,0:T(8,128)S(1)} %get-tuple-element.25.list_in, s32[1,16]{1,0:T(1,128)S(1)} %get-tuple-element.26.count_in, bf16[9,64,128]{2,1,0:T(8,128)(2,1)S(1)} %collective-permute-done.refs_1_.payload.refs_0_, bf16[9,64,128]{2,1,0:T(8,128)(2,1)S(1)} %collective-permute-done.1.refs_2_.refs_1_, ...), custom_call_target="tpu_custom_call" | custom-call | flops 268435456 | bytes 2097152 | tf_op jit(solution)/shard_map/far/pallas_call | solution.py:544
  19.4 0.4 %base.1 = (f32[16,64,256]{2,1,0:T(8,128)S(1)}, f32[64,64]{1,0:T(8,128)S(1)}) custom-call(f32[8,64,128]{2,1,0:T(8,128)S(1)} %far.1.coupled, bf16[16,64,256]{2,1,0:T(8,128)(2,1)S(1)} %get-tuple-element.40.basis, f32[16,64,256]{2,1,0:T(8,128)S(1)} %get-tuple-element.32.refs_4_.near, bf16[8,64,64]{2,1,0:T(8,128)(2,1)S(1)} %get-tuple-element.39.refs_1_.down_high, ...), custom_call_target="tpu_custom_call" | custom-call | tf_op jit(solution)/shard_map/base/pallas_call | solution.py:572
  19.7 1.4 %down.1 = bf16[16,64,256]{2,1,0:T(8,128)(2,1)} custom-call(f32[64,64]{1,0:T(8,128)S(1)} %get-tuple-element.42.part, bf16[1,64,128]{2,1,0:T(8,128)(2,1)S(1)} %collective-permute-done.8.swapped, bf16[8,64,64]{2,1,0:T(8,128)(2,1)S(1)} %get-tuple-element.39.refs_1_.down_high, bf16[8,64,64]{2,1,0:T(8,128)(2,1)S(1)} %get-tuple-element.41.down_low, ...), custom_call_target="tpu_custom_call" | custom-call | tf_op jit(solution)/shard_map/down/pallas_call | solution.py:584
  (12 shorter events, 0.0 us)
Async XLA Ops:
  2.1 5.3 %slice-start = ((s8[8388608]{0:T(1024)(128)(4,1)}), s8[4194304]{0:T(1024)(128)(4,1)S(1)}, s32[]{:S(2)}) async-start(s8[8388608]{0:T(1024)(128)(4,1)} %bitcast.4), calls=%async_computation | async-start | bytes 8388608
  2.1 5.3 %slice-start.1 = ((s8[8388608]{0:T(1024)(128)(4,1)}), s8[4194304]{0:T(1024)(128)(4,1)S(1)}, s32[]{:S(2)}) async-start(s8[8388608]{0:T(1024)(128)(4,1)} %bitcast.4), calls=%async_computation.1 | async-start | bytes 8388608
  2.1 4.6 %collective-permute-start.2 = (bf16[9,64,128]{2,1,0:T(8,128)(2,1)S(1)}, bf16[9,64,128]{2,1,0:T(8,128)(2,1)S(1)}, u32[]{:S(2)}, u32[]{:S(2)}) collective-permute-start(bf16[9,64,128]{2,1,0:T(8,128)(2,1)S(1)} %mark.1.own.refs_0_), channel_id=1, source_target_pairs={{0,4},{4,0},{8,12},{12,8},{16,20},{20,16},{24,28},{28,24},{1,5},{5... | collective-permute-start | bytes 442376 | tf_op jit(solution)/shard_map/ppermute | solution.py:353
  2.6 8.4 %collective-permute-start = (bf16[9,64,128]{2,1,0:T(8,128)(2,1)S(1)}, bf16[9,64,128]{2,1,0:T(8,128)(2,1)S(1)}, u32[]{:S(2)}, u32[]{:S(2)}) collective-permute-start(bf16[9,64,128]{2,1,0:T(8,128)(2,1)S(1)} %mark.1.own.refs_0_), channel_id=1, source_target_pairs={{0,1},{1,0},{2,3},{3,2},{4,6},{5,7},{6,4},{7,5},{8,9},{9,8},{10,11... | collective-permute-start | bytes 442376 | tf_op jit(solution)/shard_map/ppermute | solution.py:358
  5.2 5.8 %collective-permute-start.1 = (bf16[9,64,128]{2,1,0:T(8,128)(2,1)S(1)}, bf16[9,64,128]{2,1,0:T(8,128)(2,1)S(1)}, u32[]{:S(2)}, u32[]{:S(2)}) collective-permute-start(bf16[9,64,128]{2,1,0:T(8,128)(2,1)S(1)} %mark.1.own.refs_0_), channel_id=1, source_target_pairs={{0,2},{1,3},{2,0},{3,1},{4,5},{5,4},{6,7},{7,6},{8,10},{9,11},{10,... | collective-permute-start | bytes 442376 | tf_op jit(solution)/shard_map/ppermute | solution.py:358
  6.9 4.2 %collective-permute-start.3 = (bf16[64,128]{1,0:T(8,128)(2,1)S(1)}, bf16[64,128]{1,0:T(8,128)(2,1)S(1)}, u32[]{:S(2)}, u32[]{:S(2)}) collective-permute-start(bf16[64,128]{1,0:T(8,128)(2,1)S(1)} %terms.1.after), channel_id=1, source_target_pairs={{0,1},{1,0},{2,3},{3,2},{4,7},{5,6},{6,5},{7,4},{8,9},{9,8},{10,11... | collective-permute-start | bytes 49160 | tf_op jit(solution)/shard_map/ppermute | solution.py:358
  11.1 1.3 %collective-permute-start.5 = (f32[2,64,128]{2,1,0:T(8,128)S(1)}, f32[2,64,128]{2,1,0:T(8,128)S(1)}, u32[]{:S(2)}, u32[]{:S(2)}) collective-permute-start(f32[2,64,128]{2,1,0:T(8,128)S(1)} %group_sum.1.near.after.mine), channel_id=1, source_target_pairs={{0,4},{4,0},{8,12},{12,8},{16,20},{20,16},{24,28},{28,24},{1,5},{5... | collective-permute-start | bytes 196616 | tf_op jit(solution)/shard_map/ppermute | solution.py:353
  11.3 6.4 %collective-permute-start.4 = (bf16[8,64,128]{2,1,0:T(8,128)(2,1)S(1)}, bf16[8,64,128]{2,1,0:T(8,128)(2,1)S(1)}, u32[]{:S(2)}, u32[]{:S(2)}) collective-permute-start(bf16[8,64,128]{2,1,0:T(8,128)(2,1)S(1)} %forward.1), channel_id=1, source_target_pairs={{0,2},{1,3},{2,0},{3,1},{4,5},{5,4},{6,7},{7,6},{8,10},{9,11},{10,... | collective-permute-start | bytes 393224 | tf_op jit(solution)/shard_map/ppermute | solution.py:358
  12.6 5.0 %collective-permute-start.6 = (bf16[64,128]{1,0:T(8,128)(2,1)S(1)}, bf16[64,128]{1,0:T(8,128)(2,1)S(1)}, u32[]{:S(2)}, u32[]{:S(2)}) collective-permute-start(bf16[64,128]{1,0:T(8,128)(2,1)S(1)} %get-tuple-element.34), channel_id=1, source_target_pairs={{0,16},{4,28},{8,24},{12,20},{16,0},{20,12},{24,8},{28,4},{1,17},{... | collective-permute-start | bytes 49160 | tf_op jit(solution)/shard_map/ppermute | solution.py:518
  15.2 4.2 %collective-permute-start.7 = (f32[64,128]{1,0:T(8,128)S(1)}, f32[64,128]{1,0:T(8,128)S(1)}, u32[]{:S(2)}, u32[]{:S(2)}) collective-permute-start(f32[64,128]{1,0:T(8,128)S(1)} %get-tuple-element.38.sums.own), channel_id=1, source_target_pairs={{0,8},{4,12},{8,0},{12,4},{16,24},{20,28},{24,16},{28,20},{1,9},{5... | collective-permute-start | bytes 98312 | tf_op jit(solution)/shard_map/ppermute | solution.py:353
  17.6 2.2 %collective-permute-start.8 = (bf16[1,64,128]{2,1,0:T(8,128)(2,1)S(1)}, bf16[1,64,128]{2,1,0:T(8,128)(2,1)S(1)}, u32[]{:S(2)}, u32[]{:S(2)}) collective-permute-start(bf16[1,64,128]{2,1,0:T(8,128)(2,1)S(1)} %relay.1.refs_4_), channel_id=1, source_target_pairs={{0,4},{4,0},{8,12},{12,8},{16,20},{20,16},{24,28},{28,24},{1,5},{5... | collective-permute-start | bytes 49160 | tf_op jit(solution)/shard_map/ppermute | solution.py:353

commit v7 on v6

--- a/solution.py
+++ b/solution.py
@@ -196,11 +196,10 @@
     for leaf in range(transfer.shape[0]):
         high, low = split(transfer[leaf])
         full = times(high.T, basis[leaf]) + times(low.T, basis[leaf])
-        full_high, full_low = split(full)
-        weights[leaf] = jnp.concatenate([full_high, full_high, full_low], axis=0)
-
-
-def base_kernel(coupled, basis, near, down_high, down_low, own, beside, *refs):
+        weights[leaf] = full.astype(bf16)
+
+
+def base_kernel(coupled, basis, near, down_high, down_low, own, *refs):
     pairs, base, part = refs[:-2], refs[-2], refs[-1]
     rank = basis.shape[1]
     for pair in range(coupled.shape[0]):
@@ -212,7 +211,6 @@
     place = lax.axis_index("leaf")
     chip, core = place // 2, place % 2
     total = down_product(down_high, down_low, own[...], chip, core)
-    total = total + down_product(down_high, down_low, beside[...], chip ^ 1, core)
     for step, pair in enumerate(pairs):
         at = chip ^ (2 + step + len(pairs) * core)
         total = total + down_product(down_high, down_low, pair[...], at, core)
@@ -227,13 +225,8 @@
 
 def far_kernel(peer_count, list_in, count_in, *refs):
     peers = refs[:peer_count]
-    coupling, after, coupled, table, rights, far_list, far_count, sem = refs[peer_count:]
-    copies = [
-        pltpu.make_async_copy(list_in, far_list, sem.at[0]),
-        pltpu.make_async_copy(count_in, far_count, sem.at[1]),
-    ]
-    for copy in copies:
-        copy.start()
+    coupling, after, coupled, table = refs[peer_count:]
+    far_list, far_count = list_in[...], count_in[...]
     leaves, slots, rank = coupling.shape[0], coupling.shape[1], coupling.shape[2]
     rows = table.shape[1]
     empty = peer_count * leaves
@@ -246,15 +239,8 @@
             first, second = block[:, :rank], block[:, rank:]
             table[begin + 2 * pair] = jnp.concatenate([first, first], axis=1)
             table[begin + 2 * pair + 1] = jnp.concatenate([second, second], axis=1)
-    for leaf in range(leaves // 2):
-        for slot in range(0, slots, 2):
-            rights[leaf, :, rank * slot : rank * (slot + 2)] = jnp.concatenate(
-                [coupling[leaf, slot], coupling[leaf, slot + 1]], axis=1
-            )
     own = lax.axis_index("list")
     lower = lax.broadcasted_iota(jnp.int32, (rows, 2 * rank), 1) < rank
-    for copy in copies:
-        copy.wait()
 
     def entry(leaf, slot):
         source = far_list[slot, leaf]
@@ -267,16 +253,13 @@
             jnp.where(lower, table[entry(leaf, slot)], table[entry(leaf, slot + 1)])
             for slot in range(0, slots, 2)
         ]
-        if leaf < leaves // 2:
-            right = rights[leaf]
-        else:
-            right = jnp.concatenate(
-                [
-                    jnp.concatenate([coupling[leaf, slot], coupling[leaf, slot + 1]], axis=1)
-                    for slot in range(0, slots, 2)
-                ],
-                axis=1,
-            )
+        right = jnp.concatenate(
+            [
+                jnp.concatenate([coupling[leaf, slot], coupling[leaf, slot + 1]], axis=1)
+                for slot in range(0, slots, 2)
+            ],
+            axis=1,
+        )
         return times_transposed(jnp.concatenate(lefts, axis=1), right)
 
     for pair in range(leaves // 2):
@@ -298,16 +281,16 @@
     )
 
 
-def down_kernel(part, swapped, down_high, down_low, weights, base, out, buffer, sem):
+def down_kernel(part, beside, swapped, down_high, down_low, weights, base, out, buffer, sem):
     place = lax.axis_index("leaf")
     chip, other = place // 2, 1 - place % 2
     total = part[...]
+    total = total + down_product(down_high, down_low, beside[...], chip ^ 1, 1 - other)
     steps = swapped.shape[0]
     for step in range(steps):
         at = chip ^ (2 + step + steps * other)
         total = total + down_product(down_high, down_low, swapped[step], at, other)
-    high, low = split(total)
-    wide = jnp.concatenate([high, low, high], axis=1)
+    wide = total.astype(bf16)
     copies = []
     group = 2
     for begin in range(0, base.shape[0], group):
@@ -424,7 +407,7 @@
             shape(leaves, rows, panels, dtype=f32),
             *[like(array) for array in fetched],
             shape(depth, *level_coupling.shape[1:], dtype=f32),
-            shape(leaves, 3 * rank, panels),
+            shape(leaves, rank, panels),
         ],
         in_specs=[anywhere, whole, whole, anywhere, whole, whole] + [anywhere] * (1 + len(fetched)),
         out_specs=[whole] * (3 + len(fetched)),
@@ -544,14 +527,10 @@
     coupled = pl.pallas_call(
         functools.partial(far_kernel, list_count - 1),
         out_shape=shape(leaves // 2, rows, 2 * rank, dtype=f32),
-        in_specs=[anywhere] * 2 + [whole] * list_count + [anywhere],
+        in_specs=[whole] * 2 + [whole] * list_count + [anywhere],
         out_specs=whole,
         scratch_shapes=[
             pltpu.VMEM(((list_count - 1) * leaves + 1, rows, 2 * rank), bf16),
-            pltpu.VMEM((leaves, rank, far_list.shape[0] * rank), bf16),
-            pltpu.SMEM(far_list.shape, jnp.int32),
-            pltpu.SMEM(far_count.shape, jnp.int32),
-            pltpu.SemaphoreType.DMA((2,)),
         ],
         compiler_params=params(8),
         cost_estimate=pl.CostEstimate(
@@ -575,16 +554,16 @@
             shape(leaves, rows, panels, dtype=f32),
             shape(rows, rank, dtype=f32),
         ],
-        in_specs=[whole] * (7 + steps),
+        in_specs=[whole] * (6 + steps),
         out_specs=[whole] * 2,
         compiler_params=params(4),
         name="base",
-    )(coupled, basis_later, near, down_high, down_low, own_pair, beside, *received)
+    )(coupled, basis_later, near, down_high, down_low, own_pair, *received)
 
     return pl.pallas_call(
         down_kernel,
         out_shape=shape(leaves, rows, panels),
-        in_specs=[whole] * 6,
+        in_specs=[whole] * 7,
         out_specs=anywhere,
         scratch_shapes=[
             pltpu.VMEM((leaves, rows, panels), bf16),
@@ -592,7 +571,7 @@
         ],
         compiler_params=params(4),
         name="down",
-    )(part, swapped, down_high, down_low, weights, base)
+    )(part, beside, swapped, down_high, down_low, weights, base)
 
 
 def solution(mesh):

time: 21.3 us -> 20.5 us (0.962)
  Pallas kernels: 10.2 us -> 9.31 us
    pallas_call x1, Pallas kernels: 1.69 us -> 1.28 us  [on_device(): pl.pallas_call(functools.partial(far_kernel, list_count - 1), out_shape=s...]
    pallas_call x1, Pallas kernels: 3.59 us -> 3.28 us  [on_device(): pl.pallas_call(functools.partial(near_kernel, leaf_count), out_shape=[sha...]
  transfers between devices with their start and end apart: 9 -> 9, of which waited for: 0 -> 0; matrix products, arithmetic and copies ran while one was open for 0% -> 0% of each run, Pallas kernels for 31% -> 29%
where the time goes in v7:
time: 20.5 us; the launch traced here: 20.4 us
  starting transfers between devices  10.9 us (53%)
  Pallas kernels  9.31 us (45%)
    ppermute x4, starting transfers between devices, spread(): return lax.ppermute(array, ('leaf', 'list'), list(enumerate(ends)))  5.97 us
    pallas_call x1, Pallas kernels, on_device(): pl.pallas_call(functools.partial(near_kernel, leaf_count), out_shape=[sha...  3.28 us
    ppermute x1, starting transfers between devices, on_device(): lax.ppermute(rounded_pair, 'leaf', [(i, i ^ 2 * (2 + step + steps * (i %...  2.6 us
    ppermute x4, starting transfers between devices, exchange(): return lax.ppermute(array, axis, pairs)  2.29 us
    pallas_call x1, Pallas kernels, on_device(): pl.pallas_call(functools.partial(upward_kernel, count), out_shape=[shape(...  2.09 us
    pallas_call x1, Pallas kernels, on_device(): pl.pallas_call(functools.partial(far_kernel, list_count - 1), out_shape=s...  1.28 us
    pallas_call x1, Pallas kernels, on_device(): pl.pallas_call(down_kernel, out_shape=shape(leaves, rows, panels), in_spe...  1.25 us
    pallas_call x1, Pallas kernels, on_device(): pl.pallas_call(functools.partial(tree_kernel, leaf_count), out_shape=[sha...  0.75 us
  transfers between devices with their start and end apart: 9, of which 0 were waited for; matrix products, arithmetic and copies ran while one was open for 0% of the time, Pallas kernels for 29%

profile of v7, /device:TPU:0, one launch (start us, length us, event | category | flops | bytes accessed | tf_op | source)
XLA Modules:
  0.0 20.4 jit_solution(16896636986998041884)
XLA Ops:
  0.0 2.1 %upward.1 = (bf16[9,64,128]{2,1,0:T(8,128)(2,1)S(1)}, bf16[16,64,256]{2,1,0:T(8,128)(2,1)S(1)}, bf16[16,64,256]{2,1,0:T(8,128)(2,1)S(1)}, f32[16,64,64]{2,1,0:T(...) custom-call(bf16[16,64,256]{2,1,0:T(8,128)(2,1)} %refs_0_.2, ...), custom_call_target="tpu_custom_call" | custom-call | tf_op jit(solution)/shard_map/upward/pallas_call | solution.py:349
  2.1 0.0 slice-start
  2.1 0.0 slice-start.1
  2.1 0.5 %collective-permute-start.2 = (bf16[9,64,128]{2,1,0:T(8,128)(2,1)S(1)}, bf16[9,64,128]{2,1,0:T(8,128)(2,1)S(1)}, u32[]{:S(2)}, u32[]{:S(2)}) collective-permute-start(bf16[9,64,128]{2,1,0:T(8,128)(2,1)S(1)} %mark.1.own.refs_0_), channel_id=1, source_target_pairs={{0,4},{4,0},{8,12},{12,8},{16,20},{20,16},{24,28},{28,24},{1,5},{5... | collective-permute-start | bytes 442376 | tf_op jit(solution)/shard_map/ppermute | solution.py:336
  2.6 2.6 %collective-permute-start = (bf16[9,64,128]{2,1,0:T(8,128)(2,1)S(1)}, bf16[9,64,128]{2,1,0:T(8,128)(2,1)S(1)}, u32[]{:S(2)}, u32[]{:S(2)}) collective-permute-start(bf16[9,64,128]{2,1,0:T(8,128)(2,1)S(1)} %mark.1.own.refs_0_), channel_id=1, source_target_pairs={{0,1},{1,0},{2,3},{3,2},{4,6},{5,7},{6,4},{7,5},{8,9},{9,8},{10,11... | collective-permute-start | bytes 442376 | tf_op jit(solution)/shard_map/ppermute | solution.py:341
  5.2 1.5 %collective-permute-start.1 = (bf16[9,64,128]{2,1,0:T(8,128)(2,1)S(1)}, bf16[9,64,128]{2,1,0:T(8,128)(2,1)S(1)}, u32[]{:S(2)}, u32[]{:S(2)}) collective-permute-start(bf16[9,64,128]{2,1,0:T(8,128)(2,1)S(1)} %mark.1.own.refs_0_), channel_id=1, source_target_pairs={{0,2},{1,3},{2,0},{3,1},{4,5},{5,4},{6,7},{7,6},{8,10},{9,11},{10,... | collective-permute-start | bytes 442376 | tf_op jit(solution)/shard_map/ppermute | solution.py:341
  6.7 0.0 collective-permute-done.2.other
  6.7 0.1 terms.1.after
  6.9 0.5 %collective-permute-start.3 = (bf16[64,128]{1,0:T(8,128)(2,1)S(1)}, bf16[64,128]{1,0:T(8,128)(2,1)S(1)}, u32[]{:S(2)}, u32[]{:S(2)}) collective-permute-start(bf16[64,128]{1,0:T(8,128)(2,1)S(1)} %terms.1.after), channel_id=1, source_target_pairs={{0,1},{1,0},{2,3},{3,2},{4,7},{5,6},{6,5},{7,4},{8,9},{9,8},{10,11... | collective-permute-start | bytes 49160 | tf_op jit(solution)/shard_map/ppermute | solution.py:341
  7.4 3.3 %near.1 = (f32[16,64,256]{2,1,0:T(8,128)S(1)}, f32[8,64,64]{2,1,0:T(8,128)S(1)}, f32[64,64]{1,0:T(8,128)S(1)}, bf16[16,64,256]{2,1,0:T(8,128)(2,1)S(1)}, bf16[16...) custom-call(s32[4,16]{1,0:T(4,128)S(1)} %get-tuple-element.28.list_in, ...), custom_call_target="tpu_custom_call" | custom-call | flops 536870912 | bytes 8388608 | tf_op jit(solution)/shard_map/near/pallas_call | solution.py:404
  10.7 0.0 collective-permute-done.1.refs_2_.refs_1_
  10.7 0.0 collective-permute-done.3.refs_3_
  10.7 0.1 group_sum.1.near.after.mine
  10.8 0.1 collective-permute-start.5
  11.0 1.3 %collective-permute-start.4 = (bf16[8,64,128]{2,1,0:T(8,128)(2,1)S(1)}, bf16[8,64,128]{2,1,0:T(8,128)(2,1)S(1)}, u32[]{:S(2)}, u32[]{:S(2)}) collective-permute-start(bf16[8,64,128]{2,1,0:T(8,128)(2,1)S(1)} %forward.1), channel_id=1, source_target_pairs={{0,2},{1,3},{2,0},{3,1},{4,5},{5,4},{6,7},{7,6},{8,10},{9,11},{10,... | collective-permute-start | bytes 393224 | tf_op jit(solution)/shard_map/ppermute | solution.py:341
  12.3 0.0 collective-permute-done.5.theirs
  12.3 0.1 pair.1
  12.4 2.6 %collective-permute-start.6 = (bf16[64,128]{1,0:T(8,128)(2,1)S(1)}, bf16[64,128]{1,0:T(8,128)(2,1)S(1)}, u32[]{:S(2)}, u32[]{:S(2)}) collective-permute-start(bf16[64,128]{1,0:T(8,128)(2,1)S(1)} %get-tuple-element.34), channel_id=1, source_target_pairs={{0,16},{4,28},{8,24},{12,20},{16,0},{20,12},{24,8},{28,4},{1,17},{... | collective-permute-start | bytes 49160 | tf_op jit(solution)/shard_map/ppermute | solution.py:501
  15.0 1.6 %collective-permute-start.7 = (f32[64,128]{1,0:T(8,128)S(1)}, f32[64,128]{1,0:T(8,128)S(1)}, u32[]{:S(2)}, u32[]{:S(2)}) collective-permute-start(f32[64,128]{1,0:T(8,128)S(1)} %get-tuple-element.38.sums.own), channel_id=1, source_target_pairs={{0,8},{4,12},{8,0},{12,4},{16,24},{20,28},{24,16},{28,20},{1,9},{5... | collective-permute-start | bytes 98312 | tf_op jit(solution)/shard_map/ppermute | solution.py:336
  16.6 0.7 %tree.1 = (bf16[8,64,64]{2,1,0:T(8,128)(2,1)S(1)}, bf16[8,64,64]{2,1,0:T(8,128)(2,1)S(1)}) custom-call(f32[8,64,64]{2,1,0:T(8,128)S(1)} %get-tuple-element.35.tree, f32[2,4,64,64]{3,2,1,0:T(8,128)S(1)} %get-tuple-element.36.couplings, f32[64,64]{1,0:T(8,128)S(1)} %get-tuple-element.37.matrix, f32[64,128]{1,0:T(8,128)S(1)} %get-tuple-element.38.sums.own), custom_call_target="tpu_custom_call" | custom-call | flops 17179869184 | bytes 268435456 | tf_op jit(solution)/shard_map/tree/pallas_call | solution.py:481
  17.4 0.1 collective-permute-start.8
  17.5 1.3 %far.1.coupled = f32[8,64,128]{2,1,0:T(8,128)S(1)} custom-call(s32[8,16]{1,0:T(8,128)S(1)} %get-tuple-element.25.list_in, s32[1,16]{1,0:T(1,128)S(1)} %get-tuple-element.26.count_in, bf16[9,64,128]{2,1,0:T(8,128)(2,1)S(1)} %collective-permute-done.refs_1_.payload.refs_0_, bf16[9,64,128]{2,1,0:T(8,128)(2,1)S(1)} %collective-permute-done.1.refs_2_.refs_1_, ...), custom_call_target="tpu_custom_call" | custom-call | flops 268435456 | bytes 2097152 | tf_op jit(solution)/shard_map/far/pallas_call | solution.py:527
  18.7 0.3 %base.1 = (f32[16,64,256]{2,1,0:T(8,128)S(1)}, f32[64,64]{1,0:T(8,128)S(1)}) custom-call(f32[8,64,128]{2,1,0:T(8,128)S(1)} %far.1.coupled, bf16[16,64,256]{2,1,0:T(8,128)(2,1)S(1)} %get-tuple-element.40.basis, f32[16,64,256]{2,1,0:T(8,128)S(1)} %get-tuple-element.32.refs_4_.near, bf16[8,64,64]{2,1,0:T(8,128)(2,1)S(1)} %get-tuple-element.39.refs_1_.down_high, ...), custom_call_target="tpu_custom_call" | custom-call | tf_op jit(solution)/shard_map/base/pallas_call | solution.py:551
  19.1 1.3 %down.1 = bf16[16,64,256]{2,1,0:T(8,128)(2,1)} custom-call(f32[64,64]{1,0:T(8,128)S(1)} %get-tuple-element.42.part, f32[64,128]{1,0:T(8,128)S(1)} %collective-permute-done.7.beside, bf16[1,64,128]{2,1,0:T(8,128)(2,1)S(1)} %collective-permute-done.8.swapped, bf16[8,64,64]{2,1,0:T(8,128)(2,1)S(1)} %get-tuple-element.39.refs_1_.down_high, ...), custom_call_target="tpu_custom_call" | custom-call | tf_op jit(solution)/shard_map/down/pallas_call | solution.py:563
  (12 shorter events, 0.0 us)
Async XLA Ops:
  2.1 5.3 %slice-start = ((s8[8388608]{0:T(1024)(128)(4,1)}), s8[4194304]{0:T(1024)(128)(4,1)S(1)}, s32[]{:S(2)}) async-start(s8[8388608]{0:T(1024)(128)(4,1)} %bitcast.4), calls=%async_computation | async-start | bytes 8388608
  2.1 5.3 %slice-start.1 = ((s8[8388608]{0:T(1024)(128)(4,1)}), s8[4194304]{0:T(1024)(128)(4,1)S(1)}, s32[]{:S(2)}) async-start(s8[8388608]{0:T(1024)(128)(4,1)} %bitcast.4), calls=%async_computation.1 | async-start | bytes 8388608
  2.1 4.6 %collective-permute-start.2 = (bf16[9,64,128]{2,1,0:T(8,128)(2,1)S(1)}, bf16[9,64,128]{2,1,0:T(8,128)(2,1)S(1)}, u32[]{:S(2)}, u32[]{:S(2)}) collective-permute-start(bf16[9,64,128]{2,1,0:T(8,128)(2,1)S(1)} %mark.1.own.refs_0_), channel_id=1, source_target_pairs={{0,4},{4,0},{8,12},{12,8},{16,20},{20,16},{24,28},{28,24},{1,5},{5... | collective-permute-start | bytes 442376 | tf_op jit(solution)/shard_map/ppermute | solution.py:336
  2.6 8.1 %collective-permute-start = (bf16[9,64,128]{2,1,0:T(8,128)(2,1)S(1)}, bf16[9,64,128]{2,1,0:T(8,128)(2,1)S(1)}, u32[]{:S(2)}, u32[]{:S(2)}) collective-permute-start(bf16[9,64,128]{2,1,0:T(8,128)(2,1)S(1)} %mark.1.own.refs_0_), channel_id=1, source_target_pairs={{0,1},{1,0},{2,3},{3,2},{4,6},{5,7},{6,4},{7,5},{8,9},{9,8},{10,11... | collective-permute-start | bytes 442376 | tf_op jit(solution)/shard_map/ppermute | solution.py:341
  5.2 5.5 %collective-permute-start.1 = (bf16[9,64,128]{2,1,0:T(8,128)(2,1)S(1)}, bf16[9,64,128]{2,1,0:T(8,128)(2,1)S(1)}, u32[]{:S(2)}, u32[]{:S(2)}) collective-permute-start(bf16[9,64,128]{2,1,0:T(8,128)(2,1)S(1)} %mark.1.own.refs_0_), channel_id=1, source_target_pairs={{0,2},{1,3},{2,0},{3,1},{4,5},{5,4},{6,7},{7,6},{8,10},{9,11},{10,... | collective-permute-start | bytes 442376 | tf_op jit(solution)/shard_map/ppermute | solution.py:341
  6.9 3.9 %collective-permute-start.3 = (bf16[64,128]{1,0:T(8,128)(2,1)S(1)}, bf16[64,128]{1,0:T(8,128)(2,1)S(1)}, u32[]{:S(2)}, u32[]{:S(2)}) collective-permute-start(bf16[64,128]{1,0:T(8,128)(2,1)S(1)} %terms.1.after), channel_id=1, source_target_pairs={{0,1},{1,0},{2,3},{3,2},{4,7},{5,6},{6,5},{7,4},{8,9},{9,8},{10,11... | collective-permute-start | bytes 49160 | tf_op jit(solution)/shard_map/ppermute | solution.py:341
  10.8 1.5 %collective-permute-start.5 = (f32[2,64,128]{2,1,0:T(8,128)S(1)}, f32[2,64,128]{2,1,0:T(8,128)S(1)}, u32[]{:S(2)}, u32[]{:S(2)}) collective-permute-start(f32[2,64,128]{2,1,0:T(8,128)S(1)} %group_sum.1.near.after.mine), channel_id=1, source_target_pairs={{0,4},{4,0},{8,12},{12,8},{16,20},{20,16},{24,28},{28,24},{1,5},{5... | collective-permute-start | bytes 196616 | tf_op jit(solution)/shard_map/ppermute | solution.py:336
  11.0 6.5 %collective-permute-start.4 = (bf16[8,64,128]{2,1,0:T(8,128)(2,1)S(1)}, bf16[8,64,128]{2,1,0:T(8,128)(2,1)S(1)}, u32[]{:S(2)}, u32[]{:S(2)}) collective-permute-start(bf16[8,64,128]{2,1,0:T(8,128)(2,1)S(1)} %forward.1), channel_id=1, source_target_pairs={{0,2},{1,3},{2,0},{3,1},{4,5},{5,4},{6,7},{7,6},{8,10},{9,11},{10,... | collective-permute-start | bytes 393224 | tf_op jit(solution)/shard_map/ppermute | solution.py:341
  12.4 4.9 %collective-permute-start.6 = (bf16[64,128]{1,0:T(8,128)(2,1)S(1)}, bf16[64,128]{1,0:T(8,128)(2,1)S(1)}, u32[]{:S(2)}, u32[]{:S(2)}) collective-permute-start(bf16[64,128]{1,0:T(8,128)(2,1)S(1)} %get-tuple-element.34), channel_id=1, source_target_pairs={{0,16},{4,28},{8,24},{12,20},{16,0},{20,12},{24,8},{28,4},{1,17},{... | collective-permute-start | bytes 49160 | tf_op jit(solution)/shard_map/ppermute | solution.py:501
  15.0 4.1 %collective-permute-start.7 = (f32[64,128]{1,0:T(8,128)S(1)}, f32[64,128]{1,0:T(8,128)S(1)}, u32[]{:S(2)}, u32[]{:S(2)}) collective-permute-start(f32[64,128]{1,0:T(8,128)S(1)} %get-tuple-element.38.sums.own), channel_id=1, source_target_pairs={{0,8},{4,12},{8,0},{12,4},{16,24},{20,28},{24,16},{28,20},{1,9},{5... | collective-permute-start | bytes 98312 | tf_op jit(solution)/shard_map/ppermute | solution.py:336
  17.4 1.7 %collective-permute-start.8 = (bf16[1,64,128]{2,1,0:T(8,128)(2,1)S(1)}, bf16[1,64,128]{2,1,0:T(8,128)(2,1)S(1)}, u32[]{:S(2)}, u32[]{:S(2)}) collective-permute-start(bf16[1,64,128]{2,1,0:T(8,128)(2,1)S(1)} %relay.1.refs_4_), channel_id=1, source_target_pairs={{0,4},{4,0},{8,12},{12,8},{16,20},{20,16},{24,28},{28,24},{1,5},{5... | collective-permute-start | bytes 49160 | tf_op jit(solution)/shard_map/ppermute | solution.py:336

commit v8 on v7

--- a/solution.py
+++ b/solution.py
@@ -7,7 +7,6 @@
 from jax.experimental.pallas import tpu as pltpu
 from jax.sharding import PartitionSpec as P
 
-offsets = (-3, -2, 2, 3)
 f32 = jnp.float32
 bf16 = jnp.bfloat16
 whole = pl.BlockSpec(memory_space=pltpu.VMEM)
@@ -158,36 +157,43 @@
     sums[1] = total
 
 
-def tree_kernel(
-    leaf_count, tree, couplings, matrix, sums, down_high, down_low, down
-):
-    rank = matrix.shape[0]
+def tree_kernel(leaf_count, tree, couplings, matrix, sums, down_high, down_low):
     depth = leaf_count.bit_length() - 2
     place = lax.axis_index("leaf")
     begins = [2 * leaf_count - 2 * (leaf_count >> height) for height in range(depth)]
-    down[...] = jnp.zeros_like(down)
     back = matrix[...]
+    added = []
     for height in range(depth):
-        members = leaf_count >> height
         spot = place >> height
-        for slot, offset in enumerate(offsets):
-            source = spot + offset
-            usable = jnp.logical_and(source >= 0, source < members)
-            if abs(offset) == 3:
-                usable = jnp.logical_and(usable, spot % 2 == (0 if offset > 0 else 1))
-            entry = begins[height] + jnp.clip(source, 0, members - 1)
-            part = exact(times, back, couplings[height, slot])
-            down[entry] += jnp.where(usable, part, jnp.zeros_like(part))
+        even = spot % 2 == 0
+        picks = [(jnp.where(even, 3, 0), spot + jnp.where(even, 3, -3))]
+        if height == depth - 1:
+            picks.append((jnp.where(spot < 2, 2, 1), spot ^ 2))
+        else:
+            picks += [(1, spot - 2), (2, spot + 2)]
+        added.append([(at, exact(times, back, couplings[height, slot])) for slot, at in picks])
         if height < depth - 1:
             back = exact(times, back, tree[begins[height] + spot])
+    nodes = added[-1]
     for height in reversed(range(depth - 1)):
-        for parent in range(leaf_count >> (height + 1)):
+        members = leaf_count >> height
+        parts = list(added[height])
+        for parent, value in nodes:
             for child in (2 * parent, 2 * parent + 1):
-                down[begins[height] + child] += exact(
-                    times_transposed, down[begins[height + 1] + parent], tree[begins[height] + child]
-                )
-    for node in range(leaf_count):
-        high, low = split(down[node])
+                safe = child if isinstance(child, int) else jnp.clip(child, 0, members - 1)
+                product = exact(times_transposed, value, tree[begins[height] + safe])
+                parts.append((child, product))
+        nodes = []
+        for node in range(members):
+            total = jnp.zeros(matrix.shape, f32)
+            for at, value in parts:
+                if isinstance(at, int):
+                    total = total + value if at == node else total
+                else:
+                    total = total + jnp.where(at == node, value, jnp.zeros_like(value))
+            nodes.append((node, total))
+    for node, value in nodes:
+        high, low = split(value)
         down_high[node] = high
         down_low[node] = low
 
@@ -486,7 +492,6 @@
         ],
         in_specs=[whole] * 3 + [anywhere],
         out_specs=[whole] * 2,
-        scratch_shapes=[pltpu.VMEM((2 * leaf_count, rank, rank), f32)],
         compiler_params=params(4),
         cost_estimate=pl.CostEstimate(
             flops=64 * near_blocks.size * rows,

time: 20.5 us -> 20.5 us (level)
  transfers between devices with their start and end apart: 9 -> 9, of which waited for: 0 -> 1; matrix products, arithmetic and copies ran while one was open for 0% -> 0% of each run, Pallas kernels for 29% -> 28%
where the time goes in v8:
time: 20.5 us; the launch traced here: 20.3 us
  starting transfers between devices  10.9 us (53%)
  Pallas kernels  9.21 us (45%)
    ppermute x4, starting transfers between devices, spread(): return lax.ppermute(array, ('leaf', 'list'), list(enumerate(ends)))  5.97 us
    pallas_call x1, Pallas kernels, on_device(): pl.pallas_call(functools.partial(near_kernel, leaf_count), out_shape=[sha...  3.28 us
    ppermute x1, starting transfers between devices, on_device(): lax.ppermute(rounded_pair, 'leaf', [(i, i ^ 2 * (2 + step + steps * (i %...  2.6 us
    ppermute x4, starting transfers between devices, exchange(): return lax.ppermute(array, axis, pairs)  2.29 us
    pallas_call x1, Pallas kernels, on_device(): pl.pallas_call(functools.partial(upward_kernel, count), out_shape=[shape(...  2.09 us
    pallas_call x1, Pallas kernels, on_device(): pl.pallas_call(functools.partial(far_kernel, list_count - 1), out_shape=s...  1.28 us
    pallas_call x1, Pallas kernels, on_device(): pl.pallas_call(down_kernel, out_shape=shape(leaves, rows, panels), in_spe...  1.25 us
    pallas_call x1, Pallas kernels, on_device(): pl.pallas_call(functools.partial(tree_kernel, leaf_count), out_shape=[sha...  0.64 us
  transfers between devices with their start and end apart: 9, of which 1 were waited for; matrix products, arithmetic and copies ran while one was open for 0% of the time, Pallas kernels for 28%

profile of v8, /device:TPU:0, one launch (start us, length us, event | category | flops | bytes accessed | tf_op | source)
XLA Modules:
  0.0 20.3 jit_solution(17660819848278093391)
XLA Ops:
  0.0 2.1 %upward.1 = (bf16[9,64,128]{2,1,0:T(8,128)(2,1)S(1)}, bf16[16,64,256]{2,1,0:T(8,128)(2,1)S(1)}, bf16[16,64,256]{2,1,0:T(8,128)(2,1)S(1)}, f32[16,64,64]{2,1,0:T(...) custom-call(bf16[16,64,256]{2,1,0:T(8,128)(2,1)} %refs_0_.2, ...), custom_call_target="tpu_custom_call" | custom-call | tf_op jit(solution)/shard_map/upward/pallas_call | solution.py:355
  2.1 0.0 slice-start
  2.1 0.5 %collective-permute-start.2 = (bf16[9,64,128]{2,1,0:T(8,128)(2,1)S(1)}, bf16[9,64,128]{2,1,0:T(8,128)(2,1)S(1)}, u32[]{:S(2)}, u32[]{:S(2)}) collective-permute-start(bf16[9,64,128]{2,1,0:T(8,128)(2,1)S(1)} %mark.1.own.refs_0_), channel_id=1, source_target_pairs={{0,4},{4,0},{8,12},{12,8},{16,20},{20,16},{24,28},{28,24},{1,5},{5... | collective-permute-start | bytes 442376 | tf_op jit(solution)/shard_map/ppermute | solution.py:342
  2.6 2.6 %collective-permute-start = (bf16[9,64,128]{2,1,0:T(8,128)(2,1)S(1)}, bf16[9,64,128]{2,1,0:T(8,128)(2,1)S(1)}, u32[]{:S(2)}, u32[]{:S(2)}) collective-permute-start(bf16[9,64,128]{2,1,0:T(8,128)(2,1)S(1)} %mark.1.own.refs_0_), channel_id=1, source_target_pairs={{0,1},{1,0},{2,3},{3,2},{4,6},{5,7},{6,4},{7,5},{8,9},{9,8},{10,11... | collective-permute-start | bytes 442376 | tf_op jit(solution)/shard_map/ppermute | solution.py:347
  5.2 1.5 %collective-permute-start.1 = (bf16[9,64,128]{2,1,0:T(8,128)(2,1)S(1)}, bf16[9,64,128]{2,1,0:T(8,128)(2,1)S(1)}, u32[]{:S(2)}, u32[]{:S(2)}) collective-permute-start(bf16[9,64,128]{2,1,0:T(8,128)(2,1)S(1)} %mark.1.own.refs_0_), channel_id=1, source_target_pairs={{0,2},{1,3},{2,0},{3,1},{4,5},{5,4},{6,7},{7,6},{8,10},{9,11},{10,... | collective-permute-start | bytes 442376 | tf_op jit(solution)/shard_map/ppermute | solution.py:347
  6.7 0.1 terms.1.after
  6.9 0.5 %collective-permute-start.3 = (bf16[64,128]{1,0:T(8,128)(2,1)S(1)}, bf16[64,128]{1,0:T(8,128)(2,1)S(1)}, u32[]{:S(2)}, u32[]{:S(2)}) collective-permute-start(bf16[64,128]{1,0:T(8,128)(2,1)S(1)} %terms.1.after), channel_id=1, source_target_pairs={{0,1},{1,0},{2,3},{3,2},{4,7},{5,6},{6,5},{7,4},{8,9},{9,8},{10,11... | collective-permute-start | bytes 49160 | tf_op jit(solution)/shard_map/ppermute | solution.py:347
  7.4 3.3 %near.1 = (f32[16,64,256]{2,1,0:T(8,128)S(1)}, f32[8,64,64]{2,1,0:T(8,128)S(1)}, f32[64,64]{1,0:T(8,128)S(1)}, bf16[16,64,256]{2,1,0:T(8,128)(2,1)S(1)}, bf16[16...) custom-call(s32[4,16]{1,0:T(4,128)S(1)} %get-tuple-element.28.list_in, ...), custom_call_target="tpu_custom_call" | custom-call | flops 536870912 | bytes 8388608 | tf_op jit(solution)/shard_map/near/pallas_call | solution.py:410
  10.7 0.0 collective-permute-done.refs_1_.payload.refs_0_
  10.7 0.0 collective-permute-done.3.refs_3_
  10.7 0.1 group_sum.1.near.after.mine
  10.8 0.1 collective-permute-start.5
  11.0 1.3 %collective-permute-start.4 = (bf16[8,64,128]{2,1,0:T(8,128)(2,1)S(1)}, bf16[8,64,128]{2,1,0:T(8,128)(2,1)S(1)}, u32[]{:S(2)}, u32[]{:S(2)}) collective-permute-start(bf16[8,64,128]{2,1,0:T(8,128)(2,1)S(1)} %forward.1), channel_id=1, source_target_pairs={{0,2},{1,3},{2,0},{3,1},{4,5},{5,4},{6,7},{7,6},{8,10},{9,11},{10,... | collective-permute-start | bytes 393224 | tf_op jit(solution)/shard_map/ppermute | solution.py:347
  12.3 0.0 collective-permute-done.5.theirs
  12.3 0.1 pair.1
  12.4 2.6 %collective-permute-start.6 = (bf16[64,128]{1,0:T(8,128)(2,1)S(1)}, bf16[64,128]{1,0:T(8,128)(2,1)S(1)}, u32[]{:S(2)}, u32[]{:S(2)}) collective-permute-start(bf16[64,128]{1,0:T(8,128)(2,1)S(1)} %get-tuple-element.34), channel_id=1, source_target_pairs={{0,16},{4,28},{8,24},{12,20},{16,0},{20,12},{24,8},{28,4},{1,17},{... | collective-permute-start | bytes 49160 | tf_op jit(solution)/shard_map/ppermute | solution.py:506
  15.0 1.6 %collective-permute-start.7 = (f32[64,128]{1,0:T(8,128)S(1)}, f32[64,128]{1,0:T(8,128)S(1)}, u32[]{:S(2)}, u32[]{:S(2)}) collective-permute-start(f32[64,128]{1,0:T(8,128)S(1)} %get-tuple-element.38.sums.own), channel_id=1, source_target_pairs={{0,8},{4,12},{8,0},{12,4},{16,24},{20,28},{24,16},{28,20},{1,9},{5... | collective-permute-start | bytes 98312 | tf_op jit(solution)/shard_map/ppermute | solution.py:342
  16.6 0.6 %tree.1 = (bf16[8,64,64]{2,1,0:T(8,128)(2,1)S(1)}, bf16[8,64,64]{2,1,0:T(8,128)(2,1)S(1)}) custom-call(f32[8,64,64]{2,1,0:T(8,128)S(1)} %get-tuple-element.35.tree, f32[2,4,64,64]{3,2,1,0:T(8,128)S(1)} %get-tuple-element.36.couplings, f32[64,64]{1,0:T(8,128)S(1)} %get-tuple-element.37.matrix, f32[64,128]{1,0:T(8,128)S(1)} %get-tuple-element.38.sums.own), custom_call_target="tpu_custom_call" | custom-call | flops 17179869184 | bytes 268435456 | tf_op jit(solution)/shard_map/tree/pallas_call | solution.py:487
  17.2 0.0 collective-permute-done.6.refs_0_
  17.3 0.1 collective-permute-start.8
  17.3 1.3 %far.1.coupled = f32[8,64,128]{2,1,0:T(8,128)S(1)} custom-call(s32[8,16]{1,0:T(8,128)S(1)} %get-tuple-element.25.list_in, s32[1,16]{1,0:T(1,128)S(1)} %get-tuple-element.26.count_in, bf16[9,64,128]{2,1,0:T(8,128)(2,1)S(1)} %collective-permute-done.refs_1_.payload.refs_0_, bf16[9,64,128]{2,1,0:T(8,128)(2,1)S(1)} %collective-permute-done.1.refs_2_.refs_1_, ...), custom_call_target="tpu_custom_call" | custom-call | flops 268435456 | bytes 2097152 | tf_op jit(solution)/shard_map/far/pallas_call | solution.py:532
  18.6 0.3 %base.1 = (f32[16,64,256]{2,1,0:T(8,128)S(1)}, f32[64,64]{1,0:T(8,128)S(1)}) custom-call(f32[8,64,128]{2,1,0:T(8,128)S(1)} %far.1.coupled, bf16[16,64,256]{2,1,0:T(8,128)(2,1)S(1)} %get-tuple-element.40.basis, f32[16,64,256]{2,1,0:T(8,128)S(1)} %get-tuple-element.32.refs_4_.near, bf16[8,64,64]{2,1,0:T(8,128)(2,1)S(1)} %get-tuple-element.39.refs_1_.down_high, ...), custom_call_target="tpu_custom_call" | custom-call | tf_op jit(solution)/shard_map/base/pallas_call | solution.py:556
  19.0 0.1 collective-permute-done.7.beside
  19.1 1.3 %down.1 = bf16[16,64,256]{2,1,0:T(8,128)(2,1)} custom-call(f32[64,64]{1,0:T(8,128)S(1)} %get-tuple-element.42.part, f32[64,128]{1,0:T(8,128)S(1)} %collective-permute-done.7.beside, bf16[1,64,128]{2,1,0:T(8,128)(2,1)S(1)} %collective-permute-done.8.swapped, bf16[8,64,64]{2,1,0:T(8,128)(2,1)S(1)} %get-tuple-element.39.refs_1_.down_high, ...), custom_call_target="tpu_custom_call" | custom-call | tf_op jit(solution)/shard_map/down/pallas_call | solution.py:568
  (12 shorter events, 0.0 us)
Async XLA Ops:
  2.1 5.3 %slice-start = ((s8[8388608]{0:T(1024)(128)(4,1)}), s8[4194304]{0:T(1024)(128)(4,1)S(1)}, s32[]{:S(2)}) async-start(s8[8388608]{0:T(1024)(128)(4,1)} %bitcast.4), calls=%async_computation | async-start | bytes 8388608
  2.1 5.3 %slice-start.1 = ((s8[8388608]{0:T(1024)(128)(4,1)}), s8[4194304]{0:T(1024)(128)(4,1)S(1)}, s32[]{:S(2)}) async-start(s8[8388608]{0:T(1024)(128)(4,1)} %bitcast.4), calls=%async_computation.1 | async-start | bytes 8388608
  2.1 4.6 %collective-permute-start.2 = (bf16[9,64,128]{2,1,0:T(8,128)(2,1)S(1)}, bf16[9,64,128]{2,1,0:T(8,128)(2,1)S(1)}, u32[]{:S(2)}, u32[]{:S(2)}) collective-permute-start(bf16[9,64,128]{2,1,0:T(8,128)(2,1)S(1)} %mark.1.own.refs_0_), channel_id=1, source_target_pairs={{0,4},{4,0},{8,12},{12,8},{16,20},{20,16},{24,28},{28,24},{1,5},{5... | collective-permute-start | bytes 442376 | tf_op jit(solution)/shard_map/ppermute | solution.py:342
  2.6 8.1 %collective-permute-start = (bf16[9,64,128]{2,1,0:T(8,128)(2,1)S(1)}, bf16[9,64,128]{2,1,0:T(8,128)(2,1)S(1)}, u32[]{:S(2)}, u32[]{:S(2)}) collective-permute-start(bf16[9,64,128]{2,1,0:T(8,128)(2,1)S(1)} %mark.1.own.refs_0_), channel_id=1, source_target_pairs={{0,1},{1,0},{2,3},{3,2},{4,6},{5,7},{6,4},{7,5},{8,9},{9,8},{10,11... | collective-permute-start | bytes 442376 | tf_op jit(solution)/shard_map/ppermute | solution.py:347
  5.2 5.5 %collective-permute-start.1 = (bf16[9,64,128]{2,1,0:T(8,128)(2,1)S(1)}, bf16[9,64,128]{2,1,0:T(8,128)(2,1)S(1)}, u32[]{:S(2)}, u32[]{:S(2)}) collective-permute-start(bf16[9,64,128]{2,1,0:T(8,128)(2,1)S(1)} %mark.1.own.refs_0_), channel_id=1, source_target_pairs={{0,2},{1,3},{2,0},{3,1},{4,5},{5,4},{6,7},{7,6},{8,10},{9,11},{10,... | collective-permute-start | bytes 442376 | tf_op jit(solution)/shard_map/ppermute | solution.py:347
  6.9 3.9 %collective-permute-start.3 = (bf16[64,128]{1,0:T(8,128)(2,1)S(1)}, bf16[64,128]{1,0:T(8,128)(2,1)S(1)}, u32[]{:S(2)}, u32[]{:S(2)}) collective-permute-start(bf16[64,128]{1,0:T(8,128)(2,1)S(1)} %terms.1.after), channel_id=1, source_target_pairs={{0,1},{1,0},{2,3},{3,2},{4,7},{5,6},{6,5},{7,4},{8,9},{9,8},{10,11... | collective-permute-start | bytes 49160 | tf_op jit(solution)/shard_map/ppermute | solution.py:347
  10.8 1.5 %collective-permute-start.5 = (f32[2,64,128]{2,1,0:T(8,128)S(1)}, f32[2,64,128]{2,1,0:T(8,128)S(1)}, u32[]{:S(2)}, u32[]{:S(2)}) collective-permute-start(f32[2,64,128]{2,1,0:T(8,128)S(1)} %group_sum.1.near.after.mine), channel_id=1, source_target_pairs={{0,4},{4,0},{8,12},{12,8},{16,20},{20,16},{24,28},{28,24},{1,5},{5... | collective-permute-start | bytes 196616 | tf_op jit(solution)/shard_map/ppermute | solution.py:342
  11.0 6.4 %collective-permute-start.4 = (bf16[8,64,128]{2,1,0:T(8,128)(2,1)S(1)}, bf16[8,64,128]{2,1,0:T(8,128)(2,1)S(1)}, u32[]{:S(2)}, u32[]{:S(2)}) collective-permute-start(bf16[8,64,128]{2,1,0:T(8,128)(2,1)S(1)} %forward.1), channel_id=1, source_target_pairs={{0,2},{1,3},{2,0},{3,1},{4,5},{5,4},{6,7},{7,6},{8,10},{9,11},{10,... | collective-permute-start | bytes 393224 | tf_op jit(solution)/shard_map/ppermute | solution.py:347
  12.4 4.8 %collective-permute-start.6 = (bf16[64,128]{1,0:T(8,128)(2,1)S(1)}, bf16[64,128]{1,0:T(8,128)(2,1)S(1)}, u32[]{:S(2)}, u32[]{:S(2)}) collective-permute-start(bf16[64,128]{1,0:T(8,128)(2,1)S(1)} %get-tuple-element.34), channel_id=1, source_target_pairs={{0,16},{4,28},{8,24},{12,20},{16,0},{20,12},{24,8},{28,4},{1,17},{... | collective-permute-start | bytes 49160 | tf_op jit(solution)/shard_map/ppermute | solution.py:506
  15.0 4.1 %collective-permute-start.7 = (f32[64,128]{1,0:T(8,128)S(1)}, f32[64,128]{1,0:T(8,128)S(1)}, u32[]{:S(2)}, u32[]{:S(2)}) collective-permute-start(f32[64,128]{1,0:T(8,128)S(1)} %get-tuple-element.38.sums.own), channel_id=1, source_target_pairs={{0,8},{4,12},{8,0},{12,4},{16,24},{20,28},{24,16},{28,20},{1,9},{5... | collective-permute-start | bytes 98312 | tf_op jit(solution)/shard_map/ppermute | solution.py:342
  17.3 1.8 %collective-permute-start.8 = (bf16[1,64,128]{2,1,0:T(8,128)(2,1)S(1)}, bf16[1,64,128]{2,1,0:T(8,128)(2,1)S(1)}, u32[]{:S(2)}, u32[]{:S(2)}) collective-permute-start(bf16[1,64,128]{2,1,0:T(8,128)(2,1)S(1)} %relay.1.refs_4_), channel_id=1, source_target_pairs={{0,4},{4,0},{8,12},{12,8},{16,20},{20,16},{24,28},{28,24},{1,5},{5... | collective-permute-start | bytes 49160 | tf_op jit(solution)/shard_map/ppermute | solution.py:342

commit v9 on v8

--- a/solution.py
+++ b/solution.py
@@ -298,7 +298,7 @@
         total = total + down_product(down_high, down_low, swapped[step], at, other)
     wide = total.astype(bf16)
     copies = []
-    group = 2
+    group = 8
     for begin in range(0, base.shape[0], group):
         for leaf in range(begin, begin + group):
             buffer[leaf] = (base[leaf] + times(wide, weights[leaf])).astype(bf16)
@@ -510,7 +510,7 @@
         )
         for step in range(steps)
     ]
-    beside = exchange(own_pair, "leaf", 2)
+    beside = exchange(rounded_pair, "leaf", 2)
 
     skeletons = {distance: arrived[distance] for distance in direct}
     for distance in range(1, list_count):
@@ -572,7 +572,7 @@
         out_specs=anywhere,
         scratch_shapes=[
             pltpu.VMEM((leaves, rows, panels), bf16),
-            pltpu.SemaphoreType.DMA((leaves // 2,)),
+            pltpu.SemaphoreType.DMA((leaves // 8,)),
         ],
         compiler_params=params(4),
         name="down",

time: 20.5 us -> 20.4 us (level)
  transfers between devices with their start and end apart: 9 -> 9, of which waited for: 1 -> 0; matrix products, arithmetic and copies ran while one was open for 0% -> 0% of each run, Pallas kernels for 28% -> 28%
where the time goes in v9:
time: 20.4 us; the launch traced here: 20.3 us
  starting transfers between devices  10.9 us (53%)
  Pallas kernels  9.22 us (45%)
    ppermute x4, starting transfers between devices, spread(): return lax.ppermute(array, ('leaf', 'list'), list(enumerate(ends)))  5.97 us
    pallas_call x1, Pallas kernels, on_device(): pl.pallas_call(functools.partial(near_kernel, leaf_count), out_shape=[sha...  3.28 us
    ppermute x1, starting transfers between devices, on_device(): lax.ppermute(rounded_pair, 'leaf', [(i, i ^ 2 * (2 + step + steps * (i %...  2.6 us
    ppermute x4, starting transfers between devices, exchange(): return lax.ppermute(array, axis, pairs)  2.29 us
    pallas_call x1, Pallas kernels, on_device(): pl.pallas_call(functools.partial(upward_kernel, count), out_shape=[shape(...  2.09 us
    pallas_call x1, Pallas kernels, on_device(): pl.pallas_call(functools.partial(far_kernel, list_count - 1), out_shape=s...  1.28 us
    pallas_call x1, Pallas kernels, on_device(): pl.pallas_call(down_kernel, out_shape=shape(leaves, rows, panels), in_spe...  1.27 us
    pallas_call x1, Pallas kernels, on_device(): pl.pallas_call(functools.partial(tree_kernel, leaf_count), out_shape=[sha...  0.64 us
  transfers between devices with their start and end apart: 9, of which 0 were waited for; matrix products, arithmetic and copies ran while one was open for 0% of the time, Pallas kernels for 28%

profile of v9, /device:TPU:0, one launch (start us, length us, event | category | flops | bytes accessed | tf_op | source)
XLA Modules:
  0.0 20.3 jit_solution(8733443740324169841)
XLA Ops:
  0.0 2.1 %upward.1 = (bf16[9,64,128]{2,1,0:T(8,128)(2,1)S(1)}, bf16[16,64,256]{2,1,0:T(8,128)(2,1)S(1)}, bf16[16,64,256]{2,1,0:T(8,128)(2,1)S(1)}, f32[16,64,64]{2,1,0:T(...) custom-call(bf16[16,64,256]{2,1,0:T(8,128)(2,1)} %refs_0_.2, ...), custom_call_target="tpu_custom_call" | custom-call | tf_op jit(solution)/shard_map/upward/pallas_call | solution.py:355
  2.1 0.0 slice-start
  2.1 0.0 slice-start.1
  2.1 0.5 %collective-permute-start.2 = (bf16[9,64,128]{2,1,0:T(8,128)(2,1)S(1)}, bf16[9,64,128]{2,1,0:T(8,128)(2,1)S(1)}, u32[]{:S(2)}, u32[]{:S(2)}) collective-permute-start(bf16[9,64,128]{2,1,0:T(8,128)(2,1)S(1)} %mark.1.own.refs_0_), channel_id=1, source_target_pairs={{0,4},{4,0},{8,12},{12,8},{16,20},{20,16},{24,28},{28,24},{1,5},{5... | collective-permute-start | bytes 442376 | tf_op jit(solution)/shard_map/ppermute | solution.py:342
  2.6 2.6 %collective-permute-start = (bf16[9,64,128]{2,1,0:T(8,128)(2,1)S(1)}, bf16[9,64,128]{2,1,0:T(8,128)(2,1)S(1)}, u32[]{:S(2)}, u32[]{:S(2)}) collective-permute-start(bf16[9,64,128]{2,1,0:T(8,128)(2,1)S(1)} %mark.1.own.refs_0_), channel_id=1, source_target_pairs={{0,1},{1,0},{2,3},{3,2},{4,6},{5,7},{6,4},{7,5},{8,9},{9,8},{10,11... | collective-permute-start | bytes 442376 | tf_op jit(solution)/shard_map/ppermute | solution.py:347
  5.2 1.5 %collective-permute-start.1 = (bf16[9,64,128]{2,1,0:T(8,128)(2,1)S(1)}, bf16[9,64,128]{2,1,0:T(8,128)(2,1)S(1)}, u32[]{:S(2)}, u32[]{:S(2)}) collective-permute-start(bf16[9,64,128]{2,1,0:T(8,128)(2,1)S(1)} %mark.1.own.refs_0_), channel_id=1, source_target_pairs={{0,2},{1,3},{2,0},{3,1},{4,5},{5,4},{6,7},{7,6},{8,10},{9,11},{10,... | collective-permute-start | bytes 442376 | tf_op jit(solution)/shard_map/ppermute | solution.py:347
  6.7 0.0 collective-permute-done.2.other
  6.7 0.1 terms.1.after
  6.9 0.5 %collective-permute-start.3 = (bf16[64,128]{1,0:T(8,128)(2,1)S(1)}, bf16[64,128]{1,0:T(8,128)(2,1)S(1)}, u32[]{:S(2)}, u32[]{:S(2)}) collective-permute-start(bf16[64,128]{1,0:T(8,128)(2,1)S(1)} %terms.1.after), channel_id=1, source_target_pairs={{0,1},{1,0},{2,3},{3,2},{4,7},{5,6},{6,5},{7,4},{8,9},{9,8},{10,11... | collective-permute-start | bytes 49160 | tf_op jit(solution)/shard_map/ppermute | solution.py:347
  7.4 3.3 %near.1 = (f32[16,64,256]{2,1,0:T(8,128)S(1)}, f32[8,64,64]{2,1,0:T(8,128)S(1)}, f32[64,64]{1,0:T(8,128)S(1)}, bf16[16,64,256]{2,1,0:T(8,128)(2,1)S(1)}, bf16[16...) custom-call(s32[4,16]{1,0:T(4,128)S(1)} %get-tuple-element.28.list_in, ...), custom_call_target="tpu_custom_call" | custom-call | flops 536870912 | bytes 8388608 | tf_op jit(solution)/shard_map/near/pallas_call | solution.py:410
  10.7 0.0 collective-permute-done.1.refs_2_.refs_1_
  10.7 0.0 collective-permute-done.3.refs_3_
  10.7 0.1 group_sum.1.near.after.mine
  10.8 0.1 collective-permute-start.5
  11.0 1.3 %collective-permute-start.4 = (bf16[8,64,128]{2,1,0:T(8,128)(2,1)S(1)}, bf16[8,64,128]{2,1,0:T(8,128)(2,1)S(1)}, u32[]{:S(2)}, u32[]{:S(2)}) collective-permute-start(bf16[8,64,128]{2,1,0:T(8,128)(2,1)S(1)} %forward.1), channel_id=1, source_target_pairs={{0,2},{1,3},{2,0},{3,1},{4,5},{5,4},{6,7},{7,6},{8,10},{9,11},{10,... | collective-permute-start | bytes 393224 | tf_op jit(solution)/shard_map/ppermute | solution.py:347
  12.3 0.0 collective-permute-done.5.theirs
  12.3 0.1 pair.1
  12.4 2.6 %collective-permute-start.6 = (bf16[64,128]{1,0:T(8,128)(2,1)S(1)}, bf16[64,128]{1,0:T(8,128)(2,1)S(1)}, u32[]{:S(2)}, u32[]{:S(2)}) collective-permute-start(bf16[64,128]{1,0:T(8,128)(2,1)S(1)} %get-tuple-element.34), channel_id=1, source_target_pairs={{0,16},{4,28},{8,24},{12,20},{16,0},{20,12},{24,8},{28,4},{1,17},{... | collective-permute-start | bytes 49160 | tf_op jit(solution)/shard_map/ppermute | solution.py:506
  15.0 1.6 %collective-permute-start.7 = (bf16[64,128]{1,0:T(8,128)(2,1)S(1)}, bf16[64,128]{1,0:T(8,128)(2,1)S(1)}, u32[]{:S(2)}, u32[]{:S(2)}) collective-permute-start(bf16[64,128]{1,0:T(8,128)(2,1)S(1)} %get-tuple-element.34), channel_id=1, source_target_pairs={{0,8},{4,12},{8,0},{12,4},{16,24},{20,28},{24,16},{28,20},{1,9},{5... | collective-permute-start | bytes 49160 | tf_op jit(solution)/shard_map/ppermute | solution.py:342
  16.6 0.6 %tree.1 = (bf16[8,64,64]{2,1,0:T(8,128)(2,1)S(1)}, bf16[8,64,64]{2,1,0:T(8,128)(2,1)S(1)}) custom-call(f32[8,64,64]{2,1,0:T(8,128)S(1)} %get-tuple-element.35.tree, f32[2,4,64,64]{3,2,1,0:T(8,128)S(1)} %get-tuple-element.36.couplings, f32[64,64]{1,0:T(8,128)S(1)} %get-tuple-element.37.matrix, f32[64,128]{1,0:T(8,128)S(1)} %get-tuple-element.38.sums.own), custom_call_target="tpu_custom_call" | custom-call | flops 17179869184 | bytes 268435456 | tf_op jit(solution)/shard_map/tree/pallas_call | solution.py:487
  17.3 0.1 collective-permute-start.8
  17.3 1.3 %far.1.coupled = f32[8,64,128]{2,1,0:T(8,128)S(1)} custom-call(s32[8,16]{1,0:T(8,128)S(1)} %get-tuple-element.25.list_in, s32[1,16]{1,0:T(1,128)S(1)} %get-tuple-element.26.count_in, bf16[9,64,128]{2,1,0:T(8,128)(2,1)S(1)} %collective-permute-done.refs_1_.payload.refs_0_, bf16[9,64,128]{2,1,0:T(8,128)(2,1)S(1)} %collective-permute-done.1.refs_2_.refs_1_, ...), custom_call_target="tpu_custom_call" | custom-call | flops 268435456 | bytes 2097152 | tf_op jit(solution)/shard_map/far/pallas_call | solution.py:532
  18.6 0.3 %base.1 = (f32[16,64,256]{2,1,0:T(8,128)S(1)}, f32[64,64]{1,0:T(8,128)S(1)}) custom-call(f32[8,64,128]{2,1,0:T(8,128)S(1)} %far.1.coupled, bf16[16,64,256]{2,1,0:T(8,128)(2,1)S(1)} %get-tuple-element.40.basis, f32[16,64,256]{2,1,0:T(8,128)S(1)} %get-tuple-element.32.refs_4_.near, bf16[8,64,64]{2,1,0:T(8,128)(2,1)S(1)} %get-tuple-element.39.refs_1_.down_high, ...), custom_call_target="tpu_custom_call" | custom-call | tf_op jit(solution)/shard_map/base/pallas_call | solution.py:556
  19.0 1.3 %down.1 = bf16[16,64,256]{2,1,0:T(8,128)(2,1)} custom-call(f32[64,64]{1,0:T(8,128)S(1)} %get-tuple-element.42.part, bf16[64,128]{1,0:T(8,128)(2,1)S(1)} %collective-permute-done.7.beside, bf16[1,64,128]{2,1,0:T(8,128)(2,1)S(1)} %collective-permute-done.8.swapped, bf16[8,64,64]{2,1,0:T(8,128)(2,1)S(1)} %get-tuple-element.39.refs_1_.down_high, ...), custom_call_target="tpu_custom_call" | custom-call | tf_op jit(solution)/shard_map/down/pallas_call | solution.py:568
  (12 shorter events, 0.0 us)
Async XLA Ops:
  2.1 5.3 %slice-start = ((s8[8388608]{0:T(1024)(128)(4,1)}), s8[4194304]{0:T(1024)(128)(4,1)S(1)}, s32[]{:S(2)}) async-start(s8[8388608]{0:T(1024)(128)(4,1)} %bitcast.4), calls=%async_computation | async-start | bytes 8388608
  2.1 5.3 %slice-start.1 = ((s8[8388608]{0:T(1024)(128)(4,1)}), s8[4194304]{0:T(1024)(128)(4,1)S(1)}, s32[]{:S(2)}) async-start(s8[8388608]{0:T(1024)(128)(4,1)} %bitcast.4), calls=%async_computation.1 | async-start | bytes 8388608
  2.1 4.6 %collective-permute-start.2 = (bf16[9,64,128]{2,1,0:T(8,128)(2,1)S(1)}, bf16[9,64,128]{2,1,0:T(8,128)(2,1)S(1)}, u32[]{:S(2)}, u32[]{:S(2)}) collective-permute-start(bf16[9,64,128]{2,1,0:T(8,128)(2,1)S(1)} %mark.1.own.refs_0_), channel_id=1, source_target_pairs={{0,4},{4,0},{8,12},{12,8},{16,20},{20,16},{24,28},{28,24},{1,5},{5... | collective-permute-start | bytes 442376 | tf_op jit(solution)/shard_map/ppermute | solution.py:342
  2.6 8.1 %collective-permute-start = (bf16[9,64,128]{2,1,0:T(8,128)(2,1)S(1)}, bf16[9,64,128]{2,1,0:T(8,128)(2,1)S(1)}, u32[]{:S(2)}, u32[]{:S(2)}) collective-permute-start(bf16[9,64,128]{2,1,0:T(8,128)(2,1)S(1)} %mark.1.own.refs_0_), channel_id=1, source_target_pairs={{0,1},{1,0},{2,3},{3,2},{4,6},{5,7},{6,4},{7,5},{8,9},{9,8},{10,11... | collective-permute-start | bytes 442376 | tf_op jit(solution)/shard_map/ppermute | solution.py:347
  5.2 5.5 %collective-permute-start.1 = (bf16[9,64,128]{2,1,0:T(8,128)(2,1)S(1)}, bf16[9,64,128]{2,1,0:T(8,128)(2,1)S(1)}, u32[]{:S(2)}, u32[]{:S(2)}) collective-permute-start(bf16[9,64,128]{2,1,0:T(8,128)(2,1)S(1)} %mark.1.own.refs_0_), channel_id=1, source_target_pairs={{0,2},{1,3},{2,0},{3,1},{4,5},{5,4},{6,7},{7,6},{8,10},{9,11},{10,... | collective-permute-start | bytes 442376 | tf_op jit(solution)/shard_map/ppermute | solution.py:347
  6.9 3.9 %collective-permute-start.3 = (bf16[64,128]{1,0:T(8,128)(2,1)S(1)}, bf16[64,128]{1,0:T(8,128)(2,1)S(1)}, u32[]{:S(2)}, u32[]{:S(2)}) collective-permute-start(bf16[64,128]{1,0:T(8,128)(2,1)S(1)} %terms.1.after), channel_id=1, source_target_pairs={{0,1},{1,0},{2,3},{3,2},{4,7},{5,6},{6,5},{7,4},{8,9},{9,8},{10,11... | collective-permute-start | bytes 49160 | tf_op jit(solution)/shard_map/ppermute | solution.py:347
  10.8 1.5 %collective-permute-start.5 = (f32[2,64,128]{2,1,0:T(8,128)S(1)}, f32[2,64,128]{2,1,0:T(8,128)S(1)}, u32[]{:S(2)}, u32[]{:S(2)}) collective-permute-start(f32[2,64,128]{2,1,0:T(8,128)S(1)} %group_sum.1.near.after.mine), channel_id=1, source_target_pairs={{0,4},{4,0},{8,12},{12,8},{16,20},{20,16},{24,28},{28,24},{1,5},{5... | collective-permute-start | bytes 196616 | tf_op jit(solution)/shard_map/ppermute | solution.py:342
  11.0 6.4 %collective-permute-start.4 = (bf16[8,64,128]{2,1,0:T(8,128)(2,1)S(1)}, bf16[8,64,128]{2,1,0:T(8,128)(2,1)S(1)}, u32[]{:S(2)}, u32[]{:S(2)}) collective-permute-start(bf16[8,64,128]{2,1,0:T(8,128)(2,1)S(1)} %forward.1), channel_id=1, source_target_pairs={{0,2},{1,3},{2,0},{3,1},{4,5},{5,4},{6,7},{7,6},{8,10},{9,11},{10,... | collective-permute-start | bytes 393224 | tf_op jit(solution)/shard_map/ppermute | solution.py:347
  12.4 4.8 %collective-permute-start.6 = (bf16[64,128]{1,0:T(8,128)(2,1)S(1)}, bf16[64,128]{1,0:T(8,128)(2,1)S(1)}, u32[]{:S(2)}, u32[]{:S(2)}) collective-permute-start(bf16[64,128]{1,0:T(8,128)(2,1)S(1)} %get-tuple-element.34), channel_id=1, source_target_pairs={{0,16},{4,28},{8,24},{12,20},{16,0},{20,12},{24,8},{28,4},{1,17},{... | collective-permute-start | bytes 49160 | tf_op jit(solution)/shard_map/ppermute | solution.py:506
  15.0 4.0 %collective-permute-start.7 = (bf16[64,128]{1,0:T(8,128)(2,1)S(1)}, bf16[64,128]{1,0:T(8,128)(2,1)S(1)}, u32[]{:S(2)}, u32[]{:S(2)}) collective-permute-start(bf16[64,128]{1,0:T(8,128)(2,1)S(1)} %get-tuple-element.34), channel_id=1, source_target_pairs={{0,8},{4,12},{8,0},{12,4},{16,24},{20,28},{24,16},{28,20},{1,9},{5... | collective-permute-start | bytes 49160 | tf_op jit(solution)/shard_map/ppermute | solution.py:342
  17.3 1.7 %collective-permute-start.8 = (bf16[1,64,128]{2,1,0:T(8,128)(2,1)S(1)}, bf16[1,64,128]{2,1,0:T(8,128)(2,1)S(1)}, u32[]{:S(2)}, u32[]{:S(2)}) collective-permute-start(bf16[1,64,128]{2,1,0:T(8,128)(2,1)S(1)} %relay.1.refs_4_), channel_id=1, source_target_pairs={{0,4},{4,0},{8,12},{12,8},{16,20},{20,16},{24,28},{28,24},{1,5},{5... | collective-permute-start | bytes 49160 | tf_op jit(solution)/shard_map/ppermute | solution.py:342

commit v10 on v9

--- a/solution.py
+++ b/solution.py
@@ -124,8 +124,8 @@
 
 def terms_kernel(own, other, terms):
     last = own.shape[0] - 1
-    both = jnp.concatenate([joined(own[last]), joined(other[last])], axis=1)
-    terms[...] = both.astype(bf16)
+    rank = terms.shape[1] // 2
+    terms[...] = jnp.concatenate([own[last][:, :rank], other[last][:, :rank]], axis=1)
 
 
 def pair_kernel(mine, theirs, *refs):
@@ -510,7 +510,7 @@
         )
         for step in range(steps)
     ]
-    beside = exchange(rounded_pair, "leaf", 2)
+    beside = exchange(own_pair, "leaf", 2)
 
     skeletons = {distance: arrived[distance] for distance in direct}
     for distance in range(1, list_count):

time: 20.4 us -> 20.7 us (1.015)
  waiting for transfers between devices: 0.02 us -> 0.24 us
    ppermute x4, waiting for transfers between devices: 0.01 us -> 0.23 us  [exchange(): return lax.ppermute(array, axis, pairs)]
  transfers between devices with their start and end apart: 9 -> 9, of which waited for: 0 -> 1; matrix products, arithmetic and copies ran while one was open for 0% -> 0% of each run, Pallas kernels for 28% -> 28%
where the time goes in v10:
time: 20.7 us; the launch traced here: 20.5 us
  starting transfers between devices  11 us (53%)
  Pallas kernels  9.14 us (44%)
  waiting for transfers between devices  0.24 us (1%)
    ppermute x4, starting transfers between devices, spread(): return lax.ppermute(array, ('leaf', 'list'), list(enumerate(ends)))  6.04 us
    pallas_call x1, Pallas kernels, on_device(): pl.pallas_call(functools.partial(near_kernel, leaf_count), out_shape=[sha...  3.28 us
    ppermute x1, starting transfers between devices, on_device(): lax.ppermute(rounded_pair, 'leaf', [(i, i ^ 2 * (2 + step + steps * (i %...  2.65 us
    ppermute x4, starting transfers between devices, exchange(): return lax.ppermute(array, axis, pairs)  2.29 us
    pallas_call x1, Pallas kernels, on_device(): pl.pallas_call(functools.partial(upward_kernel, count), out_shape=[shape(...  2.09 us
    pallas_call x1, Pallas kernels, on_device(): pl.pallas_call(functools.partial(far_kernel, list_count - 1), out_shape=s...  1.28 us
    pallas_call x1, Pallas kernels, on_device(): pl.pallas_call(down_kernel, out_shape=shape(leaves, rows, panels), in_spe...  1.26 us
    pallas_call x1, Pallas kernels, on_device(): pl.pallas_call(functools.partial(tree_kernel, leaf_count), out_shape=[sha...  0.64 us
  transfers between devices with their start and end apart: 9, of which 1 were waited for; matrix products, arithmetic and copies ran while one was open for 0% of the time, Pallas kernels for 28%

profile of v10, /device:TPU:0, one launch (start us, length us, event | category | flops | bytes accessed | tf_op | source)
XLA Modules:
  0.0 20.5 jit_solution(5797895980027669141)
XLA Ops:
  0.0 2.1 %upward.1 = (bf16[9,64,128]{2,1,0:T(8,128)(2,1)S(1)}, bf16[16,64,256]{2,1,0:T(8,128)(2,1)S(1)}, bf16[16,64,256]{2,1,0:T(8,128)(2,1)S(1)}, f32[16,64,64]{2,1,0:T(...) custom-call(bf16[16,64,256]{2,1,0:T(8,128)(2,1)} %refs_0_.2, ...), custom_call_target="tpu_custom_call" | custom-call | tf_op jit(solution)/shard_map/upward/pallas_call | solution.py:355
  2.1 0.0 slice-start
  2.1 0.5 %collective-permute-start.2 = (bf16[9,64,128]{2,1,0:T(8,128)(2,1)S(1)}, bf16[9,64,128]{2,1,0:T(8,128)(2,1)S(1)}, u32[]{:S(2)}, u32[]{:S(2)}) collective-permute-start(bf16[9,64,128]{2,1,0:T(8,128)(2,1)S(1)} %mark.1.own.refs_0_), channel_id=1, source_target_pairs={{0,4},{4,0},{8,12},{12,8},{16,20},{20,16},{24,28},{28,24},{1,5},{5... | collective-permute-start | bytes 442376 | tf_op jit(solution)/shard_map/ppermute | solution.py:342
  2.6 2.6 %collective-permute-start = (bf16[9,64,128]{2,1,0:T(8,128)(2,1)S(1)}, bf16[9,64,128]{2,1,0:T(8,128)(2,1)S(1)}, u32[]{:S(2)}, u32[]{:S(2)}) collective-permute-start(bf16[9,64,128]{2,1,0:T(8,128)(2,1)S(1)} %mark.1.own.refs_0_), channel_id=1, source_target_pairs={{0,1},{1,0},{2,3},{3,2},{4,6},{5,7},{6,4},{7,5},{8,9},{9,8},{10,11... | collective-permute-start | bytes 442376 | tf_op jit(solution)/shard_map/ppermute | solution.py:347
  5.2 1.5 %collective-permute-start.1 = (bf16[9,64,128]{2,1,0:T(8,128)(2,1)S(1)}, bf16[9,64,128]{2,1,0:T(8,128)(2,1)S(1)}, u32[]{:S(2)}, u32[]{:S(2)}) collective-permute-start(bf16[9,64,128]{2,1,0:T(8,128)(2,1)S(1)} %mark.1.own.refs_0_), channel_id=1, source_target_pairs={{0,2},{1,3},{2,0},{3,1},{4,5},{5,4},{6,7},{7,6},{8,10},{9,11},{10,... | collective-permute-start | bytes 442376 | tf_op jit(solution)/shard_map/ppermute | solution.py:347
  6.7 0.1 terms.1.after
  6.8 0.5 %collective-permute-start.3 = (bf16[64,128]{1,0:T(8,128)(2,1)S(1)}, bf16[64,128]{1,0:T(8,128)(2,1)S(1)}, u32[]{:S(2)}, u32[]{:S(2)}) collective-permute-start(bf16[64,128]{1,0:T(8,128)(2,1)S(1)} %terms.1.after), channel_id=1, source_target_pairs={{0,1},{1,0},{2,3},{3,2},{4,7},{5,6},{6,5},{7,4},{8,9},{9,8},{10,11... | collective-permute-start | bytes 49160 | tf_op jit(solution)/shard_map/ppermute | solution.py:347
  7.4 3.3 %near.1 = (f32[16,64,256]{2,1,0:T(8,128)S(1)}, f32[8,64,64]{2,1,0:T(8,128)S(1)}, f32[64,64]{1,0:T(8,128)S(1)}, bf16[16,64,256]{2,1,0:T(8,128)(2,1)S(1)}, bf16[16...) custom-call(s32[4,16]{1,0:T(4,128)S(1)} %get-tuple-element.28.list_in, ...), custom_call_target="tpu_custom_call" | custom-call | flops 536870912 | bytes 8388608 | tf_op jit(solution)/shard_map/near/pallas_call | solution.py:410
  10.7 0.0 collective-permute-done.1.refs_2_.refs_1_
  10.7 0.0 collective-permute-done.3.refs_3_
  10.7 0.1 group_sum.1.near.after.mine
  10.8 0.1 collective-permute-start.5
  10.9 1.4 %collective-permute-start.4 = (bf16[8,64,128]{2,1,0:T(8,128)(2,1)S(1)}, bf16[8,64,128]{2,1,0:T(8,128)(2,1)S(1)}, u32[]{:S(2)}, u32[]{:S(2)}) collective-permute-start(bf16[8,64,128]{2,1,0:T(8,128)(2,1)S(1)} %forward.1), channel_id=1, source_target_pairs={{0,2},{1,3},{2,0},{3,1},{4,5},{5,4},{6,7},{7,6},{8,10},{9,11},{10,... | collective-permute-start | bytes 393224 | tf_op jit(solution)/shard_map/ppermute | solution.py:347
  12.3 0.0 collective-permute-done.5.theirs
  12.3 0.1 pair.1
  12.4 2.6 %collective-permute-start.6 = (bf16[64,128]{1,0:T(8,128)(2,1)S(1)}, bf16[64,128]{1,0:T(8,128)(2,1)S(1)}, u32[]{:S(2)}, u32[]{:S(2)}) collective-permute-start(bf16[64,128]{1,0:T(8,128)(2,1)S(1)} %get-tuple-element.34), channel_id=1, source_target_pairs={{0,16},{4,28},{8,24},{12,20},{16,0},{20,12},{24,8},{28,4},{1,17},{... | collective-permute-start | bytes 49160 | tf_op jit(solution)/shard_map/ppermute | solution.py:506
  15.1 1.6 %collective-permute-start.7 = (f32[64,128]{1,0:T(8,128)S(1)}, f32[64,128]{1,0:T(8,128)S(1)}, u32[]{:S(2)}, u32[]{:S(2)}) collective-permute-start(f32[64,128]{1,0:T(8,128)S(1)} %get-tuple-element.38.sums.own), channel_id=1, source_target_pairs={{0,8},{4,12},{8,0},{12,4},{16,24},{20,28},{24,16},{28,20},{1,9},{5... | collective-permute-start | bytes 98312 | tf_op jit(solution)/shard_map/ppermute | solution.py:342
  16.6 0.6 %tree.1 = (bf16[8,64,64]{2,1,0:T(8,128)(2,1)S(1)}, bf16[8,64,64]{2,1,0:T(8,128)(2,1)S(1)}) custom-call(f32[8,64,64]{2,1,0:T(8,128)S(1)} %get-tuple-element.35.tree, f32[2,4,64,64]{3,2,1,0:T(8,128)S(1)} %get-tuple-element.36.couplings, f32[64,64]{1,0:T(8,128)S(1)} %get-tuple-element.37.matrix, f32[64,128]{1,0:T(8,128)S(1)} %get-tuple-element.38.sums.own), custom_call_target="tpu_custom_call" | custom-call | flops 17179869184 | bytes 268435456 | tf_op jit(solution)/shard_map/tree/pallas_call | solution.py:487
  17.3 0.0 collective-permute-done.6.refs_0_
  17.3 0.1 collective-permute-start.8
  17.4 1.3 %far.1.coupled = f32[8,64,128]{2,1,0:T(8,128)S(1)} custom-call(s32[8,16]{1,0:T(8,128)S(1)} %get-tuple-element.25.list_in, s32[1,16]{1,0:T(1,128)S(1)} %get-tuple-element.26.count_in, bf16[9,64,128]{2,1,0:T(8,128)(2,1)S(1)} %collective-permute-done.refs_1_.payload.refs_0_, bf16[9,64,128]{2,1,0:T(8,128)(2,1)S(1)} %collective-permute-done.1.refs_2_.refs_1_, ...), custom_call_target="tpu_custom_call" | custom-call | flops 268435456 | bytes 2097152 | tf_op jit(solution)/shard_map/far/pallas_call | solution.py:532
  18.7 0.3 %base.1 = (f32[16,64,256]{2,1,0:T(8,128)S(1)}, f32[64,64]{1,0:T(8,128)S(1)}) custom-call(f32[8,64,128]{2,1,0:T(8,128)S(1)} %far.1.coupled, bf16[16,64,256]{2,1,0:T(8,128)(2,1)S(1)} %get-tuple-element.40.basis, f32[16,64,256]{2,1,0:T(8,128)S(1)} %get-tuple-element.32.refs_4_.near, bf16[8,64,64]{2,1,0:T(8,128)(2,1)S(1)} %get-tuple-element.39.refs_1_.down_high, ...), custom_call_target="tpu_custom_call" | custom-call | tf_op jit(solution)/shard_map/base/pallas_call | solution.py:556
  19.0 0.2 %collective-permute-done.7.beside = f32[64,128]{1,0:T(8,128)S(1)} collective-permute-done((f32[64,128]{1,0:T(8,128)S(1)}, f32[64,128]{1,0:T(8,128)S(1)}, u32[]{:S(2)}, u32[]{:S(2)}) %collective-permute-start.7) | collective-permute-done | bytes 32800 | tf_op jit(solution)/shard_map/ppermute | solution.py:342
  19.2 1.3 %down.1 = bf16[16,64,256]{2,1,0:T(8,128)(2,1)} custom-call(f32[64,64]{1,0:T(8,128)S(1)} %get-tuple-element.42.part, f32[64,128]{1,0:T(8,128)S(1)} %collective-permute-done.7.beside, bf16[1,64,128]{2,1,0:T(8,128)(2,1)S(1)} %collective-permute-done.8.swapped, bf16[8,64,64]{2,1,0:T(8,128)(2,1)S(1)} %get-tuple-element.39.refs_1_.down_high, ...), custom_call_target="tpu_custom_call" | custom-call | tf_op jit(solution)/shard_map/down/pallas_call | solution.py:568
  (12 shorter events, 0.0 us)
Async XLA Ops:
  2.1 5.3 %slice-start = ((s8[8388608]{0:T(1024)(128)(4,1)}), s8[4194304]{0:T(1024)(128)(4,1)S(1)}, s32[]{:S(2)}) async-start(s8[8388608]{0:T(1024)(128)(4,1)} %bitcast.4), calls=%async_computation | async-start | bytes 8388608
  2.1 5.2 %slice-start.1 = ((s8[8388608]{0:T(1024)(128)(4,1)}), s8[4194304]{0:T(1024)(128)(4,1)S(1)}, s32[]{:S(2)}) async-start(s8[8388608]{0:T(1024)(128)(4,1)} %bitcast.4), calls=%async_computation.1 | async-start | bytes 8388608
  2.1 4.6 %collective-permute-start.2 = (bf16[9,64,128]{2,1,0:T(8,128)(2,1)S(1)}, bf16[9,64,128]{2,1,0:T(8,128)(2,1)S(1)}, u32[]{:S(2)}, u32[]{:S(2)}) collective-permute-start(bf16[9,64,128]{2,1,0:T(8,128)(2,1)S(1)} %mark.1.own.refs_0_), channel_id=1, source_target_pairs={{0,4},{4,0},{8,12},{12,8},{16,20},{20,16},{24,28},{28,24},{1,5},{5... | collective-permute-start | bytes 442376 | tf_op jit(solution)/shard_map/ppermute | solution.py:342
  2.6 8.0 %collective-permute-start = (bf16[9,64,128]{2,1,0:T(8,128)(2,1)S(1)}, bf16[9,64,128]{2,1,0:T(8,128)(2,1)S(1)}, u32[]{:S(2)}, u32[]{:S(2)}) collective-permute-start(bf16[9,64,128]{2,1,0:T(8,128)(2,1)S(1)} %mark.1.own.refs_0_), channel_id=1, source_target_pairs={{0,1},{1,0},{2,3},{3,2},{4,6},{5,7},{6,4},{7,5},{8,9},{9,8},{10,11... | collective-permute-start | bytes 442376 | tf_op jit(solution)/shard_map/ppermute | solution.py:347
  5.2 5.4 %collective-permute-start.1 = (bf16[9,64,128]{2,1,0:T(8,128)(2,1)S(1)}, bf16[9,64,128]{2,1,0:T(8,128)(2,1)S(1)}, u32[]{:S(2)}, u32[]{:S(2)}) collective-permute-start(bf16[9,64,128]{2,1,0:T(8,128)(2,1)S(1)} %mark.1.own.refs_0_), channel_id=1, source_target_pairs={{0,2},{1,3},{2,0},{3,1},{4,5},{5,4},{6,7},{7,6},{8,10},{9,11},{10,... | collective-permute-start | bytes 442376 | tf_op jit(solution)/shard_map/ppermute | solution.py:347
  6.8 3.9 %collective-permute-start.3 = (bf16[64,128]{1,0:T(8,128)(2,1)S(1)}, bf16[64,128]{1,0:T(8,128)(2,1)S(1)}, u32[]{:S(2)}, u32[]{:S(2)}) collective-permute-start(bf16[64,128]{1,0:T(8,128)(2,1)S(1)} %terms.1.after), channel_id=1, source_target_pairs={{0,1},{1,0},{2,3},{3,2},{4,7},{5,6},{6,5},{7,4},{8,9},{9,8},{10,11... | collective-permute-start | bytes 49160 | tf_op jit(solution)/shard_map/ppermute | solution.py:347
  10.8 1.6 %collective-permute-start.5 = (f32[2,64,128]{2,1,0:T(8,128)S(1)}, f32[2,64,128]{2,1,0:T(8,128)S(1)}, u32[]{:S(2)}, u32[]{:S(2)}) collective-permute-start(f32[2,64,128]{2,1,0:T(8,128)S(1)} %group_sum.1.near.after.mine), channel_id=1, source_target_pairs={{0,4},{4,0},{8,12},{12,8},{16,20},{20,16},{24,28},{28,24},{1,5},{5... | collective-permute-start | bytes 196616 | tf_op jit(solution)/shard_map/ppermute | solution.py:342
  10.9 6.5 %collective-permute-start.4 = (bf16[8,64,128]{2,1,0:T(8,128)(2,1)S(1)}, bf16[8,64,128]{2,1,0:T(8,128)(2,1)S(1)}, u32[]{:S(2)}, u32[]{:S(2)}) collective-permute-start(bf16[8,64,128]{2,1,0:T(8,128)(2,1)S(1)} %forward.1), channel_id=1, source_target_pairs={{0,2},{1,3},{2,0},{3,1},{4,5},{5,4},{6,7},{7,6},{8,10},{9,11},{10,... | collective-permute-start | bytes 393224 | tf_op jit(solution)/shard_map/ppermute | solution.py:347
  12.4 4.9 %collective-permute-start.6 = (bf16[64,128]{1,0:T(8,128)(2,1)S(1)}, bf16[64,128]{1,0:T(8,128)(2,1)S(1)}, u32[]{:S(2)}, u32[]{:S(2)}) collective-permute-start(bf16[64,128]{1,0:T(8,128)(2,1)S(1)} %get-tuple-element.34), channel_id=1, source_target_pairs={{0,16},{4,28},{8,24},{12,20},{16,0},{20,12},{24,8},{28,4},{1,17},{... | collective-permute-start | bytes 49160 | tf_op jit(solution)/shard_map/ppermute | solution.py:506
  15.1 4.2 %collective-permute-start.7 = (f32[64,128]{1,0:T(8,128)S(1)}, f32[64,128]{1,0:T(8,128)S(1)}, u32[]{:S(2)}, u32[]{:S(2)}) collective-permute-start(f32[64,128]{1,0:T(8,128)S(1)} %get-tuple-element.38.sums.own), channel_id=1, source_target_pairs={{0,8},{4,12},{8,0},{12,4},{16,24},{20,28},{24,16},{28,20},{1,9},{5... | collective-permute-start | bytes 98312 | tf_op jit(solution)/shard_map/ppermute | solution.py:342
  17.3 1.9 %collective-permute-start.8 = (bf16[1,64,128]{2,1,0:T(8,128)(2,1)S(1)}, bf16[1,64,128]{2,1,0:T(8,128)(2,1)S(1)}, u32[]{:S(2)}, u32[]{:S(2)}) collective-permute-start(bf16[1,64,128]{2,1,0:T(8,128)(2,1)S(1)} %relay.1.refs_4_), channel_id=1, source_target_pairs={{0,4},{4,0},{8,12},{12,8},{16,20},{20,16},{24,28},{28,24},{1,5},{5... | collective-permute-start | bytes 49160 | tf_op jit(solution)/shard_map/ppermute | solution.py:342
